TPU v7x, 512 devices: a whole 4x4x16 slice. The times are simulated.
512 devices in a mesh: win: 64 (over x, y, z_hi, core), head: 8 (over z_lo).
Axes of the slice: x: 4, y: 4, z: 16 (z_hi: 2, z_lo: 8; z = z_hi * 8 + z_lo), core: 2. Of those that a mesh axis runs over, the one named last changes fastest.
Arguments:
- query_proj: bfloat16 [8192, 5120], P('win', 'head'), may hold values from -8 to 8
- key_proj: bfloat16 [8192, 5120], P('win', 'head'), may hold values from -8 to 8
- value_proj: bfloat16 [8192, 5120], P('win', 'head'), may hold values from -16 to 16
- latents: bfloat16 [8192, 5120], P('win', 'head'), may hold values from -6 to 6
- out_weight: bfloat16 [5120, 5120], P('win', 'head'), may hold values from -0.078125 to 0.078125
- level_gate: float32 [8, 5120], P(None, 'head'), may hold values from 0.3 to 1.5
- levels: int32 [64], P('win'), may hold values from 0 to 7
- frame_mask: int32 [64, 16], P('win'), may hold values 0 or 1
- seed_block: int32 [1], replicated, may hold values from 0 to 63
Outputs:
- stepped: bfloat16 [8192, 5120], P('win', 'head')
All inputs are finite; a program needn't handle non-finite values. No bound on the sum of `frame_mask` on one device may be relied on, other than what follows from the above.
Results may differ from a plain program's by a relative error of at most 0.0065.
Values may be sent and summed in bfloat16 or wider, within the bound.
No kernel may reach another device: no remote copies, remote signals or barrier semaphores. Data moves between devices by JAX's collectives and lax.ppermute only.
A program may use at most 64 MiB of HBM per device.

v0:
```python
import jax
import jax.numpy as jnp
from jax import lax
from jax.sharding import PartitionSpec as P

HD = 128
CTX = 16
GROUP = 4
LEVELS = 8


def from_behind(value, axis, steps):
    count = lax.axis_size(axis)
    pairs = [(source, (source + steps) % count) for source in range(count)]
    return lax.ppermute(value, axis, pairs)


def attend_group(query_heads, state, group_pairs, seen):
    running, total, summed = state
    group_count = group_pairs.shape[0]
    rows_here, head_count, head_size = query_heads.shape
    key_heads = group_pairs[:, 0].reshape(group_count, rows_here, head_count, head_size)
    value_heads = group_pairs[:, 1].reshape(group_count, rows_here, head_count, head_size)
    scores = jnp.einsum(
        "thd,gshd->htgs", query_heads, key_heads, preferred_element_type=jnp.float32
    ) * HD ** (-0.5)
    scores = jnp.where(seen[None, None, :, None], scores, -1e30)
    top = jnp.maximum(running, jnp.max(scores, axis=(2, 3)))
    carried = jnp.exp(running - top)
    expo = jnp.exp(scores - top[:, :, None, None])
    total = total * carried + jnp.sum(expo, axis=(2, 3))
    weights = expo.astype(jnp.bfloat16)
    summed = summed * jnp.transpose(carried)[:, :, None] + jnp.einsum(
        "htgs,gshd->thd", weights, value_heads, preferred_element_type=jnp.float32
    )
    return (top, total, summed)


def on_device(
    query_proj,
    key_proj,
    value_proj,
    latents,
    out_weight,
    level_gate,
    levels,
    frame_mask,
    seed_block,
):
    rows_here = query_proj.shape[0]
    feature_count = query_proj.shape[1]
    head_count = feature_count // HD
    block_count = lax.axis_size("win")
    position = lax.axis_index("win")
    frame_age = (position - seed_block[0] - 1) % block_count
    visible_flags = frame_mask[0]
    query_heads = query_proj.reshape(rows_here, head_count, HD)
    own_pair = jnp.stack([key_proj, value_proj])

    def visibility(lag_values):
        return (lag_values <= frame_age) & (visible_flags[lag_values - 1] == 1)

    start_state = (
        jnp.full((head_count, rows_here), -1e30, jnp.float32),
        jnp.zeros((head_count, rows_here), jnp.float32),
        jnp.zeros((rows_here, head_count, HD), jnp.float32),
    )
    state = attend_group(query_heads, start_state, own_pair[None], jnp.ones((1,), bool))

    def chain_step(carry, group_index):
        current, inner = carry
        pieces = []
        for offset in range(GROUP):
            current = from_behind(current, "win", 1)
            pieces.append(current)
        lag_values = group_index * GROUP + jnp.arange(GROUP, dtype=jnp.int32) + 1
        inner = attend_group(query_heads, inner, jnp.stack(pieces), visibility(lag_values))
        return ((current, inner), None)

    (last_pair, state), unused = lax.scan(
        chain_step, (own_pair, state), jnp.arange(CTX // GROUP, dtype=jnp.int32)
    )
    running, total, summed = state
    attended = (
        (summed / jnp.transpose(total)[:, :, None])
        .astype(jnp.bfloat16)
        .reshape(rows_here, feature_count)
    )
    all_features = lax.all_gather(attended, "head", axis=1, tiled=True)
    projected = jnp.dot(
        all_features,
        lax.all_gather(out_weight, "win", axis=0, tiled=True),
        preferred_element_type=jnp.float32,
    )
    level_pick = (jnp.arange(LEVELS, dtype=jnp.int32) == levels[0]).astype(jnp.float32)
    gate_row = jnp.sum(level_pick[:, None] * level_gate, axis=0)
    return (latents.astype(jnp.float32) + gate_row[None, :] * projected).astype(jnp.bfloat16)


def solution(mesh):
    in_specs = (
        P("win", "head"),
        P("win", "head"),
        P("win", "head"),
        P("win", "head"),
        P("win", "head"),
        P(None, "head"),
        P("win"),
        P("win", None),
        P(),
    )
    out_specs = P("win", "head")
    return jax.shard_map(
        on_device, mesh=mesh, in_specs=in_specs, out_specs=out_specs, check_vma=False
    )
```

profile of v0, /device:TPU:1, one launch (start us, length us, event | category | flops | bytes accessed | tf_op | source)
XLA Modules:
  0.0 607.8 jit_solution(8817058292195258155)
XLA Ops:
  10.5 341.5 %while.20 = (s32[]{:T(128)}, bf16[2,128,640]{1,2,0:T(8,128)(2,1)S(1)}, f32[5,128]{1,0:T(8,128)S(1)}, f32[5,128]{1,0:T(8,128)S(1)}, f32[128,5,128]{0,2,1:T(8,128)...) while((s32[]{:T(128)}, ...), condition=%wide.region_6.7_spmd, body=%wide.region_3.6_spmd.sunk | while | flops 171871136 | bytes 16590745 | solution.py:80
  10.5 17.0 %collective-permute-start = (bf16[2,128,640]{1,2,0:T(8,128)(2,1)S(1)}, bf16[2,128,640]{1,2,0:T(8,128)(2,1)S(1)}, u32[]{:S(2)}, u32[]{:S(2)}) collective-permute-start(bf16[2,128,640]{1,2,0:T(8,128)(2,1)S(1)} %get-tuple-element.313), channel_id=1, source_target_pairs={{0,8},{8,16},{16,24},{24,32},{32,40},{40,48},{48,56},{56,64},{64,7... | collective-permute-start | bytes 983048 | tf_op jit(solution)/shard_map/while/body/eval_jaxpr/ppermute | solution.py:15
  27.5 13.5 %collective-permute-done = bf16[2,128,640]{1,2,0:T(8,128)(2,1)S(1)} collective-permute-done((bf16[2,128,640]{1,2,0:T(8,128)(2,1)S(1)}, bf16[2,128,640]{1,2,0:T(8,128)(2,1)S(1)}, u32[]{:S(2)}, u32[]{:S(2)}) %collective-permute-start) | collective-permute-done | bytes 327712 | tf_op jit(solution)/shard_map/while/body/eval_jaxpr/ppermute | solution.py:15
  41.0 13.2 %collective-permute-start.1 = (bf16[2,128,640]{1,2,0:T(8,128)(2,1)S(1)}, bf16[2,128,640]{1,2,0:T(8,128)(2,1)S(1)}, u32[]{:S(2)}, u32[]{:S(2)}) collective-permute-start(bf16[2,128,640]{1,2,0:T(8,128)(2,1)S(1)} %collective-permute-done), channel_id=1, source_target_pairs={{0,8},{8,16},{16,24},{24,32},{32,40},{40,48},{48,56},{56,64},{64,7... | collective-permute-start | bytes 983048 | tf_op jit(solution)/shard_map/while/body/eval_jaxpr/ppermute | solution.py:15
  54.2 10.5 %collective-permute-done.1 = bf16[2,128,640]{1,2,0:T(8,128)(2,1)S(1)} collective-permute-done((bf16[2,128,640]{1,2,0:T(8,128)(2,1)S(1)}, bf16[2,128,640]{1,2,0:T(8,128)(2,1)S(1)}, u32[]{:S(2)}, u32[]{:S(2)}) %collective-permute-start.1) | collective-permute-done | bytes 327712 | tf_op jit(solution)/shard_map/while/body/eval_jaxpr/ppermute | solution.py:15
  64.7 13.2 %collective-permute-start.2 = (bf16[2,128,640]{1,2,0:T(8,128)(2,1)S(1)}, bf16[2,128,640]{1,2,0:T(8,128)(2,1)S(1)}, u32[]{:S(2)}, u32[]{:S(2)}) collective-permute-start(bf16[2,128,640]{1,2,0:T(8,128)(2,1)S(1)} %collective-permute-done.1), channel_id=1, source_target_pairs={{0,8},{8,16},{16,24},{24,32},{32,40},{40,48},{48,56},{56,64},{64,7... | collective-permute-start | bytes 983048 | tf_op jit(solution)/shard_map/while/body/eval_jaxpr/ppermute | solution.py:15
  84.0 13.2 %collective-permute-start.3 = (bf16[2,128,640]{1,2,0:T(8,128)(2,1)S(1)}, bf16[2,128,640]{1,2,0:T(8,128)(2,1)S(1)}, u32[]{:S(2)}, u32[]{:S(2)}) collective-permute-start(bf16[2,128,640]{1,2,0:T(8,128)(2,1)S(1)} %collective-permute-done.2), channel_id=1, source_target_pairs={{0,8},{8,16},{16,24},{24,32},{32,40},{40,48},{48,56},{56,64},{64,7... | collective-permute-start | bytes 983048 | tf_op jit(solution)/shard_map/while/body/eval_jaxpr/ppermute | solution.py:15
  103.8 13.2 %collective-permute-start = (bf16[2,128,640]{1,2,0:T(8,128)(2,1)S(1)}, bf16[2,128,640]{1,2,0:T(8,128)(2,1)S(1)}, u32[]{:S(2)}, u32[]{:S(2)}) collective-permute-start(bf16[2,128,640]{1,2,0:T(8,128)(2,1)S(1)} %get-tuple-element.313), channel_id=1, source_target_pairs={{0,8},{8,16},{16,24},{24,32},{32,40},{40,48},{48,56},{56,64},{64,7... | collective-permute-start | bytes 983048 | tf_op jit(solution)/shard_map/while/body/eval_jaxpr/ppermute | solution.py:15
  121.9 13.2 %collective-permute-start.1 = (bf16[2,128,640]{1,2,0:T(8,128)(2,1)S(1)}, bf16[2,128,640]{1,2,0:T(8,128)(2,1)S(1)}, u32[]{:S(2)}, u32[]{:S(2)}) collective-permute-start(bf16[2,128,640]{1,2,0:T(8,128)(2,1)S(1)} %collective-permute-done), channel_id=1, source_target_pairs={{0,8},{8,16},{16,24},{24,32},{32,40},{40,48},{48,56},{56,64},{64,7... | collective-permute-start | bytes 983048 | tf_op jit(solution)/shard_map/while/body/eval_jaxpr/ppermute | solution.py:15
  140.3 13.2 %collective-permute-start.2 = (bf16[2,128,640]{1,2,0:T(8,128)(2,1)S(1)}, bf16[2,128,640]{1,2,0:T(8,128)(2,1)S(1)}, u32[]{:S(2)}, u32[]{:S(2)}) collective-permute-start(bf16[2,128,640]{1,2,0:T(8,128)(2,1)S(1)} %collective-permute-done.1), channel_id=1, source_target_pairs={{0,8},{8,16},{16,24},{24,32},{32,40},{40,48},{48,56},{56,64},{64,7... | collective-permute-start | bytes 983048 | tf_op jit(solution)/shard_map/while/body/eval_jaxpr/ppermute | solution.py:15
  159.6 13.2 %collective-permute-start.3 = (bf16[2,128,640]{1,2,0:T(8,128)(2,1)S(1)}, bf16[2,128,640]{1,2,0:T(8,128)(2,1)S(1)}, u32[]{:S(2)}, u32[]{:S(2)}) collective-permute-start(bf16[2,128,640]{1,2,0:T(8,128)(2,1)S(1)} %collective-permute-done.2), channel_id=1, source_target_pairs={{0,8},{8,16},{16,24},{24,32},{32,40},{40,48},{48,56},{56,64},{64,7... | collective-permute-start | bytes 983048 | tf_op jit(solution)/shard_map/while/body/eval_jaxpr/ppermute | solution.py:15
  179.3 13.2 %collective-permute-start = (bf16[2,128,640]{1,2,0:T(8,128)(2,1)S(1)}, bf16[2,128,640]{1,2,0:T(8,128)(2,1)S(1)}, u32[]{:S(2)}, u32[]{:S(2)}) collective-permute-start(bf16[2,128,640]{1,2,0:T(8,128)(2,1)S(1)} %get-tuple-element.313), channel_id=1, source_target_pairs={{0,8},{8,16},{16,24},{24,32},{32,40},{40,48},{48,56},{56,64},{64,7... | collective-permute-start | bytes 983048 | tf_op jit(solution)/shard_map/while/body/eval_jaxpr/ppermute | solution.py:15
  197.7 13.2 %collective-permute-start.1 = (bf16[2,128,640]{1,2,0:T(8,128)(2,1)S(1)}, bf16[2,128,640]{1,2,0:T(8,128)(2,1)S(1)}, u32[]{:S(2)}, u32[]{:S(2)}) collective-permute-start(bf16[2,128,640]{1,2,0:T(8,128)(2,1)S(1)} %collective-permute-done), channel_id=1, source_target_pairs={{0,8},{8,16},{16,24},{24,32},{32,40},{40,48},{48,56},{56,64},{64,7... | collective-permute-start | bytes 983048 | tf_op jit(solution)/shard_map/while/body/eval_jaxpr/ppermute | solution.py:15
  210.9 9.6 %collective-permute-done.1 = bf16[2,128,640]{1,2,0:T(8,128)(2,1)S(1)} collective-permute-done((bf16[2,128,640]{1,2,0:T(8,128)(2,1)S(1)}, bf16[2,128,640]{1,2,0:T(8,128)(2,1)S(1)}, u32[]{:S(2)}, u32[]{:S(2)}) %collective-permute-start.1) | collective-permute-done | bytes 327712 | tf_op jit(solution)/shard_map/while/body/eval_jaxpr/ppermute | solution.py:15
  220.4 13.2 %collective-permute-start.2 = (bf16[2,128,640]{1,2,0:T(8,128)(2,1)S(1)}, bf16[2,128,640]{1,2,0:T(8,128)(2,1)S(1)}, u32[]{:S(2)}, u32[]{:S(2)}) collective-permute-start(bf16[2,128,640]{1,2,0:T(8,128)(2,1)S(1)} %collective-permute-done.1), channel_id=1, source_target_pairs={{0,8},{8,16},{16,24},{24,32},{32,40},{40,48},{48,56},{56,64},{64,7... | collective-permute-start | bytes 983048 | tf_op jit(solution)/shard_map/while/body/eval_jaxpr/ppermute | solution.py:15
  242.0 13.2 %collective-permute-start.3 = (bf16[2,128,640]{1,2,0:T(8,128)(2,1)S(1)}, bf16[2,128,640]{1,2,0:T(8,128)(2,1)S(1)}, u32[]{:S(2)}, u32[]{:S(2)}) collective-permute-start(bf16[2,128,640]{1,2,0:T(8,128)(2,1)S(1)} %collective-permute-done.2), channel_id=1, source_target_pairs={{0,8},{8,16},{16,24},{24,32},{32,40},{40,48},{48,56},{56,64},{64,7... | collective-permute-start | bytes 983048 | tf_op jit(solution)/shard_map/while/body/eval_jaxpr/ppermute | solution.py:15
  255.8 7.5 %collective-permute-done.3 = bf16[2,128,640]{1,2,0:T(8,128)(2,1)S(1)} collective-permute-done((bf16[2,128,640]{1,2,0:T(8,128)(2,1)S(1)}, bf16[2,128,640]{1,2,0:T(8,128)(2,1)S(1)}, u32[]{:S(2)}, u32[]{:S(2)}) %collective-permute-start.3) | collective-permute-done | bytes 327712 | tf_op jit(solution)/shard_map/while/body/eval_jaxpr/ppermute | solution.py:15
  264.8 13.2 %collective-permute-start = (bf16[2,128,640]{1,2,0:T(8,128)(2,1)S(1)}, bf16[2,128,640]{1,2,0:T(8,128)(2,1)S(1)}, u32[]{:S(2)}, u32[]{:S(2)}) collective-permute-start(bf16[2,128,640]{1,2,0:T(8,128)(2,1)S(1)} %get-tuple-element.313), channel_id=1, source_target_pairs={{0,8},{8,16},{16,24},{24,32},{32,40},{40,48},{48,56},{56,64},{64,7... | collective-permute-start | bytes 983048 | tf_op jit(solution)/shard_map/while/body/eval_jaxpr/ppermute | solution.py:15
  284.9 13.2 %collective-permute-start.1 = (bf16[2,128,640]{1,2,0:T(8,128)(2,1)S(1)}, bf16[2,128,640]{1,2,0:T(8,128)(2,1)S(1)}, u32[]{:S(2)}, u32[]{:S(2)}) collective-permute-start(bf16[2,128,640]{1,2,0:T(8,128)(2,1)S(1)} %collective-permute-done), channel_id=1, source_target_pairs={{0,8},{8,16},{16,24},{24,32},{32,40},{40,48},{48,56},{56,64},{64,7... | collective-permute-start | bytes 983048 | tf_op jit(solution)/shard_map/while/body/eval_jaxpr/ppermute | solution.py:15
  298.1 9.6 %collective-permute-done.1 = bf16[2,128,640]{1,2,0:T(8,128)(2,1)S(1)} collective-permute-done((bf16[2,128,640]{1,2,0:T(8,128)(2,1)S(1)}, bf16[2,128,640]{1,2,0:T(8,128)(2,1)S(1)}, u32[]{:S(2)}, u32[]{:S(2)}) %collective-permute-start.1) | collective-permute-done | bytes 327712 | tf_op jit(solution)/shard_map/while/body/eval_jaxpr/ppermute | solution.py:15
  307.6 13.2 %collective-permute-start.2 = (bf16[2,128,640]{1,2,0:T(8,128)(2,1)S(1)}, bf16[2,128,640]{1,2,0:T(8,128)(2,1)S(1)}, u32[]{:S(2)}, u32[]{:S(2)}) collective-permute-start(bf16[2,128,640]{1,2,0:T(8,128)(2,1)S(1)} %collective-permute-done.1), channel_id=1, source_target_pairs={{0,8},{8,16},{16,24},{24,32},{32,40},{40,48},{48,56},{56,64},{64,7... | collective-permute-start | bytes 983048 | tf_op jit(solution)/shard_map/while/body/eval_jaxpr/ppermute | solution.py:15
  329.2 13.2 %collective-permute-start.3 = (bf16[2,128,640]{1,2,0:T(8,128)(2,1)S(1)}, bf16[2,128,640]{1,2,0:T(8,128)(2,1)S(1)}, u32[]{:S(2)}, u32[]{:S(2)}) collective-permute-start(bf16[2,128,640]{1,2,0:T(8,128)(2,1)S(1)} %collective-permute-done.2), channel_id=1, source_target_pairs={{0,8},{8,16},{16,24},{24,32},{32,40},{40,48},{48,56},{56,64},{64,7... | collective-permute-start | bytes 983048 | tf_op jit(solution)/shard_map/while/body/eval_jaxpr/ppermute | solution.py:15
  354.2 81.0 %all-gather.3.cloned.1.call-done = bf16[128,5120]{0,1:T(8,128)(2,1)} async-done(((bf16[128,640]{0,1:T(8,128)(2,1)}), bf16[128,5120]{0,1:T(8,128)(2,1)}) %all-gather.3.cloned.1.call-update) | async-done | bytes 1310736 | tf_op jit(solution)/shard_map/all_gather | solution.py:89
  435.2 160.6 %all-gather.5.cloned.1.call-done = bf16[5120,640]{1,0:T(8,128)(2,1)} async-done(((bf16[80,640]{1,0:T(8,128)(2,1)}), bf16[5120,640]{1,0:T(8,128)(2,1)}) %all-gather.5.cloned.1.call-update) | async-done | bytes 6553616 | tf_op jit(solution)/shard_map/all_gather | solution.py:92
  (91 shorter events, 82.8 us)
Async XLA Ops:
  6.5 3.0 copy-start.2
  6.5 428.6 %all-gather.3.cloned.1.call-start = ((), (), s32[]{:S(2)}) async-start(), calls=%async_computation | async-start | bytes 1474560 | tf_op jit(solution)/shard_map/all_gather | solution.py:89
  9.5 1.0 copy-start
  10.5 343.6 %copy-start.3 = (f32[8,640]{1,0:T(8,128)S(1)}, f32[8,640]{1,0:T(8,128)}, u32[]{:S(2)}) copy-start(f32[8,640]{1,0:T(8,128)} %param.16) | copy-start | bytes 61444
  10.5 585.3 %copy-start.1 = (bf16[128,640]{1,0:T(8,128)(2,1)S(1)}, bf16[128,640]{1,0:T(8,128)(2,1)}, u32[]{:S(2)}) copy-start(bf16[128,640]{1,0:T(8,128)(2,1)} %param.14) | copy-start | bytes 491524
  10.5 30.5 %collective-permute-start = (bf16[2,128,640]{1,2,0:T(8,128)(2,1)S(1)}, bf16[2,128,640]{1,2,0:T(8,128)(2,1)S(1)}, u32[]{:S(2)}, u32[]{:S(2)}) collective-permute-start(bf16[2,128,640]{1,2,0:T(8,128)(2,1)S(1)} %get-tuple-element.313), channel_id=1, source_target_pairs={{0,8},{8,16},{16,24},{24,32},{32,40},{40,48},{48,56},{56,64},{64,7... | collective-permute-start | bytes 983048 | tf_op jit(solution)/shard_map/while/body/eval_jaxpr/ppermute | solution.py:15
  41.0 23.7 %collective-permute-start.1 = (bf16[2,128,640]{1,2,0:T(8,128)(2,1)S(1)}, bf16[2,128,640]{1,2,0:T(8,128)(2,1)S(1)}, u32[]{:S(2)}, u32[]{:S(2)}) collective-permute-start(bf16[2,128,640]{1,2,0:T(8,128)(2,1)S(1)} %collective-permute-done), channel_id=1, source_target_pairs={{0,8},{8,16},{16,24},{24,32},{32,40},{40,48},{48,56},{56,64},{64,7... | collective-permute-start | bytes 983048 | tf_op jit(solution)/shard_map/while/body/eval_jaxpr/ppermute | solution.py:15
  64.7 19.3 %collective-permute-start.2 = (bf16[2,128,640]{1,2,0:T(8,128)(2,1)S(1)}, bf16[2,128,640]{1,2,0:T(8,128)(2,1)S(1)}, u32[]{:S(2)}, u32[]{:S(2)}) collective-permute-start(bf16[2,128,640]{1,2,0:T(8,128)(2,1)S(1)} %collective-permute-done.1), channel_id=1, source_target_pairs={{0,8},{8,16},{16,24},{24,32},{32,40},{40,48},{48,56},{56,64},{64,7... | collective-permute-start | bytes 983048 | tf_op jit(solution)/shard_map/while/body/eval_jaxpr/ppermute | solution.py:15
  84.0 18.4 %collective-permute-start.3 = (bf16[2,128,640]{1,2,0:T(8,128)(2,1)S(1)}, bf16[2,128,640]{1,2,0:T(8,128)(2,1)S(1)}, u32[]{:S(2)}, u32[]{:S(2)}) collective-permute-start(bf16[2,128,640]{1,2,0:T(8,128)(2,1)S(1)} %collective-permute-done.2), channel_id=1, source_target_pairs={{0,8},{8,16},{16,24},{24,32},{32,40},{40,48},{48,56},{56,64},{64,7... | collective-permute-start | bytes 983048 | tf_op jit(solution)/shard_map/while/body/eval_jaxpr/ppermute | solution.py:15
  103.8 18.1 %collective-permute-start = (bf16[2,128,640]{1,2,0:T(8,128)(2,1)S(1)}, bf16[2,128,640]{1,2,0:T(8,128)(2,1)S(1)}, u32[]{:S(2)}, u32[]{:S(2)}) collective-permute-start(bf16[2,128,640]{1,2,0:T(8,128)(2,1)S(1)} %get-tuple-element.313), channel_id=1, source_target_pairs={{0,8},{8,16},{16,24},{24,32},{32,40},{40,48},{48,56},{56,64},{64,7... | collective-permute-start | bytes 983048 | tf_op jit(solution)/shard_map/while/body/eval_jaxpr/ppermute | solution.py:15
  121.9 18.4 %collective-permute-start.1 = (bf16[2,128,640]{1,2,0:T(8,128)(2,1)S(1)}, bf16[2,128,640]{1,2,0:T(8,128)(2,1)S(1)}, u32[]{:S(2)}, u32[]{:S(2)}) collective-permute-start(bf16[2,128,640]{1,2,0:T(8,128)(2,1)S(1)} %collective-permute-done), channel_id=1, source_target_pairs={{0,8},{8,16},{16,24},{24,32},{32,40},{40,48},{48,56},{56,64},{64,7... | collective-permute-start | bytes 983048 | tf_op jit(solution)/shard_map/while/body/eval_jaxpr/ppermute | solution.py:15
  140.3 19.3 %collective-permute-start.2 = (bf16[2,128,640]{1,2,0:T(8,128)(2,1)S(1)}, bf16[2,128,640]{1,2,0:T(8,128)(2,1)S(1)}, u32[]{:S(2)}, u32[]{:S(2)}) collective-permute-start(bf16[2,128,640]{1,2,0:T(8,128)(2,1)S(1)} %collective-permute-done.1), channel_id=1, source_target_pairs={{0,8},{8,16},{16,24},{24,32},{32,40},{40,48},{48,56},{56,64},{64,7... | collective-permute-start | bytes 983048 | tf_op jit(solution)/shard_map/while/body/eval_jaxpr/ppermute | solution.py:15
  159.6 18.4 %collective-permute-start.3 = (bf16[2,128,640]{1,2,0:T(8,128)(2,1)S(1)}, bf16[2,128,640]{1,2,0:T(8,128)(2,1)S(1)}, u32[]{:S(2)}, u32[]{:S(2)}) collective-permute-start(bf16[2,128,640]{1,2,0:T(8,128)(2,1)S(1)} %collective-permute-done.2), channel_id=1, source_target_pairs={{0,8},{8,16},{16,24},{24,32},{32,40},{40,48},{48,56},{56,64},{64,7... | collective-permute-start | bytes 983048 | tf_op jit(solution)/shard_map/while/body/eval_jaxpr/ppermute | solution.py:15
  179.3 18.3 %collective-permute-start = (bf16[2,128,640]{1,2,0:T(8,128)(2,1)S(1)}, bf16[2,128,640]{1,2,0:T(8,128)(2,1)S(1)}, u32[]{:S(2)}, u32[]{:S(2)}) collective-permute-start(bf16[2,128,640]{1,2,0:T(8,128)(2,1)S(1)} %get-tuple-element.313), channel_id=1, source_target_pairs={{0,8},{8,16},{16,24},{24,32},{32,40},{40,48},{48,56},{56,64},{64,7... | collective-permute-start | bytes 983048 | tf_op jit(solution)/shard_map/while/body/eval_jaxpr/ppermute | solution.py:15
  197.7 22.8 %collective-permute-start.1 = (bf16[2,128,640]{1,2,0:T(8,128)(2,1)S(1)}, bf16[2,128,640]{1,2,0:T(8,128)(2,1)S(1)}, u32[]{:S(2)}, u32[]{:S(2)}) collective-permute-start(bf16[2,128,640]{1,2,0:T(8,128)(2,1)S(1)} %collective-permute-done), channel_id=1, source_target_pairs={{0,8},{8,16},{16,24},{24,32},{32,40},{40,48},{48,56},{56,64},{64,7... | collective-permute-start | bytes 983048 | tf_op jit(solution)/shard_map/while/body/eval_jaxpr/ppermute | solution.py:15
  220.4 21.5 %collective-permute-start.2 = (bf16[2,128,640]{1,2,0:T(8,128)(2,1)S(1)}, bf16[2,128,640]{1,2,0:T(8,128)(2,1)S(1)}, u32[]{:S(2)}, u32[]{:S(2)}) collective-permute-start(bf16[2,128,640]{1,2,0:T(8,128)(2,1)S(1)} %collective-permute-done.1), channel_id=1, source_target_pairs={{0,8},{8,16},{16,24},{24,32},{32,40},{40,48},{48,56},{56,64},{64,7... | collective-permute-start | bytes 983048 | tf_op jit(solution)/shard_map/while/body/eval_jaxpr/ppermute | solution.py:15
  242.0 21.4 %collective-permute-start.3 = (bf16[2,128,640]{1,2,0:T(8,128)(2,1)S(1)}, bf16[2,128,640]{1,2,0:T(8,128)(2,1)S(1)}, u32[]{:S(2)}, u32[]{:S(2)}) collective-permute-start(bf16[2,128,640]{1,2,0:T(8,128)(2,1)S(1)} %collective-permute-done.2), channel_id=1, source_target_pairs={{0,8},{8,16},{16,24},{24,32},{32,40},{40,48},{48,56},{56,64},{64,7... | collective-permute-start | bytes 983048 | tf_op jit(solution)/shard_map/while/body/eval_jaxpr/ppermute | solution.py:15
  264.8 20.1 %collective-permute-start = (bf16[2,128,640]{1,2,0:T(8,128)(2,1)S(1)}, bf16[2,128,640]{1,2,0:T(8,128)(2,1)S(1)}, u32[]{:S(2)}, u32[]{:S(2)}) collective-permute-start(bf16[2,128,640]{1,2,0:T(8,128)(2,1)S(1)} %get-tuple-element.313), channel_id=1, source_target_pairs={{0,8},{8,16},{16,24},{24,32},{32,40},{40,48},{48,56},{56,64},{64,7... | collective-permute-start | bytes 983048 | tf_op jit(solution)/shard_map/while/body/eval_jaxpr/ppermute | solution.py:15
  284.9 22.8 %collective-permute-start.1 = (bf16[2,128,640]{1,2,0:T(8,128)(2,1)S(1)}, bf16[2,128,640]{1,2,0:T(8,128)(2,1)S(1)}, u32[]{:S(2)}, u32[]{:S(2)}) collective-permute-start(bf16[2,128,640]{1,2,0:T(8,128)(2,1)S(1)} %collective-permute-done), channel_id=1, source_target_pairs={{0,8},{8,16},{16,24},{24,32},{32,40},{40,48},{48,56},{56,64},{64,7... | collective-permute-start | bytes 983048 | tf_op jit(solution)/shard_map/while/body/eval_jaxpr/ppermute | solution.py:15
  307.6 21.6 %collective-permute-start.2 = (bf16[2,128,640]{1,2,0:T(8,128)(2,1)S(1)}, bf16[2,128,640]{1,2,0:T(8,128)(2,1)S(1)}, u32[]{:S(2)}, u32[]{:S(2)}) collective-permute-start(bf16[2,128,640]{1,2,0:T(8,128)(2,1)S(1)} %collective-permute-done.1), channel_id=1, source_target_pairs={{0,8},{8,16},{16,24},{24,32},{32,40},{40,48},{48,56},{56,64},{64,7... | collective-permute-start | bytes 983048 | tf_op jit(solution)/shard_map/while/body/eval_jaxpr/ppermute | solution.py:15
  329.2 21.4 %collective-permute-start.3 = (bf16[2,128,640]{1,2,0:T(8,128)(2,1)S(1)}, bf16[2,128,640]{1,2,0:T(8,128)(2,1)S(1)}, u32[]{:S(2)}, u32[]{:S(2)}) collective-permute-start(bf16[2,128,640]{1,2,0:T(8,128)(2,1)S(1)} %collective-permute-done.2), channel_id=1, source_target_pairs={{0,8},{8,16},{16,24},{24,32},{32,40},{40,48},{48,56},{56,64},{64,7... | collective-permute-start | bytes 983048 | tf_op jit(solution)/shard_map/while/body/eval_jaxpr/ppermute | solution.py:15
  352.7 243.1 %all-gather.5.cloned.1.call-start = ((), (), s32[]{:S(2)}) async-start(), calls=%async_computation.1 | async-start | bytes 6656000 | tf_op jit(solution)/shard_map/all_gather | solution.py:92
Sparse Core Ops, SparseCore 0:
  352.8 82.3 all-gather.2
  439.6 156.1 all-gather.4
where the time goes:
time: 608 us
  waiting for transfers between devices  355 us (58%)
  starting transfers between devices  215 us (35%)
  between operations  14.9 us (2%)
  matrix products  8.92 us (1%)
  local copies, waits for them, and re-layouts  8.02 us (1%)
    ppermute x16, starting transfers between devices, from_behind(): return lax.ppermute(value, axis, pairs)  215 us
    all_gather x1, waiting for transfers between devices, on_device(): lax.all_gather(out_weight, 'win', axis=0, tiled=True)  161 us
    ppermute x16, waiting for transfers between devices, from_behind(): return lax.ppermute(value, axis, pairs)  113 us
    all_gather x1, waiting for transfers between devices, on_device(): all_features = lax.all_gather(attended, 'head', axis=1, tiled=True)  81 us
  transfers between devices with their start and end apart: 18, of which 18 were waited for; matrix products, arithmetic and copies ran while one was open for 1% of the time, Pallas kernels for 0%

commit v1 on v0

v1 whole, which is shorter than its diff:
```python
import jax
import jax.numpy as jnp
import numpy as np
from jax import lax
from jax.experimental import pallas as pl
from jax.experimental.pallas import tpu as pltpu
from jax.sharding import Mesh, PartitionSpec as P

HD = 128
TOK = 128
LEVELS = 8
HEADS_HERE = 5
FEAT = 640
HALF = 320
WIDE = 384
HIDDEN = -(2.0**100)
SCORE_SCALE = 1.4426950408889634 * HD**-0.5
AXES = ("x", "y", "zh", "c", "zl")
SIZES = (4, 4, 2, 2, 8)


def move(value, rule):
    pairs = []
    for source, place in enumerate(np.ndindex(*SIZES)):
        target = rule(*place)
        if target is not None:
            pairs.append((source, int(np.ravel_multi_index(target, SIZES))))
    return lax.ppermute(value, AXES, pairs)


def half_of_feature(half, lane):
    return (2 * (lane // 80) + half) * 80 + lane % 80


def selection_tables():
    tables = np.zeros((2, 768, 768), np.float32)
    for mine in range(2):
        for slot, half in enumerate((mine, 1 - mine)):
            base = slot * WIDE
            for lane in range(HALF):
                tables[mine, half_of_feature(half, lane), base + lane] = 1
            for stat in range(24):
                tables[mine, FEAT + stat, base + HALF + stat] = 1
    return tables


def spread_tables():
    tables = np.zeros((2, 2, 128, WIDE), np.float32)
    for half in range(2):
        for lane in range(HALF):
            head = half_of_feature(half, lane) // HD
            tables[half, 0, 64 + head, lane] = 1
            tables[half, 1, 72 + head, lane] = 1
        for head in range(HEADS_HERE):
            tables[half, 0, 64 + head, HALF + 8 + head] = 1
            tables[half, 0, 64 + head, HALF + 16 + head] = 1
    return tables


SELECTION = selection_tables()
SPREAD = spread_tables()


def dot_f32(a, b):
    return jnp.dot(a, b, preferred_element_type=jnp.float32)


def attend_kernel(code_ref, qa_ref, qb_ref, kv0, kv1, kv2, kv3, kv4, select_ref, mine_ref, theirs_ref):
    kvs = (kv0, kv1, kv2, kv3, kv4)
    lane = lax.broadcasted_iota(jnp.int32, (1, 128), 1)
    lanes = lax.broadcasted_iota(jnp.int32, (TOK, 128), 1)
    for r in range(4):
        q_ref = qa_ref if r % 2 == 0 else qb_ref
        zf = r // 2
        flags = q_ref[zf, TOK : TOK + 16, 0:128].astype(jnp.float32)[0:1]
        biases = []
        for d in range(5):
            code = code_ref[r, d]
            hit = jnp.sum(jnp.where(lane == code - 1, flags, 0.0), axis=1, keepdims=True)
            hit = jnp.where(code == 0, 1.0, hit)
            biases.append(jnp.broadcast_to(jnp.where(hit > 0.5, 0.0, HIDDEN), (1, 128)))
        bias = jnp.concatenate(biases, axis=1)
        acc = jnp.zeros((TOK, 2 * WIDE), jnp.float32)
        stats = jnp.zeros((TOK, 128), jnp.float32)
        for h in range(HEADS_HERE):
            cols = slice(h * HD, (h + 1) * HD)
            keys = jnp.concatenate([kv[0, :, cols] for kv in kvs], axis=0)
            values = jnp.concatenate([kv[1, :, cols] for kv in kvs], axis=0)
            scores = lax.dot_general(
                q_ref[zf, 0:TOK, cols], keys, (((1,), (1,)), ((), ())), preferred_element_type=jnp.float32
            )
            scores = scores * SCORE_SCALE + bias
            top = jnp.max(scores, axis=1, keepdims=True).astype(jnp.bfloat16).astype(jnp.float32)
            expo = jnp.exp2(scores - top)
            total = jnp.sum(expo, axis=1, keepdims=True)
            total_hi = total.astype(jnp.bfloat16).astype(jnp.float32)
            summed = dot_f32(expo.astype(jnp.bfloat16), values)
            acc = acc + dot_f32(summed.astype(jnp.bfloat16), select_ref[cols, :])
            stats = jnp.where(lanes == h, top, stats)
            stats = jnp.where(lanes == 8 + h, total_hi, stats)
            stats = jnp.where(lanes == 16 + h, total - total_hi, stats)
        acc = acc + dot_f32(stats.astype(jnp.bfloat16), select_ref[FEAT : FEAT + 128, :])
        mine_ref[r] = acc[:, :WIDE].astype(jnp.bfloat16)
        theirs_ref[r] = acc[:, WIDE:].astype(jnp.bfloat16)


def spread(factor, table):
    high = factor.astype(jnp.bfloat16)
    low = (factor - high.astype(jnp.float32)).astype(jnp.bfloat16)
    return dot_f32(high, table) + dot_f32(low, table)


def merge(first, second, table):
    one, two = first.astype(jnp.float32), second.astype(jnp.float32)
    s1, s2 = one[:, 256:], two[:, 256:]
    top = jnp.maximum(s1, s2)
    joined = one * spread(jnp.exp2(s1 - top), table) + two * spread(jnp.exp2(s2 - top), table)
    return joined, top


def merge_cores_kernel(mine_ref, got_ref, table_ref, keep_ref, send_ref):
    lanes = lax.broadcasted_iota(jnp.int32, (TOK, 128), 1)
    for r in range(4):
        joined, top = merge(mine_ref[r], got_ref[r ^ 1], table_ref[0])
        tail = joined[:, 256:]
        high = tail.astype(jnp.bfloat16).astype(jnp.float32)
        tail = jnp.where(lanes >= 80, tail + pltpu.roll(tail - high, 8, 1), high)
        tail = jnp.where((lanes >= 64) & (lanes < 72), top, tail)
        out_ref = keep_ref if r < 2 else send_ref
        out_ref[r % 2, :, 0:256] = joined[:, :256].astype(jnp.bfloat16)
        out_ref[r % 2, :, 256:384] = tail.astype(jnp.bfloat16)


def merge_last_kernel(keep_ref, got_ref, table_ref, out_ref):
    lanes = lax.broadcasted_iota(jnp.int32, (TOK, 128), 1)
    for r in range(2):
        joined, top = merge(keep_ref[r], got_ref[r], table_ref[0])
        tail = joined[:, 256:]
        total = tail + pltpu.roll(tail, 120, 1)
        used = (lanes >= 72) & (lanes < 72 + HEADS_HERE)
        inverse = jnp.where(used, 1.0 / jnp.where(used, total, 1.0), 0.0)
        done = joined * spread(inverse, table_ref[1])
        out_ref[r] = done[:, :HALF].astype(jnp.bfloat16)


def project_kernel(place_ref, own_ref, *refs):
    lefts, rights = refs[0:7], refs[7:14]
    w_ref, keep_ref, send_ref, acc = refs[14:]
    zl = place_ref[0]
    acc[...] = dot_f32(own_ref[...].reshape(2 * TOK, HALF), w_ref[zl])
    for k in range(1, 8):

        @pl.when(zl - k >= 0)
        def from_left():
            acc[...] += dot_f32(lefts[k - 1][...].reshape(2 * TOK, HALF), w_ref[jnp.maximum(zl - k, 0)])

        @pl.when(zl + k <= 7)
        def from_right():
            acc[...] += dot_f32(rights[k - 1][...].reshape(2 * TOK, HALF), w_ref[jnp.minimum(zl + k, 7)])

    keep_ref[...] = acc[0:TOK]
    send_ref[...] = acc[TOK:].astype(jnp.bfloat16)


VMEM = pl.BlockSpec(memory_space=pltpu.VMEM)
SMEM = pl.BlockSpec(memory_space=pltpu.SMEM)
PARAMS = pltpu.CompilerParams(vmem_limit_bytes=40 * 1024 * 1024)


def bf16(*shape):
    return jax.ShapeDtypeStruct(shape, jnp.bfloat16)


def on_device(query, key, value, latents, out_weight, level_gate, levels, frame_mask, seed_block):
    x, y = lax.axis_index("x"), lax.axis_index("y")
    zh, c, zl = lax.axis_index("zh"), lax.axis_index("c"), lax.axis_index("zl")
    column = 4 * x + y

    weight_half = lax.all_gather(out_weight, ("x", "y", "zh"), axis=0, tiled=True).reshape(8, HALF, FEAT)

    flags = jnp.pad(frame_mask.astype(jnp.bfloat16), ((0, 15), (0, FEAT - 16)))
    q_own = jnp.concatenate([query, flags], axis=0)
    q_far = move(q_own, lambda x, y, h, c, l: (x, y, 1 - h, c, l))
    qa = jnp.stack([q_own, q_far])
    qb = move(qa, lambda x, y, h, c, l: (x, y, h, 1 - c, l))

    kv0 = jnp.stack([key, value])
    kv4 = move(kv0, lambda x, y, h, c, l: ((x + 1) % 4, y, h, c, l))
    kv1 = move(jnp.where(y == 3, kv4, kv0), lambda x, y, h, c, l: (x, (y + 1) % 4, h, c, l))
    kv3 = move(jnp.where(y == 0, kv0, kv4), lambda x, y, h, c, l: (x, (y - 1) % 4, h, c, l))
    kv2 = move(jnp.where(y >= 2, kv4, kv0), lambda x, y, h, c, l: (x, (y + 2) % 4, h, c, l))

    r = jnp.arange(4, dtype=jnp.int32)[:, None]
    d = jnp.arange(5, dtype=jnp.int32)[None, :]
    inner = 2 * (zh ^ (r >> 1)) + (c ^ (r & 1))
    lag = 4 * d + inner - (2 * zh + c)
    age = (4 * column + inner - seed_block[0] - 1) % 64
    code = jnp.where((lag == 0) | ((lag > 0) & (lag <= 16) & (lag <= age)), lag, -1).astype(jnp.int32)

    select = lax.dynamic_index_in_dim(jnp.asarray(SELECTION, jnp.bfloat16), c, keepdims=False)
    table = lax.dynamic_index_in_dim(jnp.asarray(SPREAD, jnp.bfloat16), c, keepdims=False)

    mine, theirs = pl.pallas_call(
        attend_kernel,
        out_shape=(bf16(4, TOK, WIDE), bf16(4, TOK, WIDE)),
        in_specs=[SMEM] + [VMEM] * 8,
        out_specs=(VMEM, VMEM),
        compiler_params=PARAMS,
        name="attend",
    )(code, qa, qb, kv0, kv1, kv2, kv3, kv4, select)
    got = move(theirs, lambda x, y, h, c, l: (x, y, h, 1 - c, l))
    keep, send = pl.pallas_call(
        merge_cores_kernel,
        out_shape=(bf16(2, TOK, WIDE), bf16(2, TOK, WIDE)),
        in_specs=[VMEM] * 3,
        out_specs=(VMEM, VMEM),
        compiler_params=PARAMS,
        name="merge_cores",
    )(mine, got, table)
    got = move(send, lambda x, y, h, c, l: (x, y, 1 - h, c, l))
    attended = pl.pallas_call(
        merge_last_kernel,
        out_shape=bf16(2, TOK, HALF),
        in_specs=[VMEM] * 3,
        out_specs=VMEM,
        compiler_params=PARAMS,
        name="merge_last",
    )(keep, got, table)

    lefts, rights = [], []
    left = right = attended
    for k in range(7):
        left = move(left, lambda x, y, h, c, l: (x, y, h, c, l + 1) if l < 7 else None)
        right = move(right, lambda x, y, h, c, l: (x, y, h, c, l - 1) if l > 0 else None)
        lefts.append(left)
        rights.append(right)

    keep, send = pl.pallas_call(
        project_kernel,
        out_shape=(jax.ShapeDtypeStruct((TOK, FEAT), jnp.float32), bf16(TOK, FEAT)),
        in_specs=[SMEM] + [VMEM] * 16,
        out_specs=(VMEM, VMEM),
        scratch_shapes=[pltpu.VMEM((2 * TOK, FEAT), jnp.float32)],
        compiler_params=PARAMS,
        name="project",
    )(zl.reshape(1), attended, *lefts, *rights, weight_half)
    got = move(send, lambda x, y, h, c, l: (x, y, h, 1 - c, l))

    level_pick = (jnp.arange(LEVELS, dtype=jnp.int32) == levels[0]).astype(jnp.float32)
    gate_row = jnp.sum(level_pick[:, None] * level_gate, axis=0)
    projected = keep + got.astype(jnp.float32)
    return (latents.astype(jnp.float32) + gate_row[None, :] * projected).astype(jnp.bfloat16)


def solution(mesh):
    fine = Mesh(mesh.devices.reshape(SIZES), AXES)
    win = ("x", "y", "zh", "c")
    in_specs = (
        P(win, "zl"),
        P(win, "zl"),
        P(win, "zl"),
        P(win, "zl"),
        P(win, "zl"),
        P(None, "zl"),
        P(win),
        P(win, None),
        P(),
    )
    return jax.shard_map(
        on_device, mesh=fine, in_specs=in_specs, out_specs=P(win, "zl"), check_vma=False
    )
```

time: 608 us -> 236 us (0.39)
  waiting for transfers between devices: 355 us -> 74.9 us
  starting transfers between devices: 215 us -> 122 us
  Pallas kernels: 0 us -> 14.6 us
  matrix products: 8.92 us -> 0 us
    all_gather x2 -> x1, waiting for transfers between devices: 242 us -> 0.01 us  [on_device(): lax.all_gather(out_weight, ('x', 'y', 'zh'), axis=0, tiled=True)]
    ppermute x16 -> x23, starting transfers between devices: 215 us -> 122 us  [move(): return lax.ppermute(value, AXES, pairs)]
    ppermute x16 -> x23, waiting for transfers between devices: 113 us -> 74.2 us  [move(): return lax.ppermute(value, AXES, pairs)]
    pallas_call x0 -> x4, Pallas kernels: none -> 14.6 us  [the longest x1 10.2 us: on_device(): pl.pallas_call(attend_kernel, out_shape=(bf16(4, TOK, WIDE), bf16(4, TOK,...]
    dot_general x11 -> x0, matrix products: 8.92 us -> none  [the longest x1 5.18 us: on_device(): jnp.dot(all_features, lax.all_gather(out_weight, 'win', axis=0, tiled=Tru...]
  transfers between devices with their start and end apart: 18 -> 24, of which waited for: 18 -> 19; matrix products, arithmetic and copies ran while one was open for 1% -> 2% of each run, Pallas kernels for 0% -> 5%
where the time goes in v1:
time: 236 us; the launch traced here: 233 us
  starting transfers between devices  122 us (52%)
  waiting for transfers between devices  74.9 us (32%)
  between operations  15 us (6%)
  Pallas kernels  14.6 us (6%)
  other arithmetic  3.69 us (2%)
  local copies, waits for them, and re-layouts  3.33 us (1%)
    ppermute x23, starting transfers between devices, move(): return lax.ppermute(value, AXES, pairs)  122 us
    ppermute x23, waiting for transfers between devices, move(): return lax.ppermute(value, AXES, pairs)  74.2 us
    pallas_call x1, Pallas kernels, on_device(): pl.pallas_call(attend_kernel, out_shape=(bf16(4, TOK, WIDE), bf16(4, TOK,...  10.2 us
  transfers between devices with their start and end apart: 24, of which 19 were waited for; matrix products, arithmetic and copies ran while one was open for 2% of the time, Pallas kernels for 5%

profile of v1, /device:TPU:1, one launch (start us, length us, event | category | flops | bytes accessed | tf_op | source)
XLA Modules:
  0.0 233.4 jit_solution(6740688826143804448)
XLA Ops:
  8.3 3.9 %collective-permute-start.2 = (bf16[2,128,640]{2,1,0:T(8,128)(2,1)S(1)}, bf16[2,128,640]{2,1,0:T(8,128)(2,1)S(1)}, u32[]{:S(2)}, u32[]{:S(2)}) collective-permute-start(bf16[2,128,640]{2,1,0:T(8,128)(2,1)S(1)} %pad_maximum_fusion.1.kv0), channel_id=1, source_target_pairs={{0,128},{1,129},{2,130},{3,131},{4,132},{5,133},{6,134},{7,135},{8... | collective-permute-start | bytes 983048 | tf_op jit(solution)/shard_map/ppermute | solution.py:28
  13.9 15.4 %collective-permute-start = (bf16[144,640]{1,0:T(8,128)(2,1)S(1)}, bf16[144,640]{1,0:T(8,128)(2,1)S(1)}, u32[]{:S(2)}, u32[]{:S(2)}) collective-permute-start(bf16[144,640]{1,0:T(8,128)(2,1)S(1)} %get-tuple-element.23), channel_id=1, source_target_pairs={{0,16},{1,17},{2,18},{3,19},{4,20},{5,21},{6,22},{7,23},{8,24},{9,... | collective-permute-start | bytes 552968 | tf_op jit(solution)/shard_map/ppermute | solution.py:28
  32.6 4.7 %collective-permute-start.1 = (bf16[2,144,640]{2,1,0:T(8,128)(2,1)S(1)}, bf16[2,144,640]{2,1,0:T(8,128)(2,1)S(1)}, u32[]{:S(2)}, u32[]{:S(2)}) collective-permute-start(bf16[2,144,640]{2,1,0:T(8,128)(2,1)S(1)} %pad_maximum_fusion.qa_ref), channel_id=1, source_target_pairs={{0,8},{1,9},{2,10},{3,11},{4,12},{5,13},{6,14},{7,15},{8,0},{9,1},... | collective-permute-start | bytes 1105928 | tf_op jit(solution)/shard_map/ppermute | solution.py:28
  37.4 3.2 %collective-permute-start.3 = (bf16[2,128,640]{2,1,0:T(8,128)(2,1)S(1)}, bf16[2,128,640]{2,1,0:T(8,128)(2,1)S(1)}, u32[]{:S(2)}, u32[]{:S(2)}) collective-permute-start(bf16[2,128,640]{2,1,0:T(8,128)(2,1)S(1)} %get-tuple-element.21), channel_id=1, source_target_pairs={{0,32},{1,33},{2,34},{3,35},{4,36},{5,37},{6,38},{7,39},{8,40},{9,... | collective-permute-start | bytes 983048 | tf_op jit(solution)/shard_map/ppermute | solution.py:28
  40.7 4.5 %collective-permute-start.4 = (bf16[2,128,640]{2,1,0:T(8,128)(2,1)S(1)}, bf16[2,128,640]{2,1,0:T(8,128)(2,1)S(1)}, u32[]{:S(2)}, u32[]{:S(2)}) collective-permute-start(bf16[2,128,640]{2,1,0:T(8,128)(2,1)S(1)} %get-tuple-element.20), channel_id=1, source_target_pairs={{0,64},{1,65},{2,66},{3,67},{4,68},{5,69},{6,70},{7,71},{8,72},{9,... | collective-permute-start | bytes 983048 | tf_op jit(solution)/shard_map/ppermute | solution.py:28
  45.2 3.0 %collective-permute-start.5 = (bf16[2,128,640]{2,1,0:T(8,128)(2,1)S(1)}, bf16[2,128,640]{2,1,0:T(8,128)(2,1)S(1)}, u32[]{:S(2)}, u32[]{:S(2)}) collective-permute-start(bf16[2,128,640]{2,1,0:T(8,128)(2,1)S(1)} %get-tuple-element.19), channel_id=1, source_target_pairs={{0,96},{1,97},{2,98},{3,99},{4,100},{5,101},{6,102},{7,103},{8,104... | collective-permute-start | bytes 983048 | tf_op jit(solution)/shard_map/ppermute | solution.py:28
  50.1 8.2 %collective-permute-done.4.kv2 = bf16[2,128,640]{2,1,0:T(8,128)(2,1)S(1)} collective-permute-done((bf16[2,128,640]{2,1,0:T(8,128)(2,1)S(1)}, bf16[2,128,640]{2,1,0:T(8,128)(2,1)S(1)}, u32[]{:S(2)}, u32[]{:S(2)}) %collective-permute-start.4) | collective-permute-done | bytes 327712 | tf_op jit(solution)/shard_map/ppermute | solution.py:28
  59.7 10.2 %attend.1 = (bf16[4,128,384]{2,1,0:T(8,128)(2,1)S(1)}, bf16[4,128,384]{2,1,0:T(8,128)(2,1)S(1)}) custom-call(s32[4,5]{1,0:T(4,128)S(1)} %fusion.2.code_ref, bf16[2,144,640]{2,1,0:T(8,128)(2,1)S(1)} %pad_maximum_fusion.qa_ref, bf16[2,144,640]{2,1,0:T(8,128)(2,1)S(1)} %collective-permute-done.1.qb_ref, bf16[2,128,640]{2,1,0:T(8,128)(2,1)S(1)} %pad_maximum_fusion.1.kv0, ...), custom_call_target="tpu_custom_call" | custom-call | tf_op jit(solution)/shard_map/attend/pallas_call | solution.py:203
  69.9 2.9 %collective-permute-start.6 = (bf16[4,128,384]{2,1,0:T(8,128)(2,1)S(1)}, bf16[4,128,384]{2,1,0:T(8,128)(2,1)S(1)}, u32[]{:S(2)}, u32[]{:S(2)}) collective-permute-start(bf16[4,128,384]{2,1,0:T(8,128)(2,1)S(1)} %get-tuple-element.12), channel_id=1, source_target_pairs={{0,8},{1,9},{2,10},{3,11},{4,12},{5,13},{6,14},{7,15},{8,0},{9,1},... | collective-permute-start | bytes 1179656 | tf_op jit(solution)/shard_map/ppermute | solution.py:28
  74.8 12.2 %collective-permute-start.7 = (bf16[2,128,384]{2,1,0:T(8,128)(2,1)S(1)}, bf16[2,128,384]{2,1,0:T(8,128)(2,1)S(1)}, u32[]{:S(2)}, u32[]{:S(2)}) collective-permute-start(bf16[2,128,384]{2,1,0:T(8,128)(2,1)S(1)} %get-tuple-element.14), channel_id=1, source_target_pairs={{0,16},{1,17},{2,18},{3,19},{4,20},{5,21},{6,22},{7,23},{8,24},{9,... | collective-permute-start | bytes 589832 | tf_op jit(solution)/shard_map/ppermute | solution.py:28
  87.0 12.9 %collective-permute-done.7.got_ref = bf16[2,128,384]{2,1,0:T(8,128)(2,1)S(1)} collective-permute-done((bf16[2,128,384]{2,1,0:T(8,128)(2,1)S(1)}, bf16[2,128,384]{2,1,0:T(8,128)(2,1)S(1)}, u32[]{:S(2)}, u32[]{:S(2)}) %collective-permute-start.7) | collective-permute-done | bytes 196640 | tf_op jit(solution)/shard_map/ppermute | solution.py:28
  100.8 27.1 %collective-permute-start.8 = (bf16[2,128,320]{2,1,0:T(8,128)(2,1)S(1)}, bf16[2,128,320]{2,1,0:T(8,128)(2,1)S(1)}, u32[]{:S(2)}, u32[]{:S(2)}) collective-permute-start(bf16[2,128,320]{2,1,0:T(8,128)(2,1)S(1)} %merge_last.1.own_ref), channel_id=1, source_target_pairs={{0,1},{1,2},{2,3},{3,4},{4,5},{5,6},{6,7},{8,9},{9,10},{10,11},{11... | collective-permute-start | bytes 491528 | tf_op jit(solution)/shard_map/ppermute | solution.py:28
  129.2 8.0 %collective-permute-done.8.refs_0_ = bf16[2,128,320]{2,1,0:T(8,128)(2,1)S(1)} collective-permute-done((bf16[2,128,320]{2,1,0:T(8,128)(2,1)S(1)}, bf16[2,128,320]{2,1,0:T(8,128)(2,1)S(1)}, u32[]{:S(2)}, u32[]{:S(2)}) %collective-permute-start.8) | collective-permute-done | bytes 163872 | tf_op jit(solution)/shard_map/ppermute | solution.py:28
  137.2 4.4 %collective-permute-start.9 = (bf16[2,128,320]{2,1,0:T(8,128)(2,1)S(1)}, bf16[2,128,320]{2,1,0:T(8,128)(2,1)S(1)}, u32[]{:S(2)}, u32[]{:S(2)}) collective-permute-start(bf16[2,128,320]{2,1,0:T(8,128)(2,1)S(1)} %collective-permute-done.8.refs_0_), channel_id=1, source_target_pairs={{0,1},{1,2},{2,3},{3,4},{4,5},{5,6},{6,7},{8,9},{9,10},{10,11},{11... | collective-permute-start | bytes 491528 | tf_op jit(solution)/shard_map/ppermute | solution.py:28
  141.6 2.9 %collective-permute-done.15.refs_7_ = bf16[2,128,320]{2,1,0:T(8,128)(2,1)S(1)} collective-permute-done((bf16[2,128,320]{2,1,0:T(8,128)(2,1)S(1)}, bf16[2,128,320]{2,1,0:T(8,128)(2,1)S(1)}, u32[]{:S(2)}, u32[]{:S(2)}) %collective-permute-start.15) | collective-permute-done | bytes 163872 | tf_op jit(solution)/shard_map/ppermute | solution.py:28
  145.8 23.0 %collective-permute-done.9.refs_1_ = bf16[2,128,320]{2,1,0:T(8,128)(2,1)S(1)} collective-permute-done((bf16[2,128,320]{2,1,0:T(8,128)(2,1)S(1)}, bf16[2,128,320]{2,1,0:T(8,128)(2,1)S(1)}, u32[]{:S(2)}, u32[]{:S(2)}) %collective-permute-start.9) | collective-permute-done | bytes 163872 | tf_op jit(solution)/shard_map/ppermute | solution.py:28
  168.8 6.6 %collective-permute-start.10 = (bf16[2,128,320]{2,1,0:T(8,128)(2,1)S(1)}, bf16[2,128,320]{2,1,0:T(8,128)(2,1)S(1)}, u32[]{:S(2)}, u32[]{:S(2)}) collective-permute-start(bf16[2,128,320]{2,1,0:T(8,128)(2,1)S(1)} %collective-permute-done.9.refs_1_), channel_id=1, source_target_pairs={{0,1},{1,2},{2,3},{3,4},{4,5},{5,6},{6,7},{8,9},{9,10},{10,11},{11... | collective-permute-start | bytes 491528 | tf_op jit(solution)/shard_map/ppermute | solution.py:28
  179.4 4.0 %collective-permute-start.11 = (bf16[2,128,320]{2,1,0:T(8,128)(2,1)S(1)}, bf16[2,128,320]{2,1,0:T(8,128)(2,1)S(1)}, u32[]{:S(2)}, u32[]{:S(2)}) collective-permute-start(bf16[2,128,320]{2,1,0:T(8,128)(2,1)S(1)} %collective-permute-done.10.refs_2_), channel_id=1, source_target_pairs={{0,1},{1,2},{2,3},{3,4},{4,5},{5,6},{6,7},{8,9},{9,10},{10,11},{11... | collective-permute-start | bytes 491528 | tf_op jit(solution)/shard_map/ppermute | solution.py:28
  186.4 4.0 %collective-permute-start.12 = (bf16[2,128,320]{2,1,0:T(8,128)(2,1)S(1)}, bf16[2,128,320]{2,1,0:T(8,128)(2,1)S(1)}, u32[]{:S(2)}, u32[]{:S(2)}) collective-permute-start(bf16[2,128,320]{2,1,0:T(8,128)(2,1)S(1)} %collective-permute-done.11.refs_3_), channel_id=1, source_target_pairs={{0,1},{1,2},{2,3},{3,4},{4,5},{5,6},{6,7},{8,9},{9,10},{10,11},{11... | collective-permute-start | bytes 491528 | tf_op jit(solution)/shard_map/ppermute | solution.py:28
  193.0 4.1 %collective-permute-start.13 = (bf16[2,128,320]{2,1,0:T(8,128)(2,1)S(1)}, bf16[2,128,320]{2,1,0:T(8,128)(2,1)S(1)}, u32[]{:S(2)}, u32[]{:S(2)}) collective-permute-start(bf16[2,128,320]{2,1,0:T(8,128)(2,1)S(1)} %collective-permute-done.12.refs_4_), channel_id=1, source_target_pairs={{0,1},{1,2},{2,3},{3,4},{4,5},{5,6},{6,7},{8,9},{9,10},{10,11},{11... | collective-permute-start | bytes 491528 | tf_op jit(solution)/shard_map/ppermute | solution.py:28
  199.7 4.1 %collective-permute-start.14 = (bf16[2,128,320]{2,1,0:T(8,128)(2,1)S(1)}, bf16[2,128,320]{2,1,0:T(8,128)(2,1)S(1)}, u32[]{:S(2)}, u32[]{:S(2)}) collective-permute-start(bf16[2,128,320]{2,1,0:T(8,128)(2,1)S(1)} %collective-permute-done.13.refs_5_), channel_id=1, source_target_pairs={{0,1},{1,2},{2,3},{3,4},{4,5},{5,6},{6,7},{8,9},{9,10},{10,11},{11... | collective-permute-start | bytes 491528 | tf_op jit(solution)/shard_map/ppermute | solution.py:28
  206.4 5.0 %collective-permute-done.21.refs_13_ = bf16[2,128,320]{2,1,0:T(8,128)(2,1)S(1)} collective-permute-done((bf16[2,128,320]{2,1,0:T(8,128)(2,1)S(1)}, bf16[2,128,320]{2,1,0:T(8,128)(2,1)S(1)}, u32[]{:S(2)}, u32[]{:S(2)}) %collective-permute-start.21) | collective-permute-done | bytes 163872 | tf_op jit(solution)/shard_map/ppermute | solution.py:28
  213.3 2.9 %project.1 = (f32[128,640]{1,0:T(8,128)S(1)}, bf16[128,640]{1,0:T(8,128)(2,1)S(1)}) custom-call(s32[1]{0:T(128)} %bitcast.1.place_ref, bf16[2,128,320]{2,1,0:T(8,128)(2,1)S(1)} %merge_last.1.own_ref, bf16[2,128,320]{2,1,0:T(8,128)(2,1)S(1)} %collective-permute-done.8.refs_0_, bf16[2,128,320]{2,1,0:T(8,128)(2,1)S(1)} %collective-permute-done.9.refs_1_, ...), custom_call_target="tpu_custom_call" | custom-call | tf_op jit(solution)/shard_map/project/pallas_call | solution.py:238
  216.2 8.6 %collective-permute-start.22 = (bf16[128,640]{1,0:T(8,128)(2,1)S(1)}, bf16[128,640]{1,0:T(8,128)(2,1)S(1)}, u32[]{:S(2)}, u32[]{:S(2)}) collective-permute-start(bf16[128,640]{1,0:T(8,128)(2,1)S(1)} %get-tuple-element.16), channel_id=1, source_target_pairs={{0,8},{1,9},{2,10},{3,11},{4,12},{5,13},{6,14},{7,15},{8,0},{9,1},... | collective-permute-start | bytes 491528 | tf_op jit(solution)/shard_map/ppermute | solution.py:28
  (54 shorter events, 32.5 us)
Async XLA Ops:
  6.5 204.8 %all-gather.2.cloned.1.call-start = ((), (), s32[]{:S(2)}) async-start(), calls=%async_computation | async-start | bytes 3379200 | tf_op jit(solution)/shard_map/all_gather | solution.py:179
  8.3 29.0 %collective-permute-start.2 = (bf16[2,128,640]{2,1,0:T(8,128)(2,1)S(1)}, bf16[2,128,640]{2,1,0:T(8,128)(2,1)S(1)}, u32[]{:S(2)}, u32[]{:S(2)}) collective-permute-start(bf16[2,128,640]{2,1,0:T(8,128)(2,1)S(1)} %pad_maximum_fusion.1.kv0), channel_id=1, source_target_pairs={{0,128},{1,129},{2,130},{3,131},{4,132},{5,133},{6,134},{7,135},{8... | collective-permute-start | bytes 983048 | tf_op jit(solution)/shard_map/ppermute | solution.py:28
  13.9 18.7 %collective-permute-start = (bf16[144,640]{1,0:T(8,128)(2,1)S(1)}, bf16[144,640]{1,0:T(8,128)(2,1)S(1)}, u32[]{:S(2)}, u32[]{:S(2)}) collective-permute-start(bf16[144,640]{1,0:T(8,128)(2,1)S(1)} %get-tuple-element.23), channel_id=1, source_target_pairs={{0,16},{1,17},{2,18},{3,19},{4,20},{5,21},{6,22},{7,23},{8,24},{9,... | collective-permute-start | bytes 552968 | tf_op jit(solution)/shard_map/ppermute | solution.py:28
  32.6 15.7 %collective-permute-start.1 = (bf16[2,144,640]{2,1,0:T(8,128)(2,1)S(1)}, bf16[2,144,640]{2,1,0:T(8,128)(2,1)S(1)}, u32[]{:S(2)}, u32[]{:S(2)}) collective-permute-start(bf16[2,144,640]{2,1,0:T(8,128)(2,1)S(1)} %pad_maximum_fusion.qa_ref), channel_id=1, source_target_pairs={{0,8},{1,9},{2,10},{3,11},{4,12},{5,13},{6,14},{7,15},{8,0},{9,1},... | collective-permute-start | bytes 1105928 | tf_op jit(solution)/shard_map/ppermute | solution.py:28
  37.4 12.6 %collective-permute-start.3 = (bf16[2,128,640]{2,1,0:T(8,128)(2,1)S(1)}, bf16[2,128,640]{2,1,0:T(8,128)(2,1)S(1)}, u32[]{:S(2)}, u32[]{:S(2)}) collective-permute-start(bf16[2,128,640]{2,1,0:T(8,128)(2,1)S(1)} %get-tuple-element.21), channel_id=1, source_target_pairs={{0,32},{1,33},{2,34},{3,35},{4,36},{5,37},{6,38},{7,39},{8,40},{9,... | collective-permute-start | bytes 983048 | tf_op jit(solution)/shard_map/ppermute | solution.py:28
  40.7 17.6 %collective-permute-start.4 = (bf16[2,128,640]{2,1,0:T(8,128)(2,1)S(1)}, bf16[2,128,640]{2,1,0:T(8,128)(2,1)S(1)}, u32[]{:S(2)}, u32[]{:S(2)}) collective-permute-start(bf16[2,128,640]{2,1,0:T(8,128)(2,1)S(1)} %get-tuple-element.20), channel_id=1, source_target_pairs={{0,64},{1,65},{2,66},{3,67},{4,68},{5,69},{6,70},{7,71},{8,72},{9,... | collective-permute-start | bytes 983048 | tf_op jit(solution)/shard_map/ppermute | solution.py:28
  45.2 14.5 %collective-permute-start.5 = (bf16[2,128,640]{2,1,0:T(8,128)(2,1)S(1)}, bf16[2,128,640]{2,1,0:T(8,128)(2,1)S(1)}, u32[]{:S(2)}, u32[]{:S(2)}) collective-permute-start(bf16[2,128,640]{2,1,0:T(8,128)(2,1)S(1)} %get-tuple-element.19), channel_id=1, source_target_pairs={{0,96},{1,97},{2,98},{3,99},{4,100},{5,101},{6,102},{7,103},{8,104... | collective-permute-start | bytes 983048 | tf_op jit(solution)/shard_map/ppermute | solution.py:28
  69.9 4.2 %collective-permute-start.6 = (bf16[4,128,384]{2,1,0:T(8,128)(2,1)S(1)}, bf16[4,128,384]{2,1,0:T(8,128)(2,1)S(1)}, u32[]{:S(2)}, u32[]{:S(2)}) collective-permute-start(bf16[4,128,384]{2,1,0:T(8,128)(2,1)S(1)} %get-tuple-element.12), channel_id=1, source_target_pairs={{0,8},{1,9},{2,10},{3,11},{4,12},{5,13},{6,14},{7,15},{8,0},{9,1},... | collective-permute-start | bytes 1179656 | tf_op jit(solution)/shard_map/ppermute | solution.py:28
  74.8 25.1 %collective-permute-start.7 = (bf16[2,128,384]{2,1,0:T(8,128)(2,1)S(1)}, bf16[2,128,384]{2,1,0:T(8,128)(2,1)S(1)}, u32[]{:S(2)}, u32[]{:S(2)}) collective-permute-start(bf16[2,128,384]{2,1,0:T(8,128)(2,1)S(1)} %get-tuple-element.14), channel_id=1, source_target_pairs={{0,16},{1,17},{2,18},{3,19},{4,20},{5,21},{6,22},{7,23},{8,24},{9,... | collective-permute-start | bytes 589832 | tf_op jit(solution)/shard_map/ppermute | solution.py:28
  100.8 36.3 %collective-permute-start.8 = (bf16[2,128,320]{2,1,0:T(8,128)(2,1)S(1)}, bf16[2,128,320]{2,1,0:T(8,128)(2,1)S(1)}, u32[]{:S(2)}, u32[]{:S(2)}) collective-permute-start(bf16[2,128,320]{2,1,0:T(8,128)(2,1)S(1)} %merge_last.1.own_ref), channel_id=1, source_target_pairs={{0,1},{1,2},{2,3},{3,4},{4,5},{5,6},{6,7},{8,9},{9,10},{10,11},{11... | collective-permute-start | bytes 491528 | tf_op jit(solution)/shard_map/ppermute | solution.py:28
  127.9 16.6 %collective-permute-start.15 = (bf16[2,128,320]{2,1,0:T(8,128)(2,1)S(1)}, bf16[2,128,320]{2,1,0:T(8,128)(2,1)S(1)}, u32[]{:S(2)}, u32[]{:S(2)}) collective-permute-start(bf16[2,128,320]{2,1,0:T(8,128)(2,1)S(1)} %merge_last.1.own_ref), channel_id=1, source_target_pairs={{1,0},{2,1},{3,2},{4,3},{5,4},{6,5},{7,6},{9,8},{10,9},{11,10},{12... | collective-permute-start | bytes 491528 | tf_op jit(solution)/shard_map/ppermute | solution.py:28
  137.2 31.6 %collective-permute-start.9 = (bf16[2,128,320]{2,1,0:T(8,128)(2,1)S(1)}, bf16[2,128,320]{2,1,0:T(8,128)(2,1)S(1)}, u32[]{:S(2)}, u32[]{:S(2)}) collective-permute-start(bf16[2,128,320]{2,1,0:T(8,128)(2,1)S(1)} %collective-permute-done.8.refs_0_), channel_id=1, source_target_pairs={{0,1},{1,2},{2,3},{3,4},{4,5},{5,6},{6,7},{8,9},{9,10},{10,11},{11... | collective-permute-start | bytes 491528 | tf_op jit(solution)/shard_map/ppermute | solution.py:28
  144.5 33.6 %collective-permute-start.16 = (bf16[2,128,320]{2,1,0:T(8,128)(2,1)S(1)}, bf16[2,128,320]{2,1,0:T(8,128)(2,1)S(1)}, u32[]{:S(2)}, u32[]{:S(2)}) collective-permute-start(bf16[2,128,320]{2,1,0:T(8,128)(2,1)S(1)} %collective-permute-done.15.refs_7_), channel_id=1, source_target_pairs={{1,0},{2,1},{3,2},{4,3},{5,4},{6,5},{7,6},{9,8},{10,9},{11,10},{12... | collective-permute-start | bytes 491528 | tf_op jit(solution)/shard_map/ppermute | solution.py:28
  168.8 10.6 %collective-permute-start.10 = (bf16[2,128,320]{2,1,0:T(8,128)(2,1)S(1)}, bf16[2,128,320]{2,1,0:T(8,128)(2,1)S(1)}, u32[]{:S(2)}, u32[]{:S(2)}) collective-permute-start(bf16[2,128,320]{2,1,0:T(8,128)(2,1)S(1)} %collective-permute-done.9.refs_1_), channel_id=1, source_target_pairs={{0,1},{1,2},{2,3},{3,4},{4,5},{5,6},{6,7},{8,9},{9,10},{10,11},{11... | collective-permute-start | bytes 491528 | tf_op jit(solution)/shard_map/ppermute | solution.py:28
  178.1 7.0 %collective-permute-start.17 = (bf16[2,128,320]{2,1,0:T(8,128)(2,1)S(1)}, bf16[2,128,320]{2,1,0:T(8,128)(2,1)S(1)}, u32[]{:S(2)}, u32[]{:S(2)}) collective-permute-start(bf16[2,128,320]{2,1,0:T(8,128)(2,1)S(1)} %collective-permute-done.16.refs_8_), channel_id=1, source_target_pairs={{1,0},{2,1},{3,2},{4,3},{5,4},{6,5},{7,6},{9,8},{10,9},{11,10},{12... | collective-permute-start | bytes 491528 | tf_op jit(solution)/shard_map/ppermute | solution.py:28
  179.4 7.0 %collective-permute-start.11 = (bf16[2,128,320]{2,1,0:T(8,128)(2,1)S(1)}, bf16[2,128,320]{2,1,0:T(8,128)(2,1)S(1)}, u32[]{:S(2)}, u32[]{:S(2)}) collective-permute-start(bf16[2,128,320]{2,1,0:T(8,128)(2,1)S(1)} %collective-permute-done.10.refs_2_), channel_id=1, source_target_pairs={{0,1},{1,2},{2,3},{3,4},{4,5},{5,6},{6,7},{8,9},{9,10},{10,11},{11... | collective-permute-start | bytes 491528 | tf_op jit(solution)/shard_map/ppermute | solution.py:28
  185.1 6.4 %collective-permute-start.18 = (bf16[2,128,320]{2,1,0:T(8,128)(2,1)S(1)}, bf16[2,128,320]{2,1,0:T(8,128)(2,1)S(1)}, u32[]{:S(2)}, u32[]{:S(2)}) collective-permute-start(bf16[2,128,320]{2,1,0:T(8,128)(2,1)S(1)} %collective-permute-done.17.refs_9_), channel_id=1, source_target_pairs={{1,0},{2,1},{3,2},{4,3},{5,4},{6,5},{7,6},{9,8},{10,9},{11,10},{12... | collective-permute-start | bytes 491528 | tf_op jit(solution)/shard_map/ppermute | solution.py:28
  186.4 6.6 %collective-permute-start.12 = (bf16[2,128,320]{2,1,0:T(8,128)(2,1)S(1)}, bf16[2,128,320]{2,1,0:T(8,128)(2,1)S(1)}, u32[]{:S(2)}, u32[]{:S(2)}) collective-permute-start(bf16[2,128,320]{2,1,0:T(8,128)(2,1)S(1)} %collective-permute-done.11.refs_3_), channel_id=1, source_target_pairs={{0,1},{1,2},{2,3},{3,4},{4,5},{5,6},{6,7},{8,9},{9,10},{10,11},{11... | collective-permute-start | bytes 491528 | tf_op jit(solution)/shard_map/ppermute | solution.py:28
  191.5 6.4 %collective-permute-start.19 = (bf16[2,128,320]{2,1,0:T(8,128)(2,1)S(1)}, bf16[2,128,320]{2,1,0:T(8,128)(2,1)S(1)}, u32[]{:S(2)}, u32[]{:S(2)}) collective-permute-start(bf16[2,128,320]{2,1,0:T(8,128)(2,1)S(1)} %collective-permute-done.18.refs_10_), channel_id=1, source_target_pairs={{1,0},{2,1},{3,2},{4,3},{5,4},{6,5},{7,6},{9,8},{10,9},{11,10},{12... | collective-permute-start | bytes 491528 | tf_op jit(solution)/shard_map/ppermute | solution.py:28
  193.0 6.7 %collective-permute-start.13 = (bf16[2,128,320]{2,1,0:T(8,128)(2,1)S(1)}, bf16[2,128,320]{2,1,0:T(8,128)(2,1)S(1)}, u32[]{:S(2)}, u32[]{:S(2)}) collective-permute-start(bf16[2,128,320]{2,1,0:T(8,128)(2,1)S(1)} %collective-permute-done.12.refs_4_), channel_id=1, source_target_pairs={{0,1},{1,2},{2,3},{3,4},{4,5},{5,6},{6,7},{8,9},{9,10},{10,11},{11... | collective-permute-start | bytes 491528 | tf_op jit(solution)/shard_map/ppermute | solution.py:28
  197.9 6.4 %collective-permute-start.20 = (bf16[2,128,320]{2,1,0:T(8,128)(2,1)S(1)}, bf16[2,128,320]{2,1,0:T(8,128)(2,1)S(1)}, u32[]{:S(2)}, u32[]{:S(2)}) collective-permute-start(bf16[2,128,320]{2,1,0:T(8,128)(2,1)S(1)} %collective-permute-done.19.refs_11_), channel_id=1, source_target_pairs={{1,0},{2,1},{3,2},{4,3},{5,4},{6,5},{7,6},{9,8},{10,9},{11,10},{12... | collective-permute-start | bytes 491528 | tf_op jit(solution)/shard_map/ppermute | solution.py:28
  199.7 6.7 %collective-permute-start.14 = (bf16[2,128,320]{2,1,0:T(8,128)(2,1)S(1)}, bf16[2,128,320]{2,1,0:T(8,128)(2,1)S(1)}, u32[]{:S(2)}, u32[]{:S(2)}) collective-permute-start(bf16[2,128,320]{2,1,0:T(8,128)(2,1)S(1)} %collective-permute-done.13.refs_5_), channel_id=1, source_target_pairs={{0,1},{1,2},{2,3},{3,4},{4,5},{5,6},{6,7},{8,9},{9,10},{10,11},{11... | collective-permute-start | bytes 491528 | tf_op jit(solution)/shard_map/ppermute | solution.py:28
  204.3 7.0 %collective-permute-start.21 = (bf16[2,128,320]{2,1,0:T(8,128)(2,1)S(1)}, bf16[2,128,320]{2,1,0:T(8,128)(2,1)S(1)}, u32[]{:S(2)}, u32[]{:S(2)}) collective-permute-start(bf16[2,128,320]{2,1,0:T(8,128)(2,1)S(1)} %collective-permute-done.20.refs_12_), channel_id=1, source_target_pairs={{1,0},{2,1},{3,2},{4,3},{5,4},{6,5},{7,6},{9,8},{10,9},{11,10},{12... | collective-permute-start | bytes 491528 | tf_op jit(solution)/shard_map/ppermute | solution.py:28
  216.2 9.6 %collective-permute-start.22 = (bf16[128,640]{1,0:T(8,128)(2,1)S(1)}, bf16[128,640]{1,0:T(8,128)(2,1)S(1)}, u32[]{:S(2)}, u32[]{:S(2)}) collective-permute-start(bf16[128,640]{1,0:T(8,128)(2,1)S(1)} %get-tuple-element.16), channel_id=1, source_target_pairs={{0,8},{1,9},{2,10},{3,11},{4,12},{5,13},{6,14},{7,15},{8,0},{9,1},... | collective-permute-start | bytes 491528 | tf_op jit(solution)/shard_map/ppermute | solution.py:28
  (6 other events, 127.8 us)
Sparse Core Ops, SparseCore 0:
  11.6 138.9 all-gather.1

commit v2 on v1

v2 whole, which is shorter than its diff:
```python
import jax
import jax.numpy as jnp
import numpy as np
from jax import lax
from jax.experimental import pallas as pl
from jax.experimental.pallas import tpu as pltpu
from jax.sharding import Mesh, PartitionSpec as P

HD = 128
TOK = 128
LEVELS = 8
HEADS_HERE = 5
FEAT = 640
HALF = 320
WIDE = 384
HIDDEN = -(2.0**100)
SCORE_SCALE = 1.4426950408889634 * HD**-0.5
AXES = ("x", "y", "zh", "c", "zl")
SIZES = (4, 4, 2, 2, 8)


def move(value, rule):
    pairs = []
    for source, place in enumerate(np.ndindex(*SIZES)):
        target = rule(*place)
        if target is not None:
            pairs.append((source, int(np.ravel_multi_index(target, SIZES))))
    return lax.ppermute(value, AXES, pairs)


def half_of_feature(half, lane):
    return (2 * (lane // 80) + half) * 80 + lane % 80


def selection_tables():
    tables = np.zeros((2, 768, 768), np.float32)
    for mine in range(2):
        for slot, half in enumerate((mine, 1 - mine)):
            base = slot * WIDE
            for lane in range(HALF):
                tables[mine, half_of_feature(half, lane), base + lane] = 1
            for stat in range(24):
                tables[mine, FEAT + stat, base + HALF + stat] = 1
    return tables


def spread_tables():
    tables = np.zeros((2, 2, 128, WIDE), np.float32)
    for half in range(2):
        for lane in range(HALF):
            head = half_of_feature(half, lane) // HD
            tables[half, 0, 64 + head, lane] = 1
            tables[half, 1, 72 + head, lane] = 1
        for head in range(HEADS_HERE):
            tables[half, 0, 64 + head, HALF + 8 + head] = 1
            tables[half, 0, 64 + head, HALF + 16 + head] = 1
    return tables


SELECTION = selection_tables()
SPREAD = spread_tables()


def dot_f32(a, b):
    return jnp.dot(a, b, preferred_element_type=jnp.float32)


def attend_kernel(code_ref, qa_ref, qb_ref, kv0, kv1, kv2, kv3, kv4, select_ref, mine_ref, theirs_ref, all_ref):
    kvs = (kv0, kv1, kv2, kv3, kv4)
    lane = lax.broadcasted_iota(jnp.int32, (1, 128), 1)
    lanes = lax.broadcasted_iota(jnp.int32, (TOK, 128), 1)
    biases = []
    for r in range(4):
        q_ref = qa_ref if r % 2 == 0 else qb_ref
        flags = q_ref[r // 2, TOK : TOK + 16, 0:128].astype(jnp.float32)[0:1]
        row = []
        for d in range(5):
            code = code_ref[r, d]
            hit = jnp.sum(jnp.where(lane == code - 1, flags, 0.0), axis=1, keepdims=True)
            hit = jnp.where(code == 0, 1.0, hit)
            row.append(jnp.broadcast_to(jnp.where(hit > 0.5, 0.0, HIDDEN), (1, 128)))
        biases.append(jnp.concatenate(row, axis=1))
    stats = [jnp.zeros((TOK, 128), jnp.float32) for r in range(4)]
    for h in range(HEADS_HERE):
        cols = slice(h * HD, (h + 1) * HD)
        keys = jnp.concatenate([kv[0, :, cols] for kv in kvs], axis=0)
        values = jnp.concatenate([kv[1, :, cols] for kv in kvs], axis=0)
        queries = jnp.concatenate(
            [(qa_ref if r % 2 == 0 else qb_ref)[r // 2, 0:TOK, cols] for r in range(4)], axis=0
        )
        scores = lax.dot_general(queries, keys, (((1,), (1,)), ((), ())), preferred_element_type=jnp.float32)
        parts = []
        for r in range(4):
            part = scores[r * TOK : (r + 1) * TOK] * SCORE_SCALE + biases[r]
            top = jnp.max(part, axis=1, keepdims=True).astype(jnp.bfloat16).astype(jnp.float32)
            expo = jnp.exp2(part - top)
            total = jnp.sum(expo, axis=1, keepdims=True)
            total_hi = total.astype(jnp.bfloat16).astype(jnp.float32)
            parts.append(expo.astype(jnp.bfloat16))
            stats[r] = jnp.where(lanes == h, top, stats[r])
            stats[r] = jnp.where(lanes == 8 + h, total_hi, stats[r])
            stats[r] = jnp.where(lanes == 16 + h, total - total_hi, stats[r])
        summed = dot_f32(jnp.concatenate(parts, axis=0), values)
        all_ref[:, cols] = summed.astype(jnp.bfloat16)
    for r in range(4):
        all_ref[r * TOK : (r + 1) * TOK, FEAT:] = stats[r].astype(jnp.bfloat16)
    mine_ref[...] = dot_f32(all_ref[...], select_ref[:, :WIDE]).astype(jnp.bfloat16).reshape(4, TOK, WIDE)
    theirs_ref[...] = dot_f32(all_ref[...], select_ref[:, WIDE:]).astype(jnp.bfloat16).reshape(4, TOK, WIDE)


def spread(factor, table):
    high = factor.astype(jnp.bfloat16)
    low = (factor - high.astype(jnp.float32)).astype(jnp.bfloat16)
    return dot_f32(high, table) + dot_f32(low, table)


def merge(first, second, table):
    one, two = first.astype(jnp.float32), second.astype(jnp.float32)
    s1, s2 = one[:, 256:], two[:, 256:]
    top = jnp.maximum(s1, s2)
    joined = one * spread(jnp.exp2(s1 - top), table) + two * spread(jnp.exp2(s2 - top), table)
    return joined, top


def merge_cores_kernel(place_ref, mine_ref, got_ref, table_ref, out_ref):
    lanes = lax.broadcasted_iota(jnp.int32, (TOK, 128), 1)
    for r in range(4):
        joined, top = merge(mine_ref[r], got_ref[r ^ 1], table_ref[0])
        tail = joined[:, 256:]
        high = tail.astype(jnp.bfloat16).astype(jnp.float32)
        tail = jnp.where(lanes >= 80, tail + pltpu.roll(tail - high, 8, 1), high)
        tail = jnp.where((lanes >= 64) & (lanes < 72), top, tail)
        to = place_ref[0] ^ (r // 2)
        out_ref[to, r % 2, :, 0:256] = joined[:, :256].astype(jnp.bfloat16)
        out_ref[to, r % 2, :, 256:384] = tail.astype(jnp.bfloat16)


def merge_last_kernel(both_ref, table_ref, out_ref):
    lanes = lax.broadcasted_iota(jnp.int32, (TOK, 128), 1)
    ends = []
    for r in range(2):
        joined, top = merge(both_ref[0, r], both_ref[1, r], table_ref[0])
        tail = joined[:, 256:]
        total = tail + pltpu.roll(tail, 120, 1)
        used = (lanes >= 72) & (lanes < 72 + HEADS_HERE)
        inverse = jnp.where(used, 1.0 / jnp.where(used, total, 1.0), 0.0)
        done = joined * spread(inverse, table_ref[1])
        out_ref[:, r * 256 : (r + 1) * 256] = done[:, :256].astype(jnp.bfloat16)
        ends.append(done[:, 256:])
    out_ref[:, 512:640] = jnp.where(lanes < 64, ends[0], pltpu.roll(ends[1], 64, 1)).astype(jnp.bfloat16)


def project_kernel(place_ref, all_ref, w_ref, keep_ref, send_ref):
    side = place_ref[0]
    here = jnp.zeros((2 * TOK, FEAT), jnp.float32)
    there = jnp.zeros((2 * TOK, FEAT), jnp.float32)
    for near in range(2):
        for odd in range(2):
            rows = all_ref[2 * near + odd]
            ends = rows[:, 512:640]
            turned = pltpu.roll(ends.astype(jnp.float32), 64, 1).astype(jnp.bfloat16)
            wide = jnp.concatenate([rows[:, 0:256], rows[:, 256:512]], axis=0)
            narrow = jnp.concatenate([ends[:, 0:64], turned[:, 0:64]], axis=0)
            w_here = w_ref.at[2 * side + near, odd]
            w_there = w_ref.at[3 - 2 * side - near, odd]
            here = here + dot_f32(wide, w_here[0:256]) + dot_f32(narrow, w_here[256:320])
            there = there + dot_f32(wide, w_there[0:256]) + dot_f32(narrow, w_there[256:320])
    keep_ref[0] = here[0:TOK]
    keep_ref[1] = there[0:TOK]
    send_ref[0] = here[TOK:].astype(jnp.bfloat16)
    send_ref[1] = there[TOK:].astype(jnp.bfloat16)


VMEM = pl.BlockSpec(memory_space=pltpu.VMEM)
SMEM = pl.BlockSpec(memory_space=pltpu.SMEM)
PARAMS = pltpu.CompilerParams(vmem_limit_bytes=40 * 1024 * 1024)


def bf16(*shape):
    return jax.ShapeDtypeStruct(shape, jnp.bfloat16)


def on_device(query, key, value, latents, out_weight, level_gate, levels, frame_mask, seed_block):
    x, y = lax.axis_index("x"), lax.axis_index("y")
    zh, c, zl = lax.axis_index("zh"), lax.axis_index("c"), lax.axis_index("zl")
    column = 4 * x + y

    valid = x // 2 == zl // 4
    w_one = move(
        out_weight,
        lambda x, y, h, c, l: (x, y, 1 - h, c, l) if x // 2 == l // 4 else (3 - x, y, h, c, l ^ 4),
    )
    w_two = move(
        out_weight,
        lambda x, y, h, c, l: None if x // 2 == l // 4 else (3 - x, y, 1 - h, c, l ^ 4),
    )
    w_same = jnp.where(valid, out_weight, w_one)
    w_other = jnp.where(valid, w_one, w_two)
    w_pair = jnp.stack([jnp.where(zh == 0, w_same, w_other), jnp.where(zh == 0, w_other, w_same)])
    weight = lax.all_gather(w_pair, ("x", "y"), axis=0).reshape(4, 2, HALF, FEAT)

    flags = jnp.pad(frame_mask.astype(jnp.bfloat16), ((0, 15), (0, FEAT - 16)))
    q_own = jnp.concatenate([query, flags], axis=0)
    q_far = move(q_own, lambda x, y, h, c, l: (x, y, 1 - h, c, l))
    qa = jnp.stack([q_own, q_far])
    qb = move(qa, lambda x, y, h, c, l: (x, y, h, 1 - c, l))

    kv0 = jnp.stack([key, value])
    kv4 = move(kv0, lambda x, y, h, c, l: ((x + 1) % 4, y, h, c, l))
    kv1 = move(jnp.where(y == 3, kv4, kv0), lambda x, y, h, c, l: (x, (y + 1) % 4, h, c, l))
    kv3 = move(jnp.where(y == 0, kv0, kv4), lambda x, y, h, c, l: (x, (y - 1) % 4, h, c, l))
    kv2 = move(jnp.where(y >= 2, kv4, kv0), lambda x, y, h, c, l: (x, (y + 2) % 4, h, c, l))

    r = jnp.arange(4, dtype=jnp.int32)[:, None]
    d = jnp.arange(5, dtype=jnp.int32)[None, :]
    inner = 2 * (zh ^ (r >> 1)) + (c ^ (r & 1))
    lag = 4 * d + inner - (2 * zh + c)
    age = (4 * column + inner - seed_block[0] - 1) % 64
    code = jnp.where((lag == 0) | ((lag > 0) & (lag <= 16) & (lag <= age)), lag, -1).astype(jnp.int32)

    select = lax.dynamic_index_in_dim(jnp.asarray(SELECTION, jnp.bfloat16), c, keepdims=False)
    table = lax.dynamic_index_in_dim(jnp.asarray(SPREAD, jnp.bfloat16), c, keepdims=False)

    mine, theirs = pl.pallas_call(
        attend_kernel,
        out_shape=(bf16(4, TOK, WIDE), bf16(4, TOK, WIDE)),
        in_specs=[SMEM] + [VMEM] * 8,
        out_specs=(VMEM, VMEM),
        scratch_shapes=[pltpu.VMEM((4 * TOK, FEAT + 128), jnp.bfloat16)],
        compiler_params=PARAMS,
        name="attend",
    )(code, qa, qb, kv0, kv1, kv2, kv3, kv4, select)
    got = move(theirs, lambda x, y, h, c, l: (x, y, h, 1 - c, l))
    both = pl.pallas_call(
        merge_cores_kernel,
        out_shape=bf16(2, 2, TOK, WIDE),
        in_specs=[SMEM] + [VMEM] * 3,
        out_specs=VMEM,
        compiler_params=PARAMS,
        name="merge_cores",
    )(zh.reshape(1), mine, got, table)
    both = lax.all_to_all(both, "zh", 0, 0, tiled=True)
    attended = pl.pallas_call(
        merge_last_kernel,
        out_shape=bf16(TOK, FEAT),
        in_specs=[VMEM] * 2,
        out_specs=VMEM,
        compiler_params=PARAMS,
        name="merge_last",
    )(both, table)
    attended = lax.all_gather(attended, "zl", axis=0, axis_index_groups=[[0, 1, 2, 3], [4, 5, 6, 7]])

    keep, send = pl.pallas_call(
        project_kernel,
        out_shape=(jax.ShapeDtypeStruct((2, TOK, FEAT), jnp.float32), bf16(2, TOK, FEAT)),
        in_specs=[SMEM] + [VMEM] * 2,
        out_specs=(VMEM, VMEM),
        compiler_params=PARAMS,
        name="project",
    )((zl // 4).reshape(1), attended, weight)
    got = move(send, lambda x, y, h, c, l: (x, y, h, 1 - c, l))
    summed = keep + got.astype(jnp.float32)
    far = move(summed[1].astype(jnp.bfloat16), lambda x, y, h, c, l: (x, y, h, c, l ^ 4))

    level_pick = (jnp.arange(LEVELS, dtype=jnp.int32) == levels[0]).astype(jnp.float32)
    gate_row = jnp.sum(level_pick[:, None] * level_gate, axis=0)
    projected = summed[0] + far.astype(jnp.float32)
    return (latents.astype(jnp.float32) + gate_row[None, :] * projected).astype(jnp.bfloat16)


def solution(mesh):
    fine = Mesh(mesh.devices.reshape(SIZES), AXES)
    win = ("x", "y", "zh", "c")
    in_specs = (
        P(win, "zl"),
        P(win, "zl"),
        P(win, "zl"),
        P(win, "zl"),
        P(win, "zl"),
        P(None, "zl"),
        P(win),
        P(win, None),
        P(),
    )
    return jax.shard_map(
        on_device, mesh=fine, in_specs=in_specs, out_specs=P(win, "zl"), check_vma=False
    )
```

time: 236 us -> 197 us (0.83)
  the two profiles are of different devices: /device:TPU:1 before, /device:TPU:15 now
where the time goes in v2:
time: 197 us; the launch traced here: 196 us
  waiting for transfers between devices  61.7 us (31%)
  starting transfers between devices  60.1 us (31%)
  blocking collectives  43.4 us (22%)
  between operations  15 us (8%)
  Pallas kernels  7.75 us (4%)
  other arithmetic  6.12 us (3%)
  local copies, waits for them, and re-layouts  2.09 us (1%)
    ppermute x11, waiting for transfers between devices, move(): return lax.ppermute(value, AXES, pairs)  61.7 us
    ppermute x11, starting transfers between devices, move(): return lax.ppermute(value, AXES, pairs)  60.1 us
    all_to_all x1, blocking collectives, on_device(): both = lax.all_to_all(both, 'zh', 0, 0, tiled=True)  22.8 us
    all_gather x1, blocking collectives, on_device(): lax.all_gather(attended, 'zl', axis=0, axis_index_groups=[[0, 1, 2, 3], [...  20.6 us
    pallas_call x1, Pallas kernels, on_device(): pl.pallas_call(attend_kernel, out_shape=(bf16(4, TOK, WIDE), bf16(4, TOK,...  4.54 us
  transfers between devices with their start and end apart: 12, of which 8 were waited for; matrix products, arithmetic and copies ran while one was open for 2% of the time, Pallas kernels for 3%

profile of v2, /device:TPU:15, one launch (start us, length us, event | category | flops | bytes accessed | tf_op | source)
XLA Modules:
  0.0 196.1 jit_solution(6799972303194536653)
XLA Ops:
  6.5 8.9 %collective-permute-start.7 = (bf16[80,640]{1,0:T(8,128)(2,1)}, bf16[80,640]{1,0:T(8,128)(2,1)S(1)}, u32[]{:S(2)}, u32[]{:S(2)}) collective-permute-start(bf16[80,640]{1,0:T(8,128)(2,1)} %param.15), channel_id=1, source_target_pairs={{0,16},{1,17},{2,18},{3,19},{4,384},{5,385},{6,386},{7,387},{8,24}... | collective-permute-start | bytes 307208 | tf_op jit(solution)/shard_map/ppermute | solution.py:28
  15.4 11.0 %collective-permute-start.8 = (bf16[80,640]{1,0:T(8,128)(2,1)}, bf16[80,640]{1,0:T(8,128)(2,1)S(1)}, u32[]{:S(2)}, u32[]{:S(2)}) collective-permute-start(bf16[80,640]{1,0:T(8,128)(2,1)} %param.15), channel_id=1, source_target_pairs={{4,400},{5,401},{6,402},{7,403},{12,408},{13,409},{14,410},{15,411... | collective-permute-start | bytes 307208 | tf_op jit(solution)/shard_map/ppermute | solution.py:28
  26.5 12.1 %collective-permute-done.8 = bf16[80,640]{1,0:T(8,128)(2,1)S(1)} collective-permute-done((bf16[80,640]{1,0:T(8,128)(2,1)}, bf16[80,640]{1,0:T(8,128)(2,1)S(1)}, u32[]{:S(2)}, u32[]{:S(2)}) %collective-permute-start.8) | collective-permute-done | bytes 102432 | tf_op jit(solution)/shard_map/ppermute | solution.py:28
  40.4 1.9 collective-permute-start.2
  43.0 1.6 fusion.16
  44.6 7.3 %collective-permute-start = (bf16[144,640]{1,0:T(8,128)(2,1)}, bf16[144,640]{1,0:T(8,128)(2,1)}, u32[]{:S(2)}, u32[]{:S(2)}) collective-permute-start(bf16[144,640]{1,0:T(8,128)(2,1)} %get-tuple-element.21), channel_id=1, source_target_pairs={{0,16},{1,17},{2,18},{3,19},{4,20},{5,21},{6,22},{7,23},{8,24},{9,... | collective-permute-start | bytes 552968 | tf_op jit(solution)/shard_map/ppermute | solution.py:28
  52.7 16.1 %collective-permute-done = bf16[144,640]{1,0:T(8,128)(2,1)} collective-permute-done((bf16[144,640]{1,0:T(8,128)(2,1)}, bf16[144,640]{1,0:T(8,128)(2,1)}, u32[]{:S(2)}, u32[]{:S(2)}) %collective-permute-start) | collective-permute-done | bytes 184352 | tf_op jit(solution)/shard_map/ppermute | solution.py:28
  69.8 3.5 %collective-permute-start.1 = (bf16[2,144,640]{2,1,0:T(8,128)(2,1)S(1)}, bf16[2,144,640]{2,1,0:T(8,128)(2,1)S(1)}, u32[]{:S(2)}, u32[]{:S(2)}) collective-permute-start(bf16[2,144,640]{2,1,0:T(8,128)(2,1)S(1)} %pad_maximum_fusion.qa_ref), channel_id=1, source_target_pairs={{0,8},{1,9},{2,10},{3,11},{4,12},{5,13},{6,14},{7,15},{8,0},{9,1},... | collective-permute-start | bytes 1105928 | tf_op jit(solution)/shard_map/ppermute | solution.py:28
  73.5 3.2 %collective-permute-start.3 = (bf16[2,128,640]{2,1,0:T(8,128)(2,1)S(1)}, bf16[2,128,640]{2,1,0:T(8,128)(2,1)S(1)}, u32[]{:S(2)}, u32[]{:S(2)}) collective-permute-start(bf16[2,128,640]{2,1,0:T(8,128)(2,1)S(1)} %get-tuple-element.17), channel_id=1, source_target_pairs={{0,32},{1,33},{2,34},{3,35},{4,36},{5,37},{6,38},{7,39},{8,40},{9,... | collective-permute-start | bytes 983048 | tf_op jit(solution)/shard_map/ppermute | solution.py:28
  76.7 2.6 %collective-permute-start.4 = (bf16[2,128,640]{2,1,0:T(8,128)(2,1)S(1)}, bf16[2,128,640]{2,1,0:T(8,128)(2,1)S(1)}, u32[]{:S(2)}, u32[]{:S(2)}) collective-permute-start(bf16[2,128,640]{2,1,0:T(8,128)(2,1)S(1)} %get-tuple-element.16), channel_id=1, source_target_pairs={{0,64},{1,65},{2,66},{3,67},{4,68},{5,69},{6,70},{7,71},{8,72},{9,... | collective-permute-start | bytes 983048 | tf_op jit(solution)/shard_map/ppermute | solution.py:28
  79.3 4.0 %collective-permute-start.5 = (bf16[2,128,640]{2,1,0:T(8,128)(2,1)S(1)}, bf16[2,128,640]{2,1,0:T(8,128)(2,1)S(1)}, u32[]{:S(2)}, u32[]{:S(2)}) collective-permute-start(bf16[2,128,640]{2,1,0:T(8,128)(2,1)S(1)} %get-tuple-element.15), channel_id=1, source_target_pairs={{0,96},{1,97},{2,98},{3,99},{4,100},{5,101},{6,102},{7,103},{8,104... | collective-permute-start | bytes 983048 | tf_op jit(solution)/shard_map/ppermute | solution.py:28
  83.4 1.3 collective-permute-done.3.kv1
  84.7 4.4 %collective-permute-done.4.kv2 = bf16[2,128,640]{2,1,0:T(8,128)(2,1)S(1)} collective-permute-done((bf16[2,128,640]{2,1,0:T(8,128)(2,1)S(1)}, bf16[2,128,640]{2,1,0:T(8,128)(2,1)S(1)}, u32[]{:S(2)}, u32[]{:S(2)}) %collective-permute-start.4) | collective-permute-done | bytes 327712 | tf_op jit(solution)/shard_map/ppermute | solution.py:28
  89.2 12.1 %collective-permute-done.5.kv3 = bf16[2,128,640]{2,1,0:T(8,128)(2,1)S(1)} collective-permute-done((bf16[2,128,640]{2,1,0:T(8,128)(2,1)S(1)}, bf16[2,128,640]{2,1,0:T(8,128)(2,1)S(1)}, u32[]{:S(2)}, u32[]{:S(2)}) %collective-permute-start.5) | collective-permute-done | bytes 327712 | tf_op jit(solution)/shard_map/ppermute | solution.py:28
  101.2 4.5 %attend.1 = (bf16[4,128,384]{2,1,0:T(8,128)(2,1)S(1)}, bf16[4,128,384]{2,1,0:T(8,128)(2,1)S(1)}) custom-call(s32[4,5]{1,0:T(4,128)S(1)} %fusion.7.code_ref, bf16[2,144,640]{2,1,0:T(8,128)(2,1)S(1)} %pad_maximum_fusion.qa_ref, bf16[2,144,640]{2,1,0:T(8,128)(2,1)S(1)} %collective-permute-done.1.qb_ref, bf16[2,128,640]{2,1,0:T(8,128)(2,1)S(1)} %pad_maximum_fusion.1.kv0, ...), custom_call_target="tpu_custom_call" | custom-call | tf_op jit(solution)/shard_map/attend/pallas_call | solution.py:224
  105.8 2.5 %collective-permute-start.6 = (bf16[4,128,384]{2,1,0:T(8,128)(2,1)S(1)}, bf16[4,128,384]{2,1,0:T(8,128)(2,1)S(1)}, u32[]{:S(2)}, u32[]{:S(2)}) collective-permute-start(bf16[4,128,384]{2,1,0:T(8,128)(2,1)S(1)} %get-tuple-element.10), channel_id=1, source_target_pairs={{0,8},{1,9},{2,10},{3,11},{4,12},{5,13},{6,14},{7,15},{8,0},{9,1},... | collective-permute-start | bytes 1179656 | tf_op jit(solution)/shard_map/ppermute | solution.py:28
  108.3 1.3 collective-permute-done.6.got_ref
  110.2 22.8 %all_to_all.5.both_ref = bf16[2,2,128,384]{3,2,1,0:T(8,128)(2,1)S(1)} all-to-all(bf16[2,2,128,384]{3,2,1,0:T(8,128)(2,1)S(1)} %merge_cores.1), channel_id=1, replica_groups=mesh['x'=4,'y'=4,'zh'=2,'c'=2,'zl'=8] {'zh'}, dimensions={0} | all-to-all | bytes 786432 | tf_op jit(solution)/shard_map/all_to_all | solution.py:242
  133.9 20.6 %all-gather = bf16[512,640]{1,0:T(8,128)(2,1)S(1)} all-gather(bf16[128,640]{1,0:T(8,128)(2,1)S(1)} %merge_last.1), channel_id=2, replica_groups={{0,1,2,3},{4,5,6,7},{8,9,10,11},{12,13,14,15},{16,17,18,19},{20,21,22,2..., dimensions={0}, use_global_device_ids=true | all-gather | bytes 819200 | tf_op jit(solution)/shard_map/all_gather | solution.py:251
  154.5 1.9 copy-done
  156.5 1.6 project.1
  158.1 5.3 %collective-permute-start.9 = (bf16[2,128,640]{2,1,0:T(8,128)(2,1)S(1)}, bf16[2,128,640]{2,1,0:T(8,128)(2,1)S(1)}, u32[]{:S(2)}, u32[]{:S(2)}) collective-permute-start(bf16[2,128,640]{2,1,0:T(8,128)(2,1)S(1)} %get-tuple-element.12), channel_id=1, source_target_pairs={{0,8},{1,9},{2,10},{3,11},{4,12},{5,13},{6,14},{7,15},{8,0},{9,1},... | collective-permute-start | bytes 983048 | tf_op jit(solution)/shard_map/ppermute | solution.py:28
  164.7 10.0 %collective-permute-start.10 = (bf16[128,640]{1,0:T(8,128)(2,1)S(1)}, bf16[128,640]{1,0:T(8,128)(2,1)S(1)}, u32[]{:S(2)}, u32[]{:S(2)}) collective-permute-start(bf16[128,640]{1,0:T(8,128)(2,1)S(1)} %fusion.6), channel_id=1, source_target_pairs={{0,4},{1,5},{2,6},{3,7},{4,0},{5,1},{6,2},{7,3},{8,12},{9,13},{10,... | collective-permute-start | bytes 491528 | tf_op jit(solution)/shard_map/ppermute | solution.py:28
  174.8 13.7 %collective-permute-done.10 = bf16[128,640]{1,0:T(8,128)(2,1)S(1)} collective-permute-done((bf16[128,640]{1,0:T(8,128)(2,1)S(1)}, bf16[128,640]{1,0:T(8,128)(2,1)S(1)}, u32[]{:S(2)}, u32[]{:S(2)}) %collective-permute-start.10) | collective-permute-done | bytes 163872 | tf_op jit(solution)/shard_map/ppermute | solution.py:28
  (38 shorter events, 6.9 us)
Async XLA Ops:
  6.5 46.1 %copy-start.3 = (bf16[2,768,768]{2,1,0:T(8,128)(2,1)S(1)}, bf16[2,768,768]{2,1,0:T(8,128)(2,1)}, u32[]{:S(2)}) copy-start(bf16[2,768,768]{2,1,0:T(8,128)(2,1)} %constant.89.clone) | copy-start | bytes 7077892
  6.5 148.0 %all-gather.4.cloned.1.call-start = ((), (), s32[]{:S(2)}) async-start(), calls=%async_computation.1 | async-start | bytes 3481600 | tf_op jit(solution)/shard_map/all_gather | solution.py:200
  6.5 19.9 %collective-permute-start.7 = (bf16[80,640]{1,0:T(8,128)(2,1)}, bf16[80,640]{1,0:T(8,128)(2,1)S(1)}, u32[]{:S(2)}, u32[]{:S(2)}) collective-permute-start(bf16[80,640]{1,0:T(8,128)(2,1)} %param.15), channel_id=1, source_target_pairs={{0,16},{1,17},{2,18},{3,19},{4,384},{5,385},{6,386},{7,387},{8,24}... | collective-permute-start | bytes 307208 | tf_op jit(solution)/shard_map/ppermute | solution.py:28
  15.4 23.2 %collective-permute-start.8 = (bf16[80,640]{1,0:T(8,128)(2,1)}, bf16[80,640]{1,0:T(8,128)(2,1)S(1)}, u32[]{:S(2)}, u32[]{:S(2)}) collective-permute-start(bf16[80,640]{1,0:T(8,128)(2,1)} %param.15), channel_id=1, source_target_pairs={{4,400},{5,401},{6,402},{7,403},{12,408},{13,409},{14,410},{15,411... | collective-permute-start | bytes 307208 | tf_op jit(solution)/shard_map/ppermute | solution.py:28
  39.3 34.0 %copy-start.1 = (bf16[128,640]{1,0:T(8,128)(2,1)S(1)}, bf16[128,640]{1,0:T(8,128)(2,1)}, u32[]{:S(2)}) copy-start(bf16[128,640]{1,0:T(8,128)(2,1)} %param.13) | copy-start | bytes 491524
  39.3 34.0 %copy-start.2 = (bf16[128,640]{1,0:T(8,128)(2,1)S(1)}, bf16[128,640]{1,0:T(8,128)(2,1)}, u32[]{:S(2)}) copy-start(bf16[128,640]{1,0:T(8,128)(2,1)} %param.12) | copy-start | bytes 491524
  40.4 32.9 %collective-permute-start.2 = (bf16[2,128,640]{2,1,0:T(8,128)(2,1)S(1)}, bf16[2,128,640]{2,1,0:T(8,128)(2,1)S(1)}, u32[]{:S(2)}, u32[]{:S(2)}) collective-permute-start(bf16[2,128,640]{2,1,0:T(8,128)(2,1)S(1)} %pad_maximum_fusion.1.kv0), channel_id=1, source_target_pairs={{0,128},{1,129},{2,130},{3,131},{4,132},{5,133},{6,134},{7,135},{8... | collective-permute-start | bytes 983048 | tf_op jit(solution)/shard_map/ppermute | solution.py:28
  44.6 24.2 %collective-permute-start = (bf16[144,640]{1,0:T(8,128)(2,1)}, bf16[144,640]{1,0:T(8,128)(2,1)}, u32[]{:S(2)}, u32[]{:S(2)}) collective-permute-start(bf16[144,640]{1,0:T(8,128)(2,1)} %get-tuple-element.21), channel_id=1, source_target_pairs={{0,16},{1,17},{2,18},{3,19},{4,20},{5,21},{6,22},{7,23},{8,24},{9,... | collective-permute-start | bytes 552968 | tf_op jit(solution)/shard_map/ppermute | solution.py:28
  69.8 38.4 %copy-start.5 = (bf16[2,2,128,384]{3,2,1,0:T(8,128)(2,1)S(1)}, bf16[2,2,128,384]{3,2,1,0:T(8,128)(2,1)}, u32[]{:S(2)}) copy-start(bf16[2,2,128,384]{3,2,1,0:T(8,128)(2,1)} %constant.90.clone) | copy-start | bytes 1179652
  69.8 13.6 %collective-permute-start.1 = (bf16[2,144,640]{2,1,0:T(8,128)(2,1)S(1)}, bf16[2,144,640]{2,1,0:T(8,128)(2,1)S(1)}, u32[]{:S(2)}, u32[]{:S(2)}) collective-permute-start(bf16[2,144,640]{2,1,0:T(8,128)(2,1)S(1)} %pad_maximum_fusion.qa_ref), channel_id=1, source_target_pairs={{0,8},{1,9},{2,10},{3,11},{4,12},{5,13},{6,14},{7,15},{8,0},{9,1},... | collective-permute-start | bytes 1105928 | tf_op jit(solution)/shard_map/ppermute | solution.py:28
  73.5 11.2 %collective-permute-start.3 = (bf16[2,128,640]{2,1,0:T(8,128)(2,1)S(1)}, bf16[2,128,640]{2,1,0:T(8,128)(2,1)S(1)}, u32[]{:S(2)}, u32[]{:S(2)}) collective-permute-start(bf16[2,128,640]{2,1,0:T(8,128)(2,1)S(1)} %get-tuple-element.17), channel_id=1, source_target_pairs={{0,32},{1,33},{2,34},{3,35},{4,36},{5,37},{6,38},{7,39},{8,40},{9,... | collective-permute-start | bytes 983048 | tf_op jit(solution)/shard_map/ppermute | solution.py:28
  76.7 12.5 %collective-permute-start.4 = (bf16[2,128,640]{2,1,0:T(8,128)(2,1)S(1)}, bf16[2,128,640]{2,1,0:T(8,128)(2,1)S(1)}, u32[]{:S(2)}, u32[]{:S(2)}) collective-permute-start(bf16[2,128,640]{2,1,0:T(8,128)(2,1)S(1)} %get-tuple-element.16), channel_id=1, source_target_pairs={{0,64},{1,65},{2,66},{3,67},{4,68},{5,69},{6,70},{7,71},{8,72},{9,... | collective-permute-start | bytes 983048 | tf_op jit(solution)/shard_map/ppermute | solution.py:28
  79.3 21.9 %collective-permute-start.5 = (bf16[2,128,640]{2,1,0:T(8,128)(2,1)S(1)}, bf16[2,128,640]{2,1,0:T(8,128)(2,1)S(1)}, u32[]{:S(2)}, u32[]{:S(2)}) collective-permute-start(bf16[2,128,640]{2,1,0:T(8,128)(2,1)S(1)} %get-tuple-element.15), channel_id=1, source_target_pairs={{0,96},{1,97},{2,98},{3,99},{4,100},{5,101},{6,102},{7,103},{8,104... | collective-permute-start | bytes 983048 | tf_op jit(solution)/shard_map/ppermute | solution.py:28
  105.8 3.8 %collective-permute-start.6 = (bf16[4,128,384]{2,1,0:T(8,128)(2,1)S(1)}, bf16[4,128,384]{2,1,0:T(8,128)(2,1)S(1)}, u32[]{:S(2)}, u32[]{:S(2)}) collective-permute-start(bf16[4,128,384]{2,1,0:T(8,128)(2,1)S(1)} %get-tuple-element.10), channel_id=1, source_target_pairs={{0,8},{1,9},{2,10},{3,11},{4,12},{5,13},{6,14},{7,15},{8,0},{9,1},... | collective-permute-start | bytes 1179656 | tf_op jit(solution)/shard_map/ppermute | solution.py:28
  154.5 1.9 copy-start
  156.5 18.3 %copy-start.6 = (f32[8,640]{1,0:T(8,128)S(1)}, f32[8,640]{1,0:T(8,128)}, u32[]{:S(2)}) copy-start(f32[8,640]{1,0:T(8,128)} %param.16) | copy-start | bytes 61444
  156.5 32.1 %copy-start.4 = (bf16[128,640]{1,0:T(8,128)(2,1)S(1)}, bf16[128,640]{1,0:T(8,128)(2,1)}, u32[]{:S(2)}) copy-start(bf16[128,640]{1,0:T(8,128)(2,1)} %param.14) | copy-start | bytes 491524
  158.1 6.5 %collective-permute-start.9 = (bf16[2,128,640]{2,1,0:T(8,128)(2,1)S(1)}, bf16[2,128,640]{2,1,0:T(8,128)(2,1)S(1)}, u32[]{:S(2)}, u32[]{:S(2)}) collective-permute-start(bf16[2,128,640]{2,1,0:T(8,128)(2,1)S(1)} %get-tuple-element.12), channel_id=1, source_target_pairs={{0,8},{1,9},{2,10},{3,11},{4,12},{5,13},{6,14},{7,15},{8,0},{9,1},... | collective-permute-start | bytes 983048 | tf_op jit(solution)/shard_map/ppermute | solution.py:28
  164.7 23.8 %collective-permute-start.10 = (bf16[128,640]{1,0:T(8,128)(2,1)S(1)}, bf16[128,640]{1,0:T(8,128)(2,1)S(1)}, u32[]{:S(2)}, u32[]{:S(2)}) collective-permute-start(bf16[128,640]{1,0:T(8,128)(2,1)S(1)} %fusion.6), channel_id=1, source_target_pairs={{0,4},{1,5},{2,6},{3,7},{4,0},{5,1},{6,2},{7,3},{8,12},{9,13},{10,... | collective-permute-start | bytes 491528 | tf_op jit(solution)/shard_map/ppermute | solution.py:28
Sparse Core Ops, SparseCore 0:
  39.5 70.9 all-gather.3

commit v3 on v2

--- a/solution.py
+++ b/solution.py
@@ -65,14 +65,23 @@
     return jnp.dot(a, b, preferred_element_type=jnp.float32)
 
 
-def attend_kernel(code_ref, qa_ref, qb_ref, kv0, kv1, kv2, kv3, kv4, select_ref, mine_ref, theirs_ref, all_ref):
-    kvs = (kv0, kv1, kv2, kv3, kv4)
+def pack_kernel(query_ref, mask_ref, out_ref):
+    for h in range(HEADS_HERE):
+        out_ref[h * HD : (h + 1) * HD, :] = query_ref[:, h * HD : (h + 1) * HD]
+    out_ref[FEAT : FEAT + 16, :] = jnp.zeros((16, HD), jnp.bfloat16)
+    flags = jnp.broadcast_to(mask_ref[...].astype(jnp.float32), (16, 16))
+    out_ref[FEAT : FEAT + 16, 0:16] = flags.astype(jnp.bfloat16)
+
+
+def attend_kernel(code_ref, qa_ref, qb_ref, *refs):
+    kv_refs = refs[0:5]
+    select_ref, mine_ref, theirs_ref, all_ref = refs[5:]
     lane = lax.broadcasted_iota(jnp.int32, (1, 128), 1)
     lanes = lax.broadcasted_iota(jnp.int32, (TOK, 128), 1)
     biases = []
     for r in range(4):
         q_ref = qa_ref if r % 2 == 0 else qb_ref
-        flags = q_ref[r // 2, TOK : TOK + 16, 0:128].astype(jnp.float32)[0:1]
+        flags = q_ref[r // 2, FEAT : FEAT + 16].astype(jnp.float32)[0:1]
         row = []
         for d in range(5):
             code = code_ref[r, d]
@@ -83,10 +92,10 @@
     stats = [jnp.zeros((TOK, 128), jnp.float32) for r in range(4)]
     for h in range(HEADS_HERE):
         cols = slice(h * HD, (h + 1) * HD)
-        keys = jnp.concatenate([kv[0, :, cols] for kv in kvs], axis=0)
-        values = jnp.concatenate([kv[1, :, cols] for kv in kvs], axis=0)
+        keys = jnp.concatenate([ref[0, :, cols] for ref in kv_refs], axis=0)
+        values = jnp.concatenate([ref[1, :, cols] for ref in kv_refs], axis=0)
         queries = jnp.concatenate(
-            [(qa_ref if r % 2 == 0 else qb_ref)[r // 2, 0:TOK, cols] for r in range(4)], axis=0
+            [(qa_ref if r % 2 == 0 else qb_ref)[r // 2, cols, :] for r in range(4)], axis=0
         )
         scores = lax.dot_general(queries, keys, (((1,), (1,)), ((), ())), preferred_element_type=jnp.float32)
         parts = []
@@ -122,7 +131,7 @@
     return joined, top
 
 
-def merge_cores_kernel(place_ref, mine_ref, got_ref, table_ref, out_ref):
+def merge_cores_kernel(mine_ref, got_ref, table_ref, keep_ref, send_ref):
     lanes = lax.broadcasted_iota(jnp.int32, (TOK, 128), 1)
     for r in range(4):
         joined, top = merge(mine_ref[r], got_ref[r ^ 1], table_ref[0])
@@ -130,16 +139,16 @@
         high = tail.astype(jnp.bfloat16).astype(jnp.float32)
         tail = jnp.where(lanes >= 80, tail + pltpu.roll(tail - high, 8, 1), high)
         tail = jnp.where((lanes >= 64) & (lanes < 72), top, tail)
-        to = place_ref[0] ^ (r // 2)
-        out_ref[to, r % 2, :, 0:256] = joined[:, :256].astype(jnp.bfloat16)
-        out_ref[to, r % 2, :, 256:384] = tail.astype(jnp.bfloat16)
-
-
-def merge_last_kernel(both_ref, table_ref, out_ref):
+        out_ref = keep_ref if r < 2 else send_ref
+        out_ref[r % 2, :, 0:256] = joined[:, :256].astype(jnp.bfloat16)
+        out_ref[r % 2, :, 256:384] = tail.astype(jnp.bfloat16)
+
+
+def merge_last_kernel(keep_ref, got_ref, table_ref, out_ref):
     lanes = lax.broadcasted_iota(jnp.int32, (TOK, 128), 1)
     ends = []
     for r in range(2):
-        joined, top = merge(both_ref[0, r], both_ref[1, r], table_ref[0])
+        joined, top = merge(keep_ref[r], got_ref[r], table_ref[0])
         tail = joined[:, 256:]
         total = tail + pltpu.roll(tail, 120, 1)
         used = (lanes >= 72) & (lanes < 72 + HEADS_HERE)
@@ -185,6 +194,27 @@
     zh, c, zl = lax.axis_index("zh"), lax.axis_index("c"), lax.axis_index("zl")
     column = 4 * x + y
 
+    def behind(own):
+        far = move(own, lambda x, y, h, c, l: ((x + 1) % 4, y, h, c, l))
+        one = move(jnp.where(y == 3, far, own), lambda x, y, h, c, l: (x, (y + 1) % 4, h, c, l))
+        three = move(jnp.where(y == 0, own, far), lambda x, y, h, c, l: (x, (y - 1) % 4, h, c, l))
+        two = move(jnp.where(y >= 2, far, own), lambda x, y, h, c, l: (x, (y + 2) % 4, h, c, l))
+        return (own, one, two, three, far)
+
+    kvs = behind(jnp.stack([key, value]))
+    keys = kvs
+
+    q_own = pl.pallas_call(
+        pack_kernel,
+        out_shape=bf16(FEAT + 16, HD),
+        in_specs=[VMEM] * 2,
+        out_specs=VMEM,
+        name="pack",
+    )(query, frame_mask)
+    q_far = move(q_own, lambda x, y, h, c, l: (x, y, 1 - h, c, l))
+    qa = jnp.stack([q_own, q_far])
+    qb = move(qa, lambda x, y, h, c, l: (x, y, h, 1 - c, l))
+
     valid = x // 2 == zl // 4
     w_one = move(
         out_weight,
@@ -197,19 +227,8 @@
     w_same = jnp.where(valid, out_weight, w_one)
     w_other = jnp.where(valid, w_one, w_two)
     w_pair = jnp.stack([jnp.where(zh == 0, w_same, w_other), jnp.where(zh == 0, w_other, w_same)])
+    w_pair, *unused = lax.optimization_barrier((w_pair, kvs[1], kvs[2], kvs[3], q_far))
     weight = lax.all_gather(w_pair, ("x", "y"), axis=0).reshape(4, 2, HALF, FEAT)
-
-    flags = jnp.pad(frame_mask.astype(jnp.bfloat16), ((0, 15), (0, FEAT - 16)))
-    q_own = jnp.concatenate([query, flags], axis=0)
-    q_far = move(q_own, lambda x, y, h, c, l: (x, y, 1 - h, c, l))
-    qa = jnp.stack([q_own, q_far])
-    qb = move(qa, lambda x, y, h, c, l: (x, y, h, 1 - c, l))
-
-    kv0 = jnp.stack([key, value])
-    kv4 = move(kv0, lambda x, y, h, c, l: ((x + 1) % 4, y, h, c, l))
-    kv1 = move(jnp.where(y == 3, kv4, kv0), lambda x, y, h, c, l: (x, (y + 1) % 4, h, c, l))
-    kv3 = move(jnp.where(y == 0, kv0, kv4), lambda x, y, h, c, l: (x, (y - 1) % 4, h, c, l))
-    kv2 = move(jnp.where(y >= 2, kv4, kv0), lambda x, y, h, c, l: (x, (y + 2) % 4, h, c, l))
 
     r = jnp.arange(4, dtype=jnp.int32)[:, None]
     d = jnp.arange(5, dtype=jnp.int32)[None, :]
@@ -229,25 +248,25 @@
         scratch_shapes=[pltpu.VMEM((4 * TOK, FEAT + 128), jnp.bfloat16)],
         compiler_params=PARAMS,
         name="attend",
-    )(code, qa, qb, kv0, kv1, kv2, kv3, kv4, select)
+    )(code, qa, qb, *kvs, select)
     got = move(theirs, lambda x, y, h, c, l: (x, y, h, 1 - c, l))
-    both = pl.pallas_call(
+    keep, send = pl.pallas_call(
         merge_cores_kernel,
-        out_shape=bf16(2, 2, TOK, WIDE),
-        in_specs=[SMEM] + [VMEM] * 3,
-        out_specs=VMEM,
+        out_shape=(bf16(2, TOK, WIDE), bf16(2, TOK, WIDE)),
+        in_specs=[VMEM] * 3,
+        out_specs=(VMEM, VMEM),
         compiler_params=PARAMS,
         name="merge_cores",
-    )(zh.reshape(1), mine, got, table)
-    both = lax.all_to_all(both, "zh", 0, 0, tiled=True)
+    )(mine, got, table)
+    got = move(send, lambda x, y, h, c, l: (x, y, 1 - h, c, l))
     attended = pl.pallas_call(
         merge_last_kernel,
         out_shape=bf16(TOK, FEAT),
-        in_specs=[VMEM] * 2,
+        in_specs=[VMEM] * 3,
         out_specs=VMEM,
         compiler_params=PARAMS,
         name="merge_last",
-    )(both, table)
+    )(keep, got, table)
     attended = lax.all_gather(attended, "zl", axis=0, axis_index_groups=[[0, 1, 2, 3], [4, 5, 6, 7]])
 
     keep, send = pl.pallas_call(

time: 197 us -> 166 us (0.84)
  the two profiles are of different devices: /device:TPU:15 before, /device:TPU:1 now
where the time goes in v3:
time: 166 us
  starting transfers between devices  61.8 us (37%)
  waiting for transfers between devices  49.7 us (30%)
  blocking collectives  22.7 us (14%)
  between operations  15 us (9%)
  Pallas kernels  9.38 us (6%)
  other arithmetic  3.96 us (2%)
  local copies, waits for them, and re-layouts  3.35 us (2%)
    ppermute x12, starting transfers between devices, move(): return lax.ppermute(value, AXES, pairs)  61.8 us
    ppermute x12, waiting for transfers between devices, move(): return lax.ppermute(value, AXES, pairs)  31 us
    all_gather x1, blocking collectives, on_device(): lax.all_gather(attended, 'zl', axis=0, axis_index_groups=[[0, 1, 2, 3], [...  22.7 us
    all_gather x1, waiting for transfers between devices, on_device(): lax.all_gather(w_pair, ('x', 'y'), axis=0).reshape(4, 2, HALF, FEAT)  18.6 us
    pallas_call x1, Pallas kernels, on_device(): pl.pallas_call(attend_kernel, out_shape=(bf16(4, TOK, WIDE), bf16(4, TOK,...  4.56 us
  transfers between devices with their start and end apart: 13, of which 9 were waited for; matrix products, arithmetic and copies ran while one was open for 2% of the time, Pallas kernels for 5%

profile of v3, /device:TPU:1, one launch (start us, length us, event | category | flops | bytes accessed | tf_op | source)
XLA Modules:
  0.0 165.8 jit_solution(673818484528835072)
XLA Ops:
  7.6 3.9 %collective-permute-start.2 = (bf16[2,128,640]{2,1,0:T(8,128)(2,1)S(1)}, bf16[2,128,640]{2,1,0:T(8,128)(2,1)S(1)}, u32[]{:S(2)}, u32[]{:S(2)}) collective-permute-start(bf16[2,128,640]{2,1,0:T(8,128)(2,1)S(1)} %pad_maximum_fusion.1.refs_0_), channel_id=1, source_target_pairs={{0,128},{1,129},{2,130},{3,131},{4,132},{5,133},{6,134},{7,135},{8... | collective-permute-start | bytes 983048 | tf_op jit(solution)/shard_map/ppermute | solution.py:28
  11.6 15.4 %collective-permute-start.8 = (bf16[80,640]{1,0:T(8,128)(2,1)}, bf16[80,640]{1,0:T(8,128)(2,1)S(1)}, u32[]{:S(2)}, u32[]{:S(2)}) collective-permute-start(bf16[80,640]{1,0:T(8,128)(2,1)} %param.15), channel_id=1, source_target_pairs={{0,16},{1,17},{2,18},{3,19},{4,384},{5,385},{6,386},{7,387},{8,24}... | collective-permute-start | bytes 307208 | tf_op jit(solution)/shard_map/ppermute | solution.py:28
  27.7 1.6 pack.1
  29.3 1.9 %collective-permute-start = (bf16[656,128]{1,0:T(8,128)(2,1)}, bf16[656,128]{1,0:T(8,128)(2,1)S(1)}, u32[]{:S(2)}, u32[]{:S(2)}) collective-permute-start(bf16[656,128]{1,0:T(8,128)(2,1)} %pack.1), channel_id=1, source_target_pairs={{0,16},{1,17},{2,18},{3,19},{4,20},{5,21},{6,22},{7,23},{8,24},{9,... | collective-permute-start | bytes 503816 | tf_op jit(solution)/shard_map/ppermute | solution.py:28
  32.4 3.2 %collective-permute-start.3 = (bf16[2,128,640]{2,1,0:T(8,128)(2,1)S(1)}, bf16[2,128,640]{2,1,0:T(8,128)(2,1)S(1)}, u32[]{:S(2)}, u32[]{:S(2)}) collective-permute-start(bf16[2,128,640]{2,1,0:T(8,128)(2,1)S(1)} %get-tuple-element.23), channel_id=1, source_target_pairs={{0,32},{1,33},{2,34},{3,35},{4,36},{5,37},{6,38},{7,39},{8,40},{9,... | collective-permute-start | bytes 983048 | tf_op jit(solution)/shard_map/ppermute | solution.py:28
  35.6 4.5 %collective-permute-start.4 = (bf16[2,128,640]{2,1,0:T(8,128)(2,1)S(1)}, bf16[2,128,640]{2,1,0:T(8,128)(2,1)S(1)}, u32[]{:S(2)}, u32[]{:S(2)}) collective-permute-start(bf16[2,128,640]{2,1,0:T(8,128)(2,1)S(1)} %get-tuple-element.22), channel_id=1, source_target_pairs={{0,64},{1,65},{2,66},{3,67},{4,68},{5,69},{6,70},{7,71},{8,72},{9,... | collective-permute-start | bytes 983048 | tf_op jit(solution)/shard_map/ppermute | solution.py:28
  40.2 3.0 %collective-permute-start.5 = (bf16[2,128,640]{2,1,0:T(8,128)(2,1)S(1)}, bf16[2,128,640]{2,1,0:T(8,128)(2,1)S(1)}, u32[]{:S(2)}, u32[]{:S(2)}) collective-permute-start(bf16[2,128,640]{2,1,0:T(8,128)(2,1)S(1)} %get-tuple-element.21), channel_id=1, source_target_pairs={{0,96},{1,97},{2,98},{3,99},{4,100},{5,101},{6,102},{7,103},{8,104... | collective-permute-start | bytes 983048 | tf_op jit(solution)/shard_map/ppermute | solution.py:28
  43.9 4.0 %collective-permute-done = bf16[656,128]{1,0:T(8,128)(2,1)S(1)} collective-permute-done((bf16[656,128]{1,0:T(8,128)(2,1)}, bf16[656,128]{1,0:T(8,128)(2,1)S(1)}, u32[]{:S(2)}, u32[]{:S(2)}) %collective-permute-start) | collective-permute-done | bytes 167968 | tf_op jit(solution)/shard_map/ppermute | solution.py:28
  47.9 3.8 %collective-permute-done.4.refs_2_ = bf16[2,128,640]{2,1,0:T(8,128)(2,1)S(1)} collective-permute-done((bf16[2,128,640]{2,1,0:T(8,128)(2,1)S(1)}, bf16[2,128,640]{2,1,0:T(8,128)(2,1)S(1)}, u32[]{:S(2)}, u32[]{:S(2)}) %collective-permute-start.4) | collective-permute-done | bytes 327712 | tf_op jit(solution)/shard_map/ppermute | solution.py:28
  53.5 1.4 dynamic-slice_bitcast_fusion.refs_5_
  54.9 4.5 %collective-permute-start.1 = (bf16[2,656,128]{2,1,0:T(8,128)(2,1)S(1)}, bf16[2,656,128]{2,1,0:T(8,128)(2,1)S(1)}, u32[]{:S(2)}, u32[]{:S(2)}) collective-permute-start(bf16[2,656,128]{2,1,0:T(8,128)(2,1)S(1)} %pad_maximum_fusion.qa_ref), channel_id=1, source_target_pairs={{0,8},{1,9},{2,10},{3,11},{4,12},{5,13},{6,14},{7,15},{8,0},{9,1},... | collective-permute-start | bytes 1007624 | tf_op jit(solution)/shard_map/ppermute | solution.py:28
  59.5 1.2 collective-permute-done.1.qb_ref
  60.7 4.6 %attend.1 = (bf16[4,128,384]{2,1,0:T(8,128)(2,1)S(1)}, bf16[4,128,384]{2,1,0:T(8,128)(2,1)S(1)}) custom-call(s32[4,5]{1,0:T(4,128)S(1)} %fusion.5.code_ref, bf16[2,656,128]{2,1,0:T(8,128)(2,1)S(1)} %pad_maximum_fusion.qa_ref, bf16[2,656,128]{2,1,0:T(8,128)(2,1)S(1)} %collective-permute-done.1.qb_ref, bf16[2,128,640]{2,1,0:T(8,128)(2,1)S(1)} %pad_maximum_fusion.1.refs_0_, ...), custom_call_target="tpu_custom_call" | custom-call | tf_op jit(solution)/shard_map/attend/pallas_call | solution.py:243
  65.2 2.3 %collective-permute-start.6 = (bf16[4,128,384]{2,1,0:T(8,128)(2,1)S(1)}, bf16[4,128,384]{2,1,0:T(8,128)(2,1)S(1)}, u32[]{:S(2)}, u32[]{:S(2)}) collective-permute-start(bf16[4,128,384]{2,1,0:T(8,128)(2,1)S(1)} %get-tuple-element.13), channel_id=1, source_target_pairs={{0,8},{1,9},{2,10},{3,11},{4,12},{5,13},{6,14},{7,15},{8,0},{9,1},... | collective-permute-start | bytes 1179656 | tf_op jit(solution)/shard_map/ppermute | solution.py:28
  67.6 1.3 collective-permute-done.6.got_ref
  69.5 12.1 %collective-permute-start.7 = (bf16[2,128,384]{2,1,0:T(8,128)(2,1)S(1)}, bf16[2,128,384]{2,1,0:T(8,128)(2,1)S(1)}, u32[]{:S(2)}, u32[]{:S(2)}) collective-permute-start(bf16[2,128,384]{2,1,0:T(8,128)(2,1)S(1)} %get-tuple-element.15), channel_id=1, source_target_pairs={{0,16},{1,17},{2,18},{3,19},{4,20},{5,21},{6,22},{7,23},{8,24},{9,... | collective-permute-start | bytes 589832 | tf_op jit(solution)/shard_map/ppermute | solution.py:28
  81.6 4.6 %collective-permute-done.7.got_ref = bf16[2,128,384]{2,1,0:T(8,128)(2,1)S(1)} collective-permute-done((bf16[2,128,384]{2,1,0:T(8,128)(2,1)S(1)}, bf16[2,128,384]{2,1,0:T(8,128)(2,1)S(1)}, u32[]{:S(2)}, u32[]{:S(2)}) %collective-permute-start.7) | collective-permute-done | bytes 196640 | tf_op jit(solution)/shard_map/ppermute | solution.py:28
  87.1 22.7 %all-gather = bf16[512,640]{1,0:T(8,128)(2,1)S(1)} all-gather(bf16[128,640]{1,0:T(8,128)(2,1)S(1)} %merge_last.1), channel_id=2, replica_groups={{0,1,2,3},{4,5,6,7},{8,9,10,11},{12,13,14,15},{16,17,18,19},{20,21,22,2..., dimensions={0}, use_global_device_ids=true | all-gather | bytes 819200 | tf_op jit(solution)/shard_map/all_gather | solution.py:270
  109.8 18.6 %all-gather.4.cloned.1.call-done = bf16[32,80,640]{2,1,0:T(8,128)(2,1)} async-done(((bf16[2,80,640]{2,1,0:T(8,128)(2,1)}), bf16[32,80,640]{2,1,0:T(8,128)(2,1)}) %all-gather.4.cloned.1.call-update) | async-done | bytes 3276816 | tf_op jit(solution)/shard_map/all_gather | solution.py:231
  128.4 1.9 %copy-done = bf16[32,80,640]{2,1,0:T(8,128)(2,1)S(1)} copy-done((bf16[32,80,640]{2,1,0:T(8,128)(2,1)S(1)}, bf16[32,80,640]{2,1,0:T(8,128)(2,1)}, u32[]{:S(2)}) %copy-start) | copy-done | bytes 3276824
  130.4 1.7 %project.1 = (f32[2,128,640]{2,1,0:T(8,128)S(1)}, bf16[2,128,640]{2,1,0:T(8,128)(2,1)S(1)}) custom-call(s32[1]{0:T(128)} %bitcast.1.place_ref, bf16[4,128,640]{2,1,0:T(8,128)(2,1)S(1)} %bitcast.32, bf16[4,2,320,640]{3,2,1,0:T(8,128)(2,1)S(1)} %bitcast.31), custom_call_target="tpu_custom_call" | custom-call | tf_op jit(solution)/shard_map/project/pallas_call | solution.py:272
  132.0 2.9 %collective-permute-start.10 = (bf16[2,128,640]{2,1,0:T(8,128)(2,1)S(1)}, bf16[2,128,640]{2,1,0:T(8,128)(2,1)S(1)}, u32[]{:S(2)}, u32[]{:S(2)}) collective-permute-start(bf16[2,128,640]{2,1,0:T(8,128)(2,1)S(1)} %get-tuple-element.18), channel_id=1, source_target_pairs={{0,8},{1,9},{2,10},{3,11},{4,12},{5,13},{6,14},{7,15},{8,0},{9,1},... | collective-permute-start | bytes 983048 | tf_op jit(solution)/shard_map/ppermute | solution.py:28
  136.3 7.4 %collective-permute-start.11 = (bf16[128,640]{1,0:T(8,128)(2,1)S(1)}, bf16[128,640]{1,0:T(8,128)(2,1)S(1)}, u32[]{:S(2)}, u32[]{:S(2)}) collective-permute-start(bf16[128,640]{1,0:T(8,128)(2,1)S(1)} %fusion.4), channel_id=1, source_target_pairs={{0,4},{1,5},{2,6},{3,7},{4,0},{5,1},{6,2},{7,3},{8,12},{9,13},{10,... | collective-permute-start | bytes 491528 | tf_op jit(solution)/shard_map/ppermute | solution.py:28
  143.7 14.5 %collective-permute-done.11 = bf16[128,640]{1,0:T(8,128)(2,1)S(1)} collective-permute-done((bf16[128,640]{1,0:T(8,128)(2,1)S(1)}, bf16[128,640]{1,0:T(8,128)(2,1)S(1)}, u32[]{:S(2)}, u32[]{:S(2)}) %collective-permute-start.11) | collective-permute-done | bytes 163872 | tf_op jit(solution)/shard_map/ppermute | solution.py:28
  (36 shorter events, 7.9 us)
Async XLA Ops:
  6.5 36.6 %copy-start.3 = (bf16[80,640]{1,0:T(8,128)(2,1)S(1)}, bf16[80,640]{1,0:T(8,128)(2,1)}, u32[]{:S(2)}) copy-start(bf16[80,640]{1,0:T(8,128)(2,1)} %param.15) | copy-start | bytes 307204
  6.5 121.9 %all-gather.4.cloned.1.call-start = ((), (), s32[]{:S(2)}) async-start(), calls=%async_computation | async-start | bytes 3481600 | tf_op jit(solution)/shard_map/all_gather | solution.py:231
  7.6 23.7 %collective-permute-start.2 = (bf16[2,128,640]{2,1,0:T(8,128)(2,1)S(1)}, bf16[2,128,640]{2,1,0:T(8,128)(2,1)S(1)}, u32[]{:S(2)}, u32[]{:S(2)}) collective-permute-start(bf16[2,128,640]{2,1,0:T(8,128)(2,1)S(1)} %pad_maximum_fusion.1.refs_0_), channel_id=1, source_target_pairs={{0,128},{1,129},{2,130},{3,131},{4,132},{5,133},{6,134},{7,135},{8... | collective-permute-start | bytes 983048 | tf_op jit(solution)/shard_map/ppermute | solution.py:28
  11.6 28.6 %collective-permute-start.8 = (bf16[80,640]{1,0:T(8,128)(2,1)}, bf16[80,640]{1,0:T(8,128)(2,1)S(1)}, u32[]{:S(2)}, u32[]{:S(2)}) collective-permute-start(bf16[80,640]{1,0:T(8,128)(2,1)} %param.15), channel_id=1, source_target_pairs={{0,16},{1,17},{2,18},{3,19},{4,384},{5,385},{6,386},{7,387},{8,24}... | collective-permute-start | bytes 307208 | tf_op jit(solution)/shard_map/ppermute | solution.py:28
  27.0 16.2 %collective-permute-start.9 = (bf16[80,640]{1,0:T(8,128)(2,1)}, bf16[80,640]{1,0:T(8,128)(2,1)S(1)}, u32[]{:S(2)}, u32[]{:S(2)}) collective-permute-start(bf16[80,640]{1,0:T(8,128)(2,1)} %param.15), channel_id=1, source_target_pairs={{4,400},{5,401},{6,402},{7,403},{12,408},{13,409},{14,410},{15,411... | collective-permute-start | bytes 307208 | tf_op jit(solution)/shard_map/ppermute | solution.py:28
  29.3 18.6 %collective-permute-start = (bf16[656,128]{1,0:T(8,128)(2,1)}, bf16[656,128]{1,0:T(8,128)(2,1)S(1)}, u32[]{:S(2)}, u32[]{:S(2)}) collective-permute-start(bf16[656,128]{1,0:T(8,128)(2,1)} %pack.1), channel_id=1, source_target_pairs={{0,16},{1,17},{2,18},{3,19},{4,20},{5,21},{6,22},{7,23},{8,24},{9,... | collective-permute-start | bytes 503816 | tf_op jit(solution)/shard_map/ppermute | solution.py:28
  31.3 23.6 %copy-start.1 = (bf16[656,128]{1,0:T(8,128)(2,1)S(1)}, bf16[656,128]{1,0:T(8,128)(2,1)}, u32[]{:S(2)}) copy-start(bf16[656,128]{1,0:T(8,128)(2,1)} %pack.1) | copy-start | bytes 503812
  32.4 15.5 %collective-permute-start.3 = (bf16[2,128,640]{2,1,0:T(8,128)(2,1)S(1)}, bf16[2,128,640]{2,1,0:T(8,128)(2,1)S(1)}, u32[]{:S(2)}, u32[]{:S(2)}) collective-permute-start(bf16[2,128,640]{2,1,0:T(8,128)(2,1)S(1)} %get-tuple-element.23), channel_id=1, source_target_pairs={{0,32},{1,33},{2,34},{3,35},{4,36},{5,37},{6,38},{7,39},{8,40},{9,... | collective-permute-start | bytes 983048 | tf_op jit(solution)/shard_map/ppermute | solution.py:28
  35.6 16.1 %collective-permute-start.4 = (bf16[2,128,640]{2,1,0:T(8,128)(2,1)S(1)}, bf16[2,128,640]{2,1,0:T(8,128)(2,1)S(1)}, u32[]{:S(2)}, u32[]{:S(2)}) collective-permute-start(bf16[2,128,640]{2,1,0:T(8,128)(2,1)S(1)} %get-tuple-element.22), channel_id=1, source_target_pairs={{0,64},{1,65},{2,66},{3,67},{4,68},{5,69},{6,70},{7,71},{8,72},{9,... | collective-permute-start | bytes 983048 | tf_op jit(solution)/shard_map/ppermute | solution.py:28
  40.2 12.6 %collective-permute-start.5 = (bf16[2,128,640]{2,1,0:T(8,128)(2,1)S(1)}, bf16[2,128,640]{2,1,0:T(8,128)(2,1)S(1)}, u32[]{:S(2)}, u32[]{:S(2)}) collective-permute-start(bf16[2,128,640]{2,1,0:T(8,128)(2,1)S(1)} %get-tuple-element.21), channel_id=1, source_target_pairs={{0,96},{1,97},{2,98},{3,99},{4,100},{5,101},{6,102},{7,103},{8,104... | collective-permute-start | bytes 983048 | tf_op jit(solution)/shard_map/ppermute | solution.py:28
  54.9 12.6 %copy-start.4 = (bf16[2,2,128,384]{3,2,1,0:T(8,128)(2,1)S(1)}, bf16[2,2,128,384]{3,2,1,0:T(8,128)(2,1)}, u32[]{:S(2)}) copy-start(bf16[2,2,128,384]{3,2,1,0:T(8,128)(2,1)} %constant.88.clone) | copy-start | bytes 1179652
  54.9 5.7 %collective-permute-start.1 = (bf16[2,656,128]{2,1,0:T(8,128)(2,1)S(1)}, bf16[2,656,128]{2,1,0:T(8,128)(2,1)S(1)}, u32[]{:S(2)}, u32[]{:S(2)}) collective-permute-start(bf16[2,656,128]{2,1,0:T(8,128)(2,1)S(1)} %pad_maximum_fusion.qa_ref), channel_id=1, source_target_pairs={{0,8},{1,9},{2,10},{3,11},{4,12},{5,13},{6,14},{7,15},{8,0},{9,1},... | collective-permute-start | bytes 1007624 | tf_op jit(solution)/shard_map/ppermute | solution.py:28
  65.2 3.6 %collective-permute-start.6 = (bf16[4,128,384]{2,1,0:T(8,128)(2,1)S(1)}, bf16[4,128,384]{2,1,0:T(8,128)(2,1)S(1)}, u32[]{:S(2)}, u32[]{:S(2)}) collective-permute-start(bf16[4,128,384]{2,1,0:T(8,128)(2,1)S(1)} %get-tuple-element.13), channel_id=1, source_target_pairs={{0,8},{1,9},{2,10},{3,11},{4,12},{5,13},{6,14},{7,15},{8,0},{9,1},... | collective-permute-start | bytes 1179656 | tf_op jit(solution)/shard_map/ppermute | solution.py:28
  69.5 16.7 %collective-permute-start.7 = (bf16[2,128,384]{2,1,0:T(8,128)(2,1)S(1)}, bf16[2,128,384]{2,1,0:T(8,128)(2,1)S(1)}, u32[]{:S(2)}, u32[]{:S(2)}) collective-permute-start(bf16[2,128,384]{2,1,0:T(8,128)(2,1)S(1)} %get-tuple-element.15), channel_id=1, source_target_pairs={{0,16},{1,17},{2,18},{3,19},{4,20},{5,21},{6,22},{7,23},{8,24},{9,... | collective-permute-start | bytes 589832 | tf_op jit(solution)/shard_map/ppermute | solution.py:28
  128.4 1.9 %copy-start = (bf16[32,80,640]{2,1,0:T(8,128)(2,1)S(1)}, bf16[32,80,640]{2,1,0:T(8,128)(2,1)}, u32[]{:S(2)}) copy-start(bf16[32,80,640]{2,1,0:T(8,128)(2,1)} %all-gather.4.cloned.1.call-done) | copy-start | bytes 9830404
  130.4 13.3 %copy-start.5 = (f32[8,640]{1,0:T(8,128)S(1)}, f32[8,640]{1,0:T(8,128)}, u32[]{:S(2)}) copy-start(f32[8,640]{1,0:T(8,128)} %param.16) | copy-start | bytes 61444
  130.4 27.8 %copy-start.2 = (bf16[128,640]{1,0:T(8,128)(2,1)S(1)}, bf16[128,640]{1,0:T(8,128)(2,1)}, u32[]{:S(2)}) copy-start(bf16[128,640]{1,0:T(8,128)(2,1)} %param.14) | copy-start | bytes 491524
  132.0 4.1 %collective-permute-start.10 = (bf16[2,128,640]{2,1,0:T(8,128)(2,1)S(1)}, bf16[2,128,640]{2,1,0:T(8,128)(2,1)S(1)}, u32[]{:S(2)}, u32[]{:S(2)}) collective-permute-start(bf16[2,128,640]{2,1,0:T(8,128)(2,1)S(1)} %get-tuple-element.18), channel_id=1, source_target_pairs={{0,8},{1,9},{2,10},{3,11},{4,12},{5,13},{6,14},{7,15},{8,0},{9,1},... | collective-permute-start | bytes 983048 | tf_op jit(solution)/shard_map/ppermute | solution.py:28
  136.3 21.9 %collective-permute-start.11 = (bf16[128,640]{1,0:T(8,128)(2,1)S(1)}, bf16[128,640]{1,0:T(8,128)(2,1)S(1)}, u32[]{:S(2)}, u32[]{:S(2)}) collective-permute-start(bf16[128,640]{1,0:T(8,128)(2,1)S(1)} %fusion.4), channel_id=1, source_target_pairs={{0,4},{1,5},{2,6},{3,7},{4,0},{5,1},{6,2},{7,3},{8,12},{9,13},{10,... | collective-permute-start | bytes 491528 | tf_op jit(solution)/shard_map/ppermute | solution.py:28
Sparse Core Ops, SparseCore 0:
  53.0 75.4 all-gather.3

commit v4 on v3

--- a/solution.py
+++ b/solution.py
@@ -66,22 +66,21 @@
 
 
 def pack_kernel(query_ref, mask_ref, out_ref):
-    for h in range(HEADS_HERE):
-        out_ref[h * HD : (h + 1) * HD, :] = query_ref[:, h * HD : (h + 1) * HD]
-    out_ref[FEAT : FEAT + 16, :] = jnp.zeros((16, HD), jnp.bfloat16)
+    out_ref[0:TOK, :] = query_ref[...]
+    out_ref[TOK : TOK + 16, :] = jnp.zeros((16, FEAT), jnp.bfloat16)
     flags = jnp.broadcast_to(mask_ref[...].astype(jnp.float32), (16, 16))
-    out_ref[FEAT : FEAT + 16, 0:16] = flags.astype(jnp.bfloat16)
-
-
-def attend_kernel(code_ref, qa_ref, qb_ref, *refs):
-    kv_refs = refs[0:5]
-    select_ref, mine_ref, theirs_ref, all_ref = refs[5:]
+    out_ref[TOK : TOK + 16, 0:16] = flags.astype(jnp.bfloat16)
+
+
+def attend_kernel(code_ref, qa_ref, qb_ref, own_ref, row_ref, far_ref, select_ref, mine_ref, theirs_ref, all_ref):
+    row = code_ref[4, 0]
+    kv_refs = [own_ref] + [row_ref.at[(row + 4 - d) % 4] for d in (1, 2, 3)] + [far_ref]
     lane = lax.broadcasted_iota(jnp.int32, (1, 128), 1)
     lanes = lax.broadcasted_iota(jnp.int32, (TOK, 128), 1)
     biases = []
     for r in range(4):
         q_ref = qa_ref if r % 2 == 0 else qb_ref
-        flags = q_ref[r // 2, FEAT : FEAT + 16].astype(jnp.float32)[0:1]
+        flags = q_ref[r // 2, TOK : TOK + 16, 0:HD].astype(jnp.float32)[0:1]
         row = []
         for d in range(5):
             code = code_ref[r, d]
@@ -95,7 +94,7 @@
         keys = jnp.concatenate([ref[0, :, cols] for ref in kv_refs], axis=0)
         values = jnp.concatenate([ref[1, :, cols] for ref in kv_refs], axis=0)
         queries = jnp.concatenate(
-            [(qa_ref if r % 2 == 0 else qb_ref)[r // 2, cols, :] for r in range(4)], axis=0
+            [(qa_ref if r % 2 == 0 else qb_ref)[r // 2, 0:TOK, cols] for r in range(4)], axis=0
         )
         scores = lax.dot_general(queries, keys, (((1,), (1,)), ((), ())), preferred_element_type=jnp.float32)
         parts = []
@@ -183,6 +182,7 @@
 VMEM = pl.BlockSpec(memory_space=pltpu.VMEM)
 SMEM = pl.BlockSpec(memory_space=pltpu.SMEM)
 PARAMS = pltpu.CompilerParams(vmem_limit_bytes=40 * 1024 * 1024)
+ROOMY = pltpu.CompilerParams(vmem_limit_bytes=60 * 1024 * 1024)
 
 
 def bf16(*shape):
@@ -194,41 +194,35 @@
     zh, c, zl = lax.axis_index("zh"), lax.axis_index("c"), lax.axis_index("zl")
     column = 4 * x + y
 
-    def behind(own):
-        far = move(own, lambda x, y, h, c, l: ((x + 1) % 4, y, h, c, l))
-        one = move(jnp.where(y == 3, far, own), lambda x, y, h, c, l: (x, (y + 1) % 4, h, c, l))
-        three = move(jnp.where(y == 0, own, far), lambda x, y, h, c, l: (x, (y - 1) % 4, h, c, l))
-        two = move(jnp.where(y >= 2, far, own), lambda x, y, h, c, l: (x, (y + 2) % 4, h, c, l))
-        return (own, one, two, three, far)
-
-    kvs = behind(jnp.stack([key, value]))
-    keys = kvs
-
-    q_own = pl.pallas_call(
+    kv_own = jnp.stack([key, value])
+    kv_far = move(kv_own, lambda x, y, h, c, l: ((x + 1) % 4, y, h, c, l))
+    to = jnp.arange(4, dtype=jnp.int32)[:, None, None, None]
+    kv_row = lax.all_to_all(jnp.where(to > y, kv_own[None], kv_far[None]), "y", 0, 0, tiled=True)
+
+    w_turned = move(out_weight, lambda x, y, h, c, l: (x, y, h, 1 - c, l))
+    w_one = move(
+        w_turned,
+        lambda x, y, h, c, l: (x, y, 1 - h, 1 - c, l) if x // 2 == l // 4 else (3 - x, y, h, 1 - c, l ^ 4),
+    )
+    w_two = move(
+        w_turned,
+        lambda x, y, h, c, l: None if x // 2 == l // 4 else (3 - x, y, 1 - h, 1 - c, l ^ 4),
+    )
+    valid = x // 2 == zl // 4
+    w_same = jnp.where(valid, out_weight, w_one)
+    w_other = jnp.where(valid, w_one, w_two)
+    w_pair = jnp.stack([jnp.where(zh == 0, w_same, w_other), jnp.where(zh == 0, w_other, w_same)])
+
+    packed = pl.pallas_call(
         pack_kernel,
-        out_shape=bf16(FEAT + 16, HD),
+        out_shape=bf16(TOK + 16, FEAT),
         in_specs=[VMEM] * 2,
         out_specs=VMEM,
         name="pack",
     )(query, frame_mask)
-    q_far = move(q_own, lambda x, y, h, c, l: (x, y, 1 - h, c, l))
-    qa = jnp.stack([q_own, q_far])
+    mate = move(packed, lambda x, y, h, c, l: (x, y, 1 - h, c, l))
+    qa = jnp.stack([packed, mate])
     qb = move(qa, lambda x, y, h, c, l: (x, y, h, 1 - c, l))
-
-    valid = x // 2 == zl // 4
-    w_one = move(
-        out_weight,
-        lambda x, y, h, c, l: (x, y, 1 - h, c, l) if x // 2 == l // 4 else (3 - x, y, h, c, l ^ 4),
-    )
-    w_two = move(
-        out_weight,
-        lambda x, y, h, c, l: None if x // 2 == l // 4 else (3 - x, y, 1 - h, c, l ^ 4),
-    )
-    w_same = jnp.where(valid, out_weight, w_one)
-    w_other = jnp.where(valid, w_one, w_two)
-    w_pair = jnp.stack([jnp.where(zh == 0, w_same, w_other), jnp.where(zh == 0, w_other, w_same)])
-    w_pair, *unused = lax.optimization_barrier((w_pair, kvs[1], kvs[2], kvs[3], q_far))
-    weight = lax.all_gather(w_pair, ("x", "y"), axis=0).reshape(4, 2, HALF, FEAT)
 
     r = jnp.arange(4, dtype=jnp.int32)[:, None]
     d = jnp.arange(5, dtype=jnp.int32)[None, :]
@@ -236,19 +230,23 @@
     lag = 4 * d + inner - (2 * zh + c)
     age = (4 * column + inner - seed_block[0] - 1) % 64
     code = jnp.where((lag == 0) | ((lag > 0) & (lag <= 16) & (lag <= age)), lag, -1).astype(jnp.int32)
+    code = jnp.concatenate([code, jnp.broadcast_to(y, (1, 5)).astype(jnp.int32)], axis=0)
 
     select = lax.dynamic_index_in_dim(jnp.asarray(SELECTION, jnp.bfloat16), c, keepdims=False)
     table = lax.dynamic_index_in_dim(jnp.asarray(SPREAD, jnp.bfloat16), c, keepdims=False)
 
+    weight = lax.all_to_all(jnp.broadcast_to(w_pair[None], (16, 2, 80, FEAT)), ("x", "y"), 0, 0, tiled=True)
+    weight = weight.reshape(4, 2, HALF, FEAT)
     mine, theirs = pl.pallas_call(
         attend_kernel,
         out_shape=(bf16(4, TOK, WIDE), bf16(4, TOK, WIDE)),
-        in_specs=[SMEM] + [VMEM] * 8,
+        in_specs=[SMEM] + [VMEM] * 6,
         out_specs=(VMEM, VMEM),
         scratch_shapes=[pltpu.VMEM((4 * TOK, FEAT + 128), jnp.bfloat16)],
-        compiler_params=PARAMS,
+        compiler_params=ROOMY,
+        cost_estimate=pl.CostEstimate(flops=60000000000, bytes_accessed=4000000, transcendentals=0),
         name="attend",
-    )(code, qa, qb, *kvs, select)
+    )(code, qa, qb, kv_own, kv_row, kv_far, select)
     got = move(theirs, lambda x, y, h, c, l: (x, y, h, 1 - c, l))
     keep, send = pl.pallas_call(
         merge_cores_kernel,

time: 166 us -> 156 us (0.940)
  between operations: 15 us -> 1.58 us
  waiting for transfers between devices: 49.7 us -> 38.8 us
  starting transfers between devices: 61.8 us -> 68.3 us
  local copies, waits for them, and re-layouts: 3.35 us -> 7.24 us
  Pallas kernels: 9.38 us -> 11.7 us
    all_gather x1 -> x0, waiting for transfers between devices: 18.6 us -> none  [on_device(): lax.all_gather(w_pair, ('x', 'y'), axis=0).reshape(4, 2, HALF, FEAT)]
    all_to_all x0 -> x2, starting transfers between devices: none -> 17.1 us  [the longest x1 12.7 us: on_device(): lax.all_to_all(jnp.broadcast_to(w_pair[None], (16, 2, 80, FEAT)), ('x', '...]
    ppermute x12 -> x10, starting transfers between devices: 61.8 us -> 51.2 us  [move(): return lax.ppermute(value, AXES, pairs)]
    ppermute x12 -> x10, waiting for transfers between devices: 31 us -> 37.9 us  [move(): return lax.ppermute(value, AXES, pairs)]
    pallas_call x1, Pallas kernels: 4.56 us -> 6.91 us  [on_device(): pl.pallas_call(attend_kernel, out_shape=(bf16(4, TOK, WIDE), bf16(4, TOK,...]
    broadcast_in_dim x0 -> x1, local copies, waits for them, and re-layouts: none -> 2.08 us  [on_device(): jnp.broadcast_to(w_pair[None], (16, 2, 80, FEAT))]
  transfers between devices with their start and end apart: 13 -> 12, of which waited for: 9 -> 6; matrix products, arithmetic and copies ran while one was open for 2% -> 5% of each run, Pallas kernels for 5% -> 6%
where the time goes in v4:
time: 156 us; the launch traced here: 155 us
  starting transfers between devices  68.3 us (44%)
  waiting for transfers between devices  38.8 us (25%)
  blocking collectives  23.5 us (15%)
  Pallas kernels  11.7 us (8%)
  local copies, waits for them, and re-layouts  7.24 us (5%)
  other arithmetic  4.16 us (3%)
  between operations  1.58 us (1%)
    ppermute x10, starting transfers between devices, move(): return lax.ppermute(value, AXES, pairs)  51.2 us
    ppermute x10, waiting for transfers between devices, move(): return lax.ppermute(value, AXES, pairs)  37.9 us
    all_gather x1, blocking collectives, on_device(): lax.all_gather(attended, 'zl', axis=0, axis_index_groups=[[0, 1, 2, 3], [...  23.5 us
    all_to_all x1, starting transfers between devices, on_device(): lax.all_to_all(jnp.broadcast_to(w_pair[None], (16, 2, 80, FEAT)), ('x', '...  12.7 us
    pallas_call x1, Pallas kernels, on_device(): pl.pallas_call(attend_kernel, out_shape=(bf16(4, TOK, WIDE), bf16(4, TOK,...  6.91 us
    all_to_all x1, starting transfers between devices, on_device(): lax.all_to_all(jnp.where(to > y, kv_own[None], kv_far[None]), 'y', 0, 0,...  4.32 us
  transfers between devices with their start and end apart: 12, of which 6 were waited for; matrix products, arithmetic and copies ran while one was open for 5% of the time, Pallas kernels for 6%

profile of v4, /device:TPU:1, one launch (start us, length us, event | category | flops | bytes accessed | tf_op | source)
XLA Modules:
  0.0 155.2 jit_solution(12490724784659332085)
XLA Ops:
  0.0 1.0 pad_maximum_fusion.1.own_ref
  1.0 3.9 %collective-permute-start.2 = (bf16[2,128,640]{2,1,0:T(8,128)(2,1)S(1)}, bf16[2,128,640]{2,1,0:T(8,128)(2,1)S(1)}, u32[]{:S(2)}, u32[]{:S(2)}) collective-permute-start(bf16[2,128,640]{2,1,0:T(8,128)(2,1)S(1)} %pad_maximum_fusion.1.own_ref), channel_id=1, source_target_pairs={{0,128},{1,129},{2,130},{3,131},{4,132},{5,133},{6,134},{7,135},{8... | collective-permute-start | bytes 983048 | tf_op jit(solution)/shard_map/ppermute | solution.py:28
  5.0 1.6 %pack.1 = bf16[144,640]{1,0:T(8,128)(2,1)} custom-call(bf16[128,640]{1,0:T(8,128)(2,1)} %query_ref.1, s32[1,16]{1,0:T(1,128)} %mask_ref.1), custom_call_target="tpu_custom_call" | custom-call | tf_op jit(solution)/shard_map/pack/pallas_call | solution.py:216
  6.6 15.4 %collective-permute-start = (bf16[144,640]{1,0:T(8,128)(2,1)}, bf16[144,640]{1,0:T(8,128)(2,1)S(1)}, u32[]{:S(2)}, u32[]{:S(2)}) collective-permute-start(bf16[144,640]{1,0:T(8,128)(2,1)} %pack.1), channel_id=1, source_target_pairs={{0,16},{1,17},{2,18},{3,19},{4,20},{5,21},{6,22},{7,23},{8,24},{9,... | collective-permute-start | bytes 552968 | tf_op jit(solution)/shard_map/ppermute | solution.py:28
  22.0 3.1 %collective-permute-start.5 = (bf16[80,640]{1,0:T(8,128)(2,1)}, bf16[80,640]{1,0:T(8,128)(2,1)S(1)}, u32[]{:S(2)}, u32[]{:S(2)}) collective-permute-start(bf16[80,640]{1,0:T(8,128)(2,1)} %param.15), channel_id=1, source_target_pairs={{0,8},{1,9},{2,10},{3,11},{4,12},{5,13},{6,14},{7,15},{8,0},{9,1},... | collective-permute-start | bytes 307208 | tf_op jit(solution)/shard_map/ppermute | solution.py:28
  25.2 1.3 broadcast_select_fusion
  26.6 4.3 %all-to-all-start = ((bf16[4,2,128,640]{3,2,1,0:T(8,128)(2,1)}), bf16[4,2,128,640]{3,2,1,0:T(8,128)(2,1)S(1)}, u32[]{:S(2)}, u32[]{:S(2)}) async-start(bf16[4,2,128,640]{3,2,1,0:T(8,128)(2,1)} %broadcast_select_fusion), calls=%async_computation | async-start | bytes 2621440 | tf_op jit(solution)/shard_map/all_to_all | solution.py:200
  31.6 5.5 %collective-permute-start.6 = (bf16[80,640]{1,0:T(8,128)(2,1)S(1)}, bf16[80,640]{1,0:T(8,128)(2,1)S(1)}, u32[]{:S(2)}, u32[]{:S(2)}) collective-permute-start(bf16[80,640]{1,0:T(8,128)(2,1)S(1)} %collective-permute-done.5), channel_id=1, source_target_pairs={{0,24},{1,25},{2,26},{3,27},{4,392},{5,393},{6,394},{7,395},{8,16}... | collective-permute-start | bytes 307208 | tf_op jit(solution)/shard_map/ppermute | solution.py:28
  38.6 2.0 %collective-permute-start.1 = (bf16[2,144,640]{2,1,0:T(8,128)(2,1)}, bf16[2,144,640]{2,1,0:T(8,128)(2,1)}, u32[]{:S(2)}, u32[]{:S(2)}) collective-permute-start(bf16[2,144,640]{2,1,0:T(8,128)(2,1)} %pad_maximum_fusion.qa_ref), channel_id=1, source_target_pairs={{0,8},{1,9},{2,10},{3,11},{4,12},{5,13},{6,14},{7,15},{8,0},{9,1},... | collective-permute-start | bytes 1105928 | tf_op jit(solution)/shard_map/ppermute | solution.py:28
  40.6 2.4 %dynamic-slice_bitcast_fusion.select_ref = bf16[768,768]{1,0:T(8,128)(2,1)} fusion(bf16[2,768,768]{2,1,0:T(8,128)(2,1)} %constant.86.clone, s32[]{:T(128)S(6)} %select_n.60), kind=kLoop, calls=%fused_computation.1 | loop fusion | bytes 2359300 | tf_op jit(solution)/shard_map/jit(dynamic_index_in_dim)/squeeze | solution.py:235
  43.6 4.1 %collective-permute-done.6 = bf16[80,640]{1,0:T(8,128)(2,1)S(1)} collective-permute-done((bf16[80,640]{1,0:T(8,128)(2,1)S(1)}, bf16[80,640]{1,0:T(8,128)(2,1)S(1)}, u32[]{:S(2)}, u32[]{:S(2)}) %collective-permute-start.6) | collective-permute-done | bytes 102432 | tf_op jit(solution)/shard_map/ppermute | solution.py:28
  48.6 2.1 %broadcast_in_dim.46 = bf16[16,2,80,640]{3,2,1,0:T(8,128)(2,1)} broadcast(bf16[2,80,640]{2,1,0:T(8,128)(2,1)S(1)} %pad_maximum_fusion.2), dimensions={1,2,3} | broadcast | bytes 3481600 | tf_op jit(solution)/shard_map/broadcast_in_dim | solution.py:238
  50.7 12.7 %all-to-all-start.1 = ((bf16[16,2,80,640]{3,2,1,0:T(8,128)(2,1)}), bf16[16,2,80,640]{3,2,1,0:T(8,128)(2,1)S(1)}, u32[]{:S(2)}, u32[]{:S(2)}) async-start(bf16[16,2,80,640]{3,2,1,0:T(8,128)(2,1)} %broadcast_in_dim.46), calls=%async_computation.1 | async-start | bytes 6553600 | tf_op jit(solution)/shard_map/all_to_all | solution.py:238
  63.5 6.9 %attend.1 = (bf16[4,128,384]{2,1,0:T(8,128)(2,1)}, bf16[4,128,384]{2,1,0:T(8,128)(2,1)}) custom-call(s32[5,5]{1,0:T(8,128)} %concatenate.3.code_ref, bf16[2,144,640]{2,1,0:T(8,128)(2,1)} %pad_maximum_fusion.qa_ref, bf16[2,144,640]{2,1,0:T(8,128)(2,1)} %collective-permute-done.1.qb_ref, bf16[2,128,640]{2,1,0:T(8,128)(2,1)} %copy-done.3, ...), custom_call_target="tpu_custom_call" | custom-call | flops 60000002048 | bytes 4000000 | tf_op jit(solution)/shard_map/attend/pallas_call | solution.py:240
  70.4 2.6 %collective-permute-start.3 = (bf16[4,128,384]{2,1,0:T(8,128)(2,1)}, bf16[4,128,384]{2,1,0:T(8,128)(2,1)S(1)}, u32[]{:S(2)}, u32[]{:S(2)}) collective-permute-start(bf16[4,128,384]{2,1,0:T(8,128)(2,1)} %get-tuple-element.12), channel_id=1, source_target_pairs={{0,8},{1,9},{2,10},{3,11},{4,12},{5,13},{6,14},{7,15},{8,0},{9,1},... | collective-permute-start | bytes 1179656 | tf_op jit(solution)/shard_map/ppermute | solution.py:28
  73.0 1.5 collective-permute-done.3.got_ref
  76.2 7.4 %collective-permute-start.4 = (bf16[2,128,384]{2,1,0:T(8,128)(2,1)S(1)}, bf16[2,128,384]{2,1,0:T(8,128)(2,1)S(1)}, u32[]{:S(2)}, u32[]{:S(2)}) collective-permute-start(bf16[2,128,384]{2,1,0:T(8,128)(2,1)S(1)} %get-tuple-element.14), channel_id=1, source_target_pairs={{0,16},{1,17},{2,18},{3,19},{4,20},{5,21},{6,22},{7,23},{8,24},{9,... | collective-permute-start | bytes 589832 | tf_op jit(solution)/shard_map/ppermute | solution.py:28
  83.6 15.8 %collective-permute-done.4.got_ref = bf16[2,128,384]{2,1,0:T(8,128)(2,1)S(1)} collective-permute-done((bf16[2,128,384]{2,1,0:T(8,128)(2,1)S(1)}, bf16[2,128,384]{2,1,0:T(8,128)(2,1)S(1)}, u32[]{:S(2)}, u32[]{:S(2)}) %collective-permute-start.4) | collective-permute-done | bytes 196640 | tf_op jit(solution)/shard_map/ppermute | solution.py:28
  100.3 23.5 %all-gather = bf16[512,640]{1,0:T(8,128)(2,1)} all-gather(bf16[128,640]{1,0:T(8,128)(2,1)S(1)} %merge_last.1), channel_id=2, replica_groups={{0,1,2,3},{4,5,6,7},{8,9,10,11},{12,13,14,15},{16,17,18,19},{20,21,22,2..., dimensions={0}, use_global_device_ids=true | all-gather | bytes 819200 | tf_op jit(solution)/shard_map/all_gather | solution.py:268
  123.7 1.1 copy-done
  124.8 1.6 %project.1 = (f32[2,128,640]{2,1,0:T(8,128)S(1)}, bf16[2,128,640]{2,1,0:T(8,128)(2,1)S(1)}) custom-call(s32[1]{0:T(128)} %bitcast.1.place_ref, bf16[4,128,640]{2,1,0:T(8,128)(2,1)S(1)} %bitcast.32, bf16[4,2,320,640]{3,2,1,0:T(8,128)(2,1)S(1)} %bitcast.31), custom_call_target="tpu_custom_call" | custom-call | tf_op jit(solution)/shard_map/project/pallas_call | solution.py:270
  126.5 4.4 %collective-permute-start.8 = (bf16[2,128,640]{2,1,0:T(8,128)(2,1)S(1)}, bf16[2,128,640]{2,1,0:T(8,128)(2,1)S(1)}, u32[]{:S(2)}, u32[]{:S(2)}) collective-permute-start(bf16[2,128,640]{2,1,0:T(8,128)(2,1)S(1)} %get-tuple-element.16), channel_id=1, source_target_pairs={{0,8},{1,9},{2,10},{3,11},{4,12},{5,13},{6,14},{7,15},{8,0},{9,1},... | collective-permute-start | bytes 983048 | tf_op jit(solution)/shard_map/ppermute | solution.py:28
  132.2 6.1 %collective-permute-start.9 = (bf16[128,640]{1,0:T(8,128)(2,1)S(1)}, bf16[128,640]{1,0:T(8,128)(2,1)S(1)}, u32[]{:S(2)}, u32[]{:S(2)}) collective-permute-start(bf16[128,640]{1,0:T(8,128)(2,1)S(1)} %fusion.4), channel_id=1, source_target_pairs={{0,4},{1,5},{2,6},{3,7},{4,0},{5,1},{6,2},{7,3},{8,12},{9,13},{10,... | collective-permute-start | bytes 491528 | tf_op jit(solution)/shard_map/ppermute | solution.py:28
  138.5 16.0 %collective-permute-done.9 = bf16[128,640]{1,0:T(8,128)(2,1)S(1)} collective-permute-done((bf16[128,640]{1,0:T(8,128)(2,1)S(1)}, bf16[128,640]{1,0:T(8,128)(2,1)S(1)}, u32[]{:S(2)}, u32[]{:S(2)}) %collective-permute-start.9) | collective-permute-done | bytes 163872 | tf_op jit(solution)/shard_map/ppermute | solution.py:28
  (44 shorter events, 7.2 us)
Async XLA Ops:
  1.0 25.5 %copy-start.3 = (bf16[2,128,640]{2,1,0:T(8,128)(2,1)}, bf16[2,128,640]{2,1,0:T(8,128)(2,1)S(1)}, u32[]{:S(2)}) copy-start(bf16[2,128,640]{2,1,0:T(8,128)(2,1)S(1)} %pad_maximum_fusion.1.own_ref) | copy-start | bytes 983044
  1.0 24.2 %collective-permute-start.2 = (bf16[2,128,640]{2,1,0:T(8,128)(2,1)S(1)}, bf16[2,128,640]{2,1,0:T(8,128)(2,1)S(1)}, u32[]{:S(2)}, u32[]{:S(2)}) collective-permute-start(bf16[2,128,640]{2,1,0:T(8,128)(2,1)S(1)} %pad_maximum_fusion.1.own_ref), channel_id=1, source_target_pairs={{0,128},{1,129},{2,130},{3,131},{4,132},{5,133},{6,134},{7,135},{8... | collective-permute-start | bytes 983048 | tf_op jit(solution)/shard_map/ppermute | solution.py:28
  6.6 31.2 %collective-permute-start = (bf16[144,640]{1,0:T(8,128)(2,1)}, bf16[144,640]{1,0:T(8,128)(2,1)S(1)}, u32[]{:S(2)}, u32[]{:S(2)}) collective-permute-start(bf16[144,640]{1,0:T(8,128)(2,1)} %pack.1), channel_id=1, source_target_pairs={{0,16},{1,17},{2,18},{3,19},{4,20},{5,21},{6,22},{7,23},{8,24},{9,... | collective-permute-start | bytes 552968 | tf_op jit(solution)/shard_map/ppermute | solution.py:28
  22.0 9.6 %collective-permute-start.5 = (bf16[80,640]{1,0:T(8,128)(2,1)}, bf16[80,640]{1,0:T(8,128)(2,1)S(1)}, u32[]{:S(2)}, u32[]{:S(2)}) collective-permute-start(bf16[80,640]{1,0:T(8,128)(2,1)} %param.15), channel_id=1, source_target_pairs={{0,8},{1,9},{2,10},{3,11},{4,12},{5,13},{6,14},{7,15},{8,0},{9,1},... | collective-permute-start | bytes 307208 | tf_op jit(solution)/shard_map/ppermute | solution.py:28
  25.2 1.3 copy-start.5
  26.5 11.2 %copy-start.4 = (bf16[144,640]{1,0:T(8,128)(2,1)S(1)}, bf16[144,640]{1,0:T(8,128)(2,1)}, u32[]{:S(2)}) copy-start(bf16[144,640]{1,0:T(8,128)(2,1)} %pack.1) | copy-start | bytes 552964
  26.6 22.1 %all-to-all-start = ((bf16[4,2,128,640]{3,2,1,0:T(8,128)(2,1)}), bf16[4,2,128,640]{3,2,1,0:T(8,128)(2,1)S(1)}, u32[]{:S(2)}, u32[]{:S(2)}) async-start(bf16[4,2,128,640]{3,2,1,0:T(8,128)(2,1)} %broadcast_select_fusion), calls=%async_computation | async-start | bytes 2621440 | tf_op jit(solution)/shard_map/all_to_all | solution.py:200
  31.6 16.1 %collective-permute-start.6 = (bf16[80,640]{1,0:T(8,128)(2,1)S(1)}, bf16[80,640]{1,0:T(8,128)(2,1)S(1)}, u32[]{:S(2)}, u32[]{:S(2)}) collective-permute-start(bf16[80,640]{1,0:T(8,128)(2,1)S(1)} %collective-permute-done.5), channel_id=1, source_target_pairs={{0,24},{1,25},{2,26},{3,27},{4,392},{5,393},{6,394},{7,395},{8,16}... | collective-permute-start | bytes 307208 | tf_op jit(solution)/shard_map/ppermute | solution.py:28
  37.1 10.6 %collective-permute-start.7 = (bf16[80,640]{1,0:T(8,128)(2,1)S(1)}, bf16[80,640]{1,0:T(8,128)(2,1)S(1)}, u32[]{:S(2)}, u32[]{:S(2)}) collective-permute-start(bf16[80,640]{1,0:T(8,128)(2,1)S(1)} %collective-permute-done.5), channel_id=1, source_target_pairs={{4,408},{5,409},{6,410},{7,411},{12,400},{13,401},{14,402},{15,403... | collective-permute-start | bytes 307208 | tf_op jit(solution)/shard_map/ppermute | solution.py:28
  38.6 9.1 %copy-start.7 = (bf16[80,640]{1,0:T(8,128)(2,1)S(1)}, bf16[80,640]{1,0:T(8,128)(2,1)}, u32[]{:S(2)}) copy-start(bf16[80,640]{1,0:T(8,128)(2,1)} %param.15) | copy-start | bytes 307204
  38.6 24.9 %collective-permute-start.1 = (bf16[2,144,640]{2,1,0:T(8,128)(2,1)}, bf16[2,144,640]{2,1,0:T(8,128)(2,1)}, u32[]{:S(2)}, u32[]{:S(2)}) collective-permute-start(bf16[2,144,640]{2,1,0:T(8,128)(2,1)} %pad_maximum_fusion.qa_ref), channel_id=1, source_target_pairs={{0,8},{1,9},{2,10},{3,11},{4,12},{5,13},{6,14},{7,15},{8,0},{9,1},... | collective-permute-start | bytes 1105928 | tf_op jit(solution)/shard_map/ppermute | solution.py:28
  48.6 2.1 %copy-start.2 = (bf16[4,2,128,640]{3,2,1,0:T(8,128)(2,1)}, bf16[4,2,128,640]{3,2,1,0:T(8,128)(2,1)S(1)}, u32[]{:S(2)}) copy-start(bf16[4,2,128,640]{3,2,1,0:T(8,128)(2,1)S(1)} %all-to-all-done.row_ref) | copy-start | bytes 3932164
  50.7 73.0 %all-to-all-start.1 = ((bf16[16,2,80,640]{3,2,1,0:T(8,128)(2,1)}), bf16[16,2,80,640]{3,2,1,0:T(8,128)(2,1)S(1)}, u32[]{:S(2)}, u32[]{:S(2)}) async-start(bf16[16,2,80,640]{3,2,1,0:T(8,128)(2,1)} %broadcast_in_dim.46), calls=%async_computation.1 | async-start | bytes 6553600 | tf_op jit(solution)/shard_map/all_to_all | solution.py:238
  63.5 9.5 %copy-start.8 = (bf16[2,2,128,384]{3,2,1,0:T(8,128)(2,1)S(1)}, bf16[2,2,128,384]{3,2,1,0:T(8,128)(2,1)}, u32[]{:S(2)}) copy-start(bf16[2,2,128,384]{3,2,1,0:T(8,128)(2,1)} %constant.87.clone) | copy-start | bytes 1179652
  70.4 4.1 %collective-permute-start.3 = (bf16[4,128,384]{2,1,0:T(8,128)(2,1)}, bf16[4,128,384]{2,1,0:T(8,128)(2,1)S(1)}, u32[]{:S(2)}, u32[]{:S(2)}) collective-permute-start(bf16[4,128,384]{2,1,0:T(8,128)(2,1)} %get-tuple-element.12), channel_id=1, source_target_pairs={{0,8},{1,9},{2,10},{3,11},{4,12},{5,13},{6,14},{7,15},{8,0},{9,1},... | collective-permute-start | bytes 1179656 | tf_op jit(solution)/shard_map/ppermute | solution.py:28
  74.5 1.0 copy-start.1
  76.2 23.2 %collective-permute-start.4 = (bf16[2,128,384]{2,1,0:T(8,128)(2,1)S(1)}, bf16[2,128,384]{2,1,0:T(8,128)(2,1)S(1)}, u32[]{:S(2)}, u32[]{:S(2)}) collective-permute-start(bf16[2,128,384]{2,1,0:T(8,128)(2,1)S(1)} %get-tuple-element.14), channel_id=1, source_target_pairs={{0,16},{1,17},{2,18},{3,19},{4,20},{5,21},{6,22},{7,23},{8,24},{9,... | collective-permute-start | bytes 589832 | tf_op jit(solution)/shard_map/ppermute | solution.py:28
  123.7 1.1 copy-start
  126.5 11.9 %copy-start.9 = (f32[8,640]{1,0:T(8,128)S(1)}, f32[8,640]{1,0:T(8,128)}, u32[]{:S(2)}) copy-start(f32[8,640]{1,0:T(8,128)} %param.16) | copy-start | bytes 61444
  126.5 28.0 %copy-start.6 = (bf16[128,640]{1,0:T(8,128)(2,1)S(1)}, bf16[128,640]{1,0:T(8,128)(2,1)}, u32[]{:S(2)}) copy-start(bf16[128,640]{1,0:T(8,128)(2,1)} %param.14) | copy-start | bytes 491524
  126.5 5.6 %collective-permute-start.8 = (bf16[2,128,640]{2,1,0:T(8,128)(2,1)S(1)}, bf16[2,128,640]{2,1,0:T(8,128)(2,1)S(1)}, u32[]{:S(2)}, u32[]{:S(2)}) collective-permute-start(bf16[2,128,640]{2,1,0:T(8,128)(2,1)S(1)} %get-tuple-element.16), channel_id=1, source_target_pairs={{0,8},{1,9},{2,10},{3,11},{4,12},{5,13},{6,14},{7,15},{8,0},{9,1},... | collective-permute-start | bytes 983048 | tf_op jit(solution)/shard_map/ppermute | solution.py:28
  132.2 22.2 %collective-permute-start.9 = (bf16[128,640]{1,0:T(8,128)(2,1)S(1)}, bf16[128,640]{1,0:T(8,128)(2,1)S(1)}, u32[]{:S(2)}, u32[]{:S(2)}) collective-permute-start(bf16[128,640]{1,0:T(8,128)(2,1)S(1)} %fusion.4), channel_id=1, source_target_pairs={{0,4},{1,5},{2,6},{3,7},{4,0},{5,1},{6,2},{7,3},{8,12},{9,13},{10,... | collective-permute-start | bytes 491528 | tf_op jit(solution)/shard_map/ppermute | solution.py:28

commit v5 on v4

--- a/solution.py
+++ b/solution.py
@@ -1,3 +1,5 @@
+import functools
+
 import jax
 import jax.numpy as jnp
 import numpy as np
@@ -158,10 +160,9 @@
     out_ref[:, 512:640] = jnp.where(lanes < 64, ends[0], pltpu.roll(ends[1], 64, 1)).astype(jnp.bfloat16)
 
 
-def project_kernel(place_ref, all_ref, w_ref, keep_ref, send_ref):
+def project_kernel(away, place_ref, all_ref, w_ref, keep_ref, send_ref):
     side = place_ref[0]
-    here = jnp.zeros((2 * TOK, FEAT), jnp.float32)
-    there = jnp.zeros((2 * TOK, FEAT), jnp.float32)
+    total = jnp.zeros((2 * TOK, FEAT), jnp.float32)
     for near in range(2):
         for odd in range(2):
             rows = all_ref[2 * near + odd]
@@ -169,14 +170,10 @@
             turned = pltpu.roll(ends.astype(jnp.float32), 64, 1).astype(jnp.bfloat16)
             wide = jnp.concatenate([rows[:, 0:256], rows[:, 256:512]], axis=0)
             narrow = jnp.concatenate([ends[:, 0:64], turned[:, 0:64]], axis=0)
-            w_here = w_ref.at[2 * side + near, odd]
-            w_there = w_ref.at[3 - 2 * side - near, odd]
-            here = here + dot_f32(wide, w_here[0:256]) + dot_f32(narrow, w_here[256:320])
-            there = there + dot_f32(wide, w_there[0:256]) + dot_f32(narrow, w_there[256:320])
-    keep_ref[0] = here[0:TOK]
-    keep_ref[1] = there[0:TOK]
-    send_ref[0] = here[TOK:].astype(jnp.bfloat16)
-    send_ref[1] = there[TOK:].astype(jnp.bfloat16)
+            w_at = w_ref.at[3 - 2 * side - near if away else 2 * side + near, odd]
+            total = total + dot_f32(wide, w_at[0:256]) + dot_f32(narrow, w_at[256:320])
+    keep_ref[...] = total[0:TOK]
+    send_ref[...] = total[TOK:].astype(jnp.bfloat16)
 
 
 VMEM = pl.BlockSpec(memory_space=pltpu.VMEM)
@@ -267,21 +264,26 @@
     )(keep, got, table)
     attended = lax.all_gather(attended, "zl", axis=0, axis_index_groups=[[0, 1, 2, 3], [4, 5, 6, 7]])
 
-    keep, send = pl.pallas_call(
-        project_kernel,
-        out_shape=(jax.ShapeDtypeStruct((2, TOK, FEAT), jnp.float32), bf16(2, TOK, FEAT)),
-        in_specs=[SMEM] + [VMEM] * 2,
-        out_specs=(VMEM, VMEM),
-        compiler_params=PARAMS,
-        name="project",
-    )((zl // 4).reshape(1), attended, weight)
-    got = move(send, lambda x, y, h, c, l: (x, y, h, 1 - c, l))
-    summed = keep + got.astype(jnp.float32)
-    far = move(summed[1].astype(jnp.bfloat16), lambda x, y, h, c, l: (x, y, h, c, l ^ 4))
+    def project(away, attended):
+        keep, send = pl.pallas_call(
+            functools.partial(project_kernel, away),
+            out_shape=(jax.ShapeDtypeStruct((TOK, FEAT), jnp.float32), bf16(TOK, FEAT)),
+            in_specs=[SMEM] + [VMEM] * 2,
+            out_specs=(VMEM, VMEM),
+            compiler_params=PARAMS,
+            name="project",
+        )((zl // 4).reshape(1), attended, weight)
+        got = move(send, lambda x, y, h, c, l: (x, y, h, 1 - c, l))
+        return keep + got.astype(jnp.float32)
+
+    there = project(True, attended).astype(jnp.bfloat16)
+    far = move(there, lambda x, y, h, c, l: (x, y, h, c, l ^ 4))
+    attended, unused = lax.optimization_barrier((attended, there))
+    here = project(False, attended)
 
     level_pick = (jnp.arange(LEVELS, dtype=jnp.int32) == levels[0]).astype(jnp.float32)
     gate_row = jnp.sum(level_pick[:, None] * level_gate, axis=0)
-    projected = summed[0] + far.astype(jnp.float32)
+    projected = here + far.astype(jnp.float32)
     return (latents.astype(jnp.float32) + gate_row[None, :] * projected).astype(jnp.bfloat16)
 
 

time: 156 us -> 155 us (level)
  waiting for transfers between devices: 38.8 us -> 34.9 us
  starting transfers between devices: 68.3 us -> 71 us
    ppermute x10 -> x11, waiting for transfers between devices: 37.9 us -> 34.1 us  [move(): return lax.ppermute(value, AXES, pairs)]
    ppermute x10 -> x11, starting transfers between devices: 51.2 us -> 53.9 us  [move(): return lax.ppermute(value, AXES, pairs)]
  transfers between devices with their start and end apart: 12 -> 13, of which waited for: 6 -> 7; matrix products, arithmetic and copies ran while one was open for 5% -> 5% of each run, Pallas kernels for 6% -> 7%
where the time goes in v5:
time: 155 us; the launch traced here: 154 us
  starting transfers between devices  71 us (46%)
  waiting for transfers between devices  34.9 us (23%)
  blocking collectives  23.4 us (15%)
  Pallas kernels  11.9 us (8%)
  local copies, waits for them, and re-layouts  7.25 us (5%)
  other arithmetic  4.19 us (3%)
  between operations  1.59 us (1%)
    ppermute x11, starting transfers between devices, move(): return lax.ppermute(value, AXES, pairs)  53.9 us
    ppermute x11, waiting for transfers between devices, move(): return lax.ppermute(value, AXES, pairs)  34.1 us
    all_gather x1, blocking collectives, on_device(): lax.all_gather(attended, 'zl', axis=0, axis_index_groups=[[0, 1, 2, 3], [...  23.4 us
    all_to_all x1, starting transfers between devices, on_device(): lax.all_to_all(jnp.broadcast_to(w_pair[None], (16, 2, 80, FEAT)), ('x', '...  12.7 us
    pallas_call x1, Pallas kernels, on_device(): pl.pallas_call(attend_kernel, out_shape=(bf16(4, TOK, WIDE), bf16(4, TOK,...  6.89 us
    all_to_all x1, starting transfers between devices, on_device(): lax.all_to_all(jnp.where(to > y, kv_own[None], kv_far[None]), 'y', 0, 0,...  4.32 us
  transfers between devices with their start and end apart: 13, of which 7 were waited for; matrix products, arithmetic and copies ran while one was open for 5% of the time, Pallas kernels for 7%

profile of v5, /device:TPU:1, one launch (start us, length us, event | category | flops | bytes accessed | tf_op | source)
XLA Modules:
  0.0 154.3 jit_solution(10459212624792910350)
XLA Ops:
  0.0 1.0 pad_maximum_fusion.1.own_ref
  1.0 3.9 %collective-permute-start.2 = (bf16[2,128,640]{2,1,0:T(8,128)(2,1)S(1)}, bf16[2,128,640]{2,1,0:T(8,128)(2,1)S(1)}, u32[]{:S(2)}, u32[]{:S(2)}) collective-permute-start(bf16[2,128,640]{2,1,0:T(8,128)(2,1)S(1)} %pad_maximum_fusion.1.own_ref), channel_id=1, source_target_pairs={{0,128},{1,129},{2,130},{3,131},{4,132},{5,133},{6,134},{7,135},{8... | collective-permute-start | bytes 983048 | tf_op jit(solution)/shard_map/ppermute | solution.py:30
  5.0 1.6 %pack.1 = bf16[144,640]{1,0:T(8,128)(2,1)} custom-call(bf16[128,640]{1,0:T(8,128)(2,1)} %query_ref.1, s32[1,16]{1,0:T(1,128)} %mask_ref.1), custom_call_target="tpu_custom_call" | custom-call | tf_op jit(solution)/shard_map/pack/pallas_call | solution.py:213
  6.6 15.4 %collective-permute-start = (bf16[144,640]{1,0:T(8,128)(2,1)}, bf16[144,640]{1,0:T(8,128)(2,1)S(1)}, u32[]{:S(2)}, u32[]{:S(2)}) collective-permute-start(bf16[144,640]{1,0:T(8,128)(2,1)} %pack.1), channel_id=1, source_target_pairs={{0,16},{1,17},{2,18},{3,19},{4,20},{5,21},{6,22},{7,23},{8,24},{9,... | collective-permute-start | bytes 552968 | tf_op jit(solution)/shard_map/ppermute | solution.py:30
  22.0 3.1 %collective-permute-start.5 = (bf16[80,640]{1,0:T(8,128)(2,1)}, bf16[80,640]{1,0:T(8,128)(2,1)S(1)}, u32[]{:S(2)}, u32[]{:S(2)}) collective-permute-start(bf16[80,640]{1,0:T(8,128)(2,1)} %param.15), channel_id=1, source_target_pairs={{0,8},{1,9},{2,10},{3,11},{4,12},{5,13},{6,14},{7,15},{8,0},{9,1},... | collective-permute-start | bytes 307208 | tf_op jit(solution)/shard_map/ppermute | solution.py:30
  25.2 1.3 broadcast_select_fusion
  26.6 4.3 %all-to-all-start = ((bf16[4,2,128,640]{3,2,1,0:T(8,128)(2,1)}), bf16[4,2,128,640]{3,2,1,0:T(8,128)(2,1)S(1)}, u32[]{:S(2)}, u32[]{:S(2)}) async-start(bf16[4,2,128,640]{3,2,1,0:T(8,128)(2,1)} %broadcast_select_fusion), calls=%async_computation | async-start | bytes 2621440 | tf_op jit(solution)/shard_map/all_to_all | solution.py:197
  31.6 5.5 %collective-permute-start.6 = (bf16[80,640]{1,0:T(8,128)(2,1)S(1)}, bf16[80,640]{1,0:T(8,128)(2,1)S(1)}, u32[]{:S(2)}, u32[]{:S(2)}) collective-permute-start(bf16[80,640]{1,0:T(8,128)(2,1)S(1)} %collective-permute-done.5), channel_id=1, source_target_pairs={{0,24},{1,25},{2,26},{3,27},{4,392},{5,393},{6,394},{7,395},{8,16}... | collective-permute-start | bytes 307208 | tf_op jit(solution)/shard_map/ppermute | solution.py:30
  38.6 2.0 %collective-permute-start.1 = (bf16[2,144,640]{2,1,0:T(8,128)(2,1)}, bf16[2,144,640]{2,1,0:T(8,128)(2,1)}, u32[]{:S(2)}, u32[]{:S(2)}) collective-permute-start(bf16[2,144,640]{2,1,0:T(8,128)(2,1)} %pad_maximum_fusion.qa_ref), channel_id=1, source_target_pairs={{0,8},{1,9},{2,10},{3,11},{4,12},{5,13},{6,14},{7,15},{8,0},{9,1},... | collective-permute-start | bytes 1105928 | tf_op jit(solution)/shard_map/ppermute | solution.py:30
  40.6 2.4 %dynamic-slice_bitcast_fusion.select_ref = bf16[768,768]{1,0:T(8,128)(2,1)} fusion(bf16[2,768,768]{2,1,0:T(8,128)(2,1)} %constant.88.clone, s32[]{:T(128)S(6)} %select_n.61), kind=kLoop, calls=%fused_computation.1 | loop fusion | bytes 2359300 | tf_op jit(solution)/shard_map/jit(dynamic_index_in_dim)/squeeze | solution.py:232
  43.6 4.0 %collective-permute-done.6 = bf16[80,640]{1,0:T(8,128)(2,1)S(1)} collective-permute-done((bf16[80,640]{1,0:T(8,128)(2,1)S(1)}, bf16[80,640]{1,0:T(8,128)(2,1)S(1)}, u32[]{:S(2)}, u32[]{:S(2)}) %collective-permute-start.6) | collective-permute-done | bytes 102432 | tf_op jit(solution)/shard_map/ppermute | solution.py:30
  48.6 2.1 %broadcast_in_dim.46 = bf16[16,2,80,640]{3,2,1,0:T(8,128)(2,1)} broadcast(bf16[2,80,640]{2,1,0:T(8,128)(2,1)S(1)} %pad_maximum_fusion.2), dimensions={1,2,3} | broadcast | bytes 3481600 | tf_op jit(solution)/shard_map/broadcast_in_dim | solution.py:235
  50.7 12.7 %all-to-all-start.1 = ((bf16[16,2,80,640]{3,2,1,0:T(8,128)(2,1)}), bf16[16,2,80,640]{3,2,1,0:T(8,128)(2,1)S(1)}, u32[]{:S(2)}, u32[]{:S(2)}) async-start(bf16[16,2,80,640]{3,2,1,0:T(8,128)(2,1)} %broadcast_in_dim.46), calls=%async_computation.1 | async-start | bytes 6553600 | tf_op jit(solution)/shard_map/all_to_all | solution.py:235
  63.5 6.9 %attend.1 = (bf16[4,128,384]{2,1,0:T(8,128)(2,1)}, bf16[4,128,384]{2,1,0:T(8,128)(2,1)}) custom-call(s32[5,5]{1,0:T(8,128)} %concatenate.3.code_ref, bf16[2,144,640]{2,1,0:T(8,128)(2,1)} %pad_maximum_fusion.qa_ref, bf16[2,144,640]{2,1,0:T(8,128)(2,1)} %collective-permute-done.1.qb_ref, bf16[2,128,640]{2,1,0:T(8,128)(2,1)} %copy-done.3, ...), custom_call_target="tpu_custom_call" | custom-call | flops 60000002048 | bytes 4000000 | tf_op jit(solution)/shard_map/attend/pallas_call | solution.py:237
  70.4 2.6 %collective-permute-start.3 = (bf16[4,128,384]{2,1,0:T(8,128)(2,1)}, bf16[4,128,384]{2,1,0:T(8,128)(2,1)S(1)}, u32[]{:S(2)}, u32[]{:S(2)}) collective-permute-start(bf16[4,128,384]{2,1,0:T(8,128)(2,1)} %get-tuple-element.15), channel_id=1, source_target_pairs={{0,8},{1,9},{2,10},{3,11},{4,12},{5,13},{6,14},{7,15},{8,0},{9,1},... | collective-permute-start | bytes 1179656 | tf_op jit(solution)/shard_map/ppermute | solution.py:30
  73.0 1.5 collective-permute-done.3.got_ref
  76.2 7.4 %collective-permute-start.4 = (bf16[2,128,384]{2,1,0:T(8,128)(2,1)S(1)}, bf16[2,128,384]{2,1,0:T(8,128)(2,1)S(1)}, u32[]{:S(2)}, u32[]{:S(2)}) collective-permute-start(bf16[2,128,384]{2,1,0:T(8,128)(2,1)S(1)} %get-tuple-element.17), channel_id=1, source_target_pairs={{0,16},{1,17},{2,18},{3,19},{4,20},{5,21},{6,22},{7,23},{8,24},{9,... | collective-permute-start | bytes 589832 | tf_op jit(solution)/shard_map/ppermute | solution.py:30
  83.6 15.8 %collective-permute-done.4.got_ref = bf16[2,128,384]{2,1,0:T(8,128)(2,1)S(1)} collective-permute-done((bf16[2,128,384]{2,1,0:T(8,128)(2,1)S(1)}, bf16[2,128,384]{2,1,0:T(8,128)(2,1)S(1)}, u32[]{:S(2)}, u32[]{:S(2)}) %collective-permute-start.4) | collective-permute-done | bytes 196640 | tf_op jit(solution)/shard_map/ppermute | solution.py:30
  100.3 23.4 %all-gather = bf16[512,640]{1,0:T(8,128)(2,1)} all-gather(bf16[128,640]{1,0:T(8,128)(2,1)S(1)} %merge_last.1), channel_id=2, replica_groups={{0,1,2,3},{4,5,6,7},{8,9,10,11},{12,13,14,15},{16,17,18,19},{20,21,22,2..., dimensions={0}, use_global_device_ids=true | all-gather | bytes 819200 | tf_op jit(solution)/shard_map/all_gather | solution.py:265
  123.7 1.1 copy-done
  125.7 4.3 %collective-permute-start.8 = (bf16[128,640]{1,0:T(8,128)(2,1)S(1)}, bf16[128,640]{1,0:T(8,128)(2,1)S(1)}, u32[]{:S(2)}, u32[]{:S(2)}) collective-permute-start(bf16[128,640]{1,0:T(8,128)(2,1)S(1)} %get-tuple-element.19), channel_id=1, source_target_pairs={{0,8},{1,9},{2,10},{3,11},{4,12},{5,13},{6,14},{7,15},{8,0},{9,1},... | collective-permute-start | bytes 491528 | tf_op jit(solution)/shard_map/ppermute | solution.py:30
  131.1 6.4 %collective-permute-start.10 = (bf16[128,640]{1,0:T(8,128)(2,1)S(1)}, bf16[128,640]{1,0:T(8,128)(2,1)S(1)}, u32[]{:S(2)}, u32[]{:S(2)}) collective-permute-start(bf16[128,640]{1,0:T(8,128)(2,1)S(1)} %add_convert_fusion.1), channel_id=1, source_target_pairs={{0,4},{1,5},{2,6},{3,7},{4,0},{5,1},{6,2},{7,3},{8,12},{9,13},{10,... | collective-permute-start | bytes 491528 | tf_op jit(solution)/shard_map/ppermute | solution.py:30
  138.4 2.5 %collective-permute-start.9 = (bf16[128,640]{1,0:T(8,128)(2,1)S(1)}, bf16[128,640]{1,0:T(8,128)(2,1)S(1)}, u32[]{:S(2)}, u32[]{:S(2)}) collective-permute-start(bf16[128,640]{1,0:T(8,128)(2,1)S(1)} %get-tuple-element.22), channel_id=1, source_target_pairs={{0,8},{1,9},{2,10},{3,11},{4,12},{5,13},{6,14},{7,15},{8,0},{9,1},... | collective-permute-start | bytes 491528 | tf_op jit(solution)/shard_map/ppermute | solution.py:30
  142.0 11.5 %collective-permute-done.10 = bf16[128,640]{1,0:T(8,128)(2,1)S(1)} collective-permute-done((bf16[128,640]{1,0:T(8,128)(2,1)S(1)}, bf16[128,640]{1,0:T(8,128)(2,1)S(1)}, u32[]{:S(2)}, u32[]{:S(2)}) %collective-permute-start.10) | collective-permute-done | bytes 163872 | tf_op jit(solution)/shard_map/ppermute | solution.py:30
  (46 shorter events, 9.7 us)
Async XLA Ops:
  1.0 25.5 %copy-start.3 = (bf16[2,128,640]{2,1,0:T(8,128)(2,1)}, bf16[2,128,640]{2,1,0:T(8,128)(2,1)S(1)}, u32[]{:S(2)}) copy-start(bf16[2,128,640]{2,1,0:T(8,128)(2,1)S(1)} %pad_maximum_fusion.1.own_ref) | copy-start | bytes 983044
  1.0 24.2 %collective-permute-start.2 = (bf16[2,128,640]{2,1,0:T(8,128)(2,1)S(1)}, bf16[2,128,640]{2,1,0:T(8,128)(2,1)S(1)}, u32[]{:S(2)}, u32[]{:S(2)}) collective-permute-start(bf16[2,128,640]{2,1,0:T(8,128)(2,1)S(1)} %pad_maximum_fusion.1.own_ref), channel_id=1, source_target_pairs={{0,128},{1,129},{2,130},{3,131},{4,132},{5,133},{6,134},{7,135},{8... | collective-permute-start | bytes 983048 | tf_op jit(solution)/shard_map/ppermute | solution.py:30
  6.6 31.2 %collective-permute-start = (bf16[144,640]{1,0:T(8,128)(2,1)}, bf16[144,640]{1,0:T(8,128)(2,1)S(1)}, u32[]{:S(2)}, u32[]{:S(2)}) collective-permute-start(bf16[144,640]{1,0:T(8,128)(2,1)} %pack.1), channel_id=1, source_target_pairs={{0,16},{1,17},{2,18},{3,19},{4,20},{5,21},{6,22},{7,23},{8,24},{9,... | collective-permute-start | bytes 552968 | tf_op jit(solution)/shard_map/ppermute | solution.py:30
  22.0 9.6 %collective-permute-start.5 = (bf16[80,640]{1,0:T(8,128)(2,1)}, bf16[80,640]{1,0:T(8,128)(2,1)S(1)}, u32[]{:S(2)}, u32[]{:S(2)}) collective-permute-start(bf16[80,640]{1,0:T(8,128)(2,1)} %param.15), channel_id=1, source_target_pairs={{0,8},{1,9},{2,10},{3,11},{4,12},{5,13},{6,14},{7,15},{8,0},{9,1},... | collective-permute-start | bytes 307208 | tf_op jit(solution)/shard_map/ppermute | solution.py:30
  25.2 1.3 copy-start.5
  26.6 11.2 %copy-start.4 = (bf16[144,640]{1,0:T(8,128)(2,1)S(1)}, bf16[144,640]{1,0:T(8,128)(2,1)}, u32[]{:S(2)}) copy-start(bf16[144,640]{1,0:T(8,128)(2,1)} %pack.1) | copy-start | bytes 552964
  26.6 22.1 %all-to-all-start = ((bf16[4,2,128,640]{3,2,1,0:T(8,128)(2,1)}), bf16[4,2,128,640]{3,2,1,0:T(8,128)(2,1)S(1)}, u32[]{:S(2)}, u32[]{:S(2)}) async-start(bf16[4,2,128,640]{3,2,1,0:T(8,128)(2,1)} %broadcast_select_fusion), calls=%async_computation | async-start | bytes 2621440 | tf_op jit(solution)/shard_map/all_to_all | solution.py:197
  31.6 16.1 %collective-permute-start.6 = (bf16[80,640]{1,0:T(8,128)(2,1)S(1)}, bf16[80,640]{1,0:T(8,128)(2,1)S(1)}, u32[]{:S(2)}, u32[]{:S(2)}) collective-permute-start(bf16[80,640]{1,0:T(8,128)(2,1)S(1)} %collective-permute-done.5), channel_id=1, source_target_pairs={{0,24},{1,25},{2,26},{3,27},{4,392},{5,393},{6,394},{7,395},{8,16}... | collective-permute-start | bytes 307208 | tf_op jit(solution)/shard_map/ppermute | solution.py:30
  37.1 10.6 %collective-permute-start.7 = (bf16[80,640]{1,0:T(8,128)(2,1)S(1)}, bf16[80,640]{1,0:T(8,128)(2,1)S(1)}, u32[]{:S(2)}, u32[]{:S(2)}) collective-permute-start(bf16[80,640]{1,0:T(8,128)(2,1)S(1)} %collective-permute-done.5), channel_id=1, source_target_pairs={{4,408},{5,409},{6,410},{7,411},{12,400},{13,401},{14,402},{15,403... | collective-permute-start | bytes 307208 | tf_op jit(solution)/shard_map/ppermute | solution.py:30
  38.6 9.1 %copy-start.7 = (bf16[80,640]{1,0:T(8,128)(2,1)S(1)}, bf16[80,640]{1,0:T(8,128)(2,1)}, u32[]{:S(2)}) copy-start(bf16[80,640]{1,0:T(8,128)(2,1)} %param.15) | copy-start | bytes 307204
  38.6 24.9 %collective-permute-start.1 = (bf16[2,144,640]{2,1,0:T(8,128)(2,1)}, bf16[2,144,640]{2,1,0:T(8,128)(2,1)}, u32[]{:S(2)}, u32[]{:S(2)}) collective-permute-start(bf16[2,144,640]{2,1,0:T(8,128)(2,1)} %pad_maximum_fusion.qa_ref), channel_id=1, source_target_pairs={{0,8},{1,9},{2,10},{3,11},{4,12},{5,13},{6,14},{7,15},{8,0},{9,1},... | collective-permute-start | bytes 1105928 | tf_op jit(solution)/shard_map/ppermute | solution.py:30
  48.6 2.1 %copy-start.2 = (bf16[4,2,128,640]{3,2,1,0:T(8,128)(2,1)}, bf16[4,2,128,640]{3,2,1,0:T(8,128)(2,1)S(1)}, u32[]{:S(2)}) copy-start(bf16[4,2,128,640]{3,2,1,0:T(8,128)(2,1)S(1)} %all-to-all-done.row_ref) | copy-start | bytes 3932164
  50.7 73.0 %all-to-all-start.1 = ((bf16[16,2,80,640]{3,2,1,0:T(8,128)(2,1)}), bf16[16,2,80,640]{3,2,1,0:T(8,128)(2,1)S(1)}, u32[]{:S(2)}, u32[]{:S(2)}) async-start(bf16[16,2,80,640]{3,2,1,0:T(8,128)(2,1)} %broadcast_in_dim.46), calls=%async_computation.1 | async-start | bytes 6553600 | tf_op jit(solution)/shard_map/all_to_all | solution.py:235
  63.5 9.5 %copy-start.8 = (bf16[2,2,128,384]{3,2,1,0:T(8,128)(2,1)S(1)}, bf16[2,2,128,384]{3,2,1,0:T(8,128)(2,1)}, u32[]{:S(2)}) copy-start(bf16[2,2,128,384]{3,2,1,0:T(8,128)(2,1)} %constant.89.clone) | copy-start | bytes 1179652
  70.4 4.1 %collective-permute-start.3 = (bf16[4,128,384]{2,1,0:T(8,128)(2,1)}, bf16[4,128,384]{2,1,0:T(8,128)(2,1)S(1)}, u32[]{:S(2)}, u32[]{:S(2)}) collective-permute-start(bf16[4,128,384]{2,1,0:T(8,128)(2,1)} %get-tuple-element.15), channel_id=1, source_target_pairs={{0,8},{1,9},{2,10},{3,11},{4,12},{5,13},{6,14},{7,15},{8,0},{9,1},... | collective-permute-start | bytes 1179656 | tf_op jit(solution)/shard_map/ppermute | solution.py:30
  74.5 1.0 copy-start.1
  76.2 23.2 %collective-permute-start.4 = (bf16[2,128,384]{2,1,0:T(8,128)(2,1)S(1)}, bf16[2,128,384]{2,1,0:T(8,128)(2,1)S(1)}, u32[]{:S(2)}, u32[]{:S(2)}) collective-permute-start(bf16[2,128,384]{2,1,0:T(8,128)(2,1)S(1)} %get-tuple-element.17), channel_id=1, source_target_pairs={{0,16},{1,17},{2,18},{3,19},{4,20},{5,21},{6,22},{7,23},{8,24},{9,... | collective-permute-start | bytes 589832 | tf_op jit(solution)/shard_map/ppermute | solution.py:30
  123.7 1.1 copy-start
  125.7 5.3 %collective-permute-start.8 = (bf16[128,640]{1,0:T(8,128)(2,1)S(1)}, bf16[128,640]{1,0:T(8,128)(2,1)S(1)}, u32[]{:S(2)}, u32[]{:S(2)}) collective-permute-start(bf16[128,640]{1,0:T(8,128)(2,1)S(1)} %get-tuple-element.19), channel_id=1, source_target_pairs={{0,8},{1,9},{2,10},{3,11},{4,12},{5,13},{6,14},{7,15},{8,0},{9,1},... | collective-permute-start | bytes 491528 | tf_op jit(solution)/shard_map/ppermute | solution.py:30
  131.1 9.9 %copy-start.9 = (f32[8,640]{1,0:T(8,128)S(1)}, f32[8,640]{1,0:T(8,128)}, u32[]{:S(2)}) copy-start(f32[8,640]{1,0:T(8,128)} %param.16) | copy-start | bytes 61444
  131.1 22.4 %copy-start.6 = (bf16[128,640]{1,0:T(8,128)(2,1)S(1)}, bf16[128,640]{1,0:T(8,128)(2,1)}, u32[]{:S(2)}) copy-start(bf16[128,640]{1,0:T(8,128)(2,1)} %param.14) | copy-start | bytes 491524
  131.1 22.4 %collective-permute-start.10 = (bf16[128,640]{1,0:T(8,128)(2,1)S(1)}, bf16[128,640]{1,0:T(8,128)(2,1)S(1)}, u32[]{:S(2)}, u32[]{:S(2)}) collective-permute-start(bf16[128,640]{1,0:T(8,128)(2,1)S(1)} %add_convert_fusion.1), channel_id=1, source_target_pairs={{0,4},{1,5},{2,6},{3,7},{4,0},{5,1},{6,2},{7,3},{8,12},{9,13},{10,... | collective-permute-start | bytes 491528 | tf_op jit(solution)/shard_map/ppermute | solution.py:30
  138.4 3.6 %collective-permute-start.9 = (bf16[128,640]{1,0:T(8,128)(2,1)S(1)}, bf16[128,640]{1,0:T(8,128)(2,1)S(1)}, u32[]{:S(2)}, u32[]{:S(2)}) collective-permute-start(bf16[128,640]{1,0:T(8,128)(2,1)S(1)} %get-tuple-element.22), channel_id=1, source_target_pairs={{0,8},{1,9},{2,10},{3,11},{4,12},{5,13},{6,14},{7,15},{8,0},{9,1},... | collective-permute-start | bytes 491528 | tf_op jit(solution)/shard_map/ppermute | solution.py:30

commit v6 on v5

--- a/solution.py
+++ b/solution.py
@@ -68,10 +68,11 @@
 
 
 def pack_kernel(query_ref, mask_ref, out_ref):
-    out_ref[0:TOK, :] = query_ref[...]
-    out_ref[TOK : TOK + 16, :] = jnp.zeros((16, FEAT), jnp.bfloat16)
+    for h in range(HEADS_HERE):
+        out_ref[h * HD : (h + 1) * HD, :] = query_ref[:, h * HD : (h + 1) * HD]
+    out_ref[FEAT : FEAT + 16, :] = jnp.zeros((16, HD), jnp.bfloat16)
     flags = jnp.broadcast_to(mask_ref[...].astype(jnp.float32), (16, 16))
-    out_ref[TOK : TOK + 16, 0:16] = flags.astype(jnp.bfloat16)
+    out_ref[FEAT : FEAT + 16, 0:16] = flags.astype(jnp.bfloat16)
 
 
 def attend_kernel(code_ref, qa_ref, qb_ref, own_ref, row_ref, far_ref, select_ref, mine_ref, theirs_ref, all_ref):
@@ -82,7 +83,7 @@
     biases = []
     for r in range(4):
         q_ref = qa_ref if r % 2 == 0 else qb_ref
-        flags = q_ref[r // 2, TOK : TOK + 16, 0:HD].astype(jnp.float32)[0:1]
+        flags = q_ref[r // 2, FEAT : FEAT + 16].astype(jnp.float32)[0:1]
         row = []
         for d in range(5):
             code = code_ref[r, d]
@@ -96,7 +97,7 @@
         keys = jnp.concatenate([ref[0, :, cols] for ref in kv_refs], axis=0)
         values = jnp.concatenate([ref[1, :, cols] for ref in kv_refs], axis=0)
         queries = jnp.concatenate(
-            [(qa_ref if r % 2 == 0 else qb_ref)[r // 2, 0:TOK, cols] for r in range(4)], axis=0
+            [(qa_ref if r % 2 == 0 else qb_ref)[r // 2, cols, :] for r in range(4)], axis=0
         )
         scores = lax.dot_general(queries, keys, (((1,), (1,)), ((), ())), preferred_element_type=jnp.float32)
         parts = []
@@ -114,8 +115,8 @@
         all_ref[:, cols] = summed.astype(jnp.bfloat16)
     for r in range(4):
         all_ref[r * TOK : (r + 1) * TOK, FEAT:] = stats[r].astype(jnp.bfloat16)
-    mine_ref[...] = dot_f32(all_ref[...], select_ref[:, :WIDE]).astype(jnp.bfloat16).reshape(4, TOK, WIDE)
-    theirs_ref[...] = dot_f32(all_ref[...], select_ref[:, WIDE:]).astype(jnp.bfloat16).reshape(4, TOK, WIDE)
+    mine_ref[...] = dot_f32(all_ref[...], select_ref[code_ref[4, 1], :, :WIDE]).astype(jnp.bfloat16).reshape(4, TOK, WIDE)
+    theirs_ref[...] = dot_f32(all_ref[...], select_ref[code_ref[4, 1], :, WIDE:]).astype(jnp.bfloat16).reshape(4, TOK, WIDE)
 
 
 def spread(factor, table):
@@ -212,7 +213,7 @@
 
     packed = pl.pallas_call(
         pack_kernel,
-        out_shape=bf16(TOK + 16, FEAT),
+        out_shape=bf16(FEAT + 16, HD),
         in_specs=[VMEM] * 2,
         out_specs=VMEM,
         name="pack",
@@ -227,9 +228,9 @@
     lag = 4 * d + inner - (2 * zh + c)
     age = (4 * column + inner - seed_block[0] - 1) % 64
     code = jnp.where((lag == 0) | ((lag > 0) & (lag <= 16) & (lag <= age)), lag, -1).astype(jnp.int32)
-    code = jnp.concatenate([code, jnp.broadcast_to(y, (1, 5)).astype(jnp.int32)], axis=0)
-
-    select = lax.dynamic_index_in_dim(jnp.asarray(SELECTION, jnp.bfloat16), c, keepdims=False)
+    code = jnp.concatenate([code, jnp.stack([y, c, c, c, c])[None].astype(jnp.int32)], axis=0)
+
+    select = jnp.asarray(SELECTION, jnp.bfloat16)
     table = lax.dynamic_index_in_dim(jnp.asarray(SPREAD, jnp.bfloat16), c, keepdims=False)
 
     weight = lax.all_to_all(jnp.broadcast_to(w_pair[None], (16, 2, 80, FEAT)), ("x", "y"), 0, 0, tiled=True)

time: 155 us -> 156 us (level)
  waiting for transfers between devices: 34.9 us -> 38.3 us
  local copies, waits for them, and re-layouts: 7.25 us -> 5.22 us
    ppermute x11, waiting for transfers between devices: 34.1 us -> 38.3 us  [move(): return lax.ppermute(value, AXES, pairs)]
    squeeze x1 -> x0, local copies, waits for them, and re-layouts: 2.41 us -> none  [on_device(): lax.dynamic_index_in_dim(jnp.asarray(SELECTION, jnp.bfloat16), c, keepdim...]
  transfers between devices with their start and end apart: 13 -> 13, of which waited for: 7 -> 6; matrix products, arithmetic and copies ran while one was open for 5% -> 4% of each run, Pallas kernels for 7% -> 8%
where the time goes in v6:
time: 156 us; the launch traced here: 155 us
  starting transfers between devices  69.7 us (45%)
  waiting for transfers between devices  38.3 us (25%)
  blocking collectives  22.3 us (14%)
  Pallas kernels  13.2 us (8%)
  local copies, waits for them, and re-layouts  5.22 us (3%)
  other arithmetic  4.74 us (3%)
  between operations  1.59 us (1%)
    ppermute x11, starting transfers between devices, move(): return lax.ppermute(value, AXES, pairs)  52.7 us
    ppermute x11, waiting for transfers between devices, move(): return lax.ppermute(value, AXES, pairs)  38.3 us
    all_gather x1, blocking collectives, on_device(): lax.all_gather(attended, 'zl', axis=0, axis_index_groups=[[0, 1, 2, 3], [...  22.3 us
    all_to_all x1, starting transfers between devices, on_device(): lax.all_to_all(jnp.broadcast_to(w_pair[None], (16, 2, 80, FEAT)), ('x', '...  12.7 us
    pallas_call x1, Pallas kernels, on_device(): pl.pallas_call(attend_kernel, out_shape=(bf16(4, TOK, WIDE), bf16(4, TOK,...  7.26 us
    all_to_all x1, starting transfers between devices, on_device(): lax.all_to_all(jnp.where(to > y, kv_own[None], kv_far[None]), 'y', 0, 0,...  4.33 us
  transfers between devices with their start and end apart: 13, of which 6 were waited for; matrix products, arithmetic and copies ran while one was open for 4% of the time, Pallas kernels for 8%

profile of v6, /device:TPU:1, one launch (start us, length us, event | category | flops | bytes accessed | tf_op | source)
XLA Modules:
  0.0 155.1 jit_solution(767735167479091613)
XLA Ops:
  0.0 1.0 pad_maximum_fusion.1.own_ref
  1.0 3.9 %collective-permute-start.2 = (bf16[2,128,640]{2,1,0:T(8,128)(2,1)S(1)}, bf16[2,128,640]{2,1,0:T(8,128)(2,1)S(1)}, u32[]{:S(2)}, u32[]{:S(2)}) collective-permute-start(bf16[2,128,640]{2,1,0:T(8,128)(2,1)S(1)} %pad_maximum_fusion.1.own_ref), channel_id=1, source_target_pairs={{0,128},{1,129},{2,130},{3,131},{4,132},{5,133},{6,134},{7,135},{8... | collective-permute-start | bytes 983048 | tf_op jit(solution)/shard_map/ppermute | solution.py:30
  5.0 1.6 %pack.1 = bf16[656,128]{1,0:T(8,128)(2,1)} custom-call(bf16[128,640]{1,0:T(8,128)(2,1)} %query_ref.1, s32[1,16]{1,0:T(1,128)} %mask_ref.1), custom_call_target="tpu_custom_call" | custom-call | tf_op jit(solution)/shard_map/pack/pallas_call | solution.py:214
  6.6 15.4 %collective-permute-start = (bf16[656,128]{1,0:T(8,128)(2,1)}, bf16[656,128]{1,0:T(8,128)(2,1)S(1)}, u32[]{:S(2)}, u32[]{:S(2)}) collective-permute-start(bf16[656,128]{1,0:T(8,128)(2,1)} %pack.1), channel_id=1, source_target_pairs={{0,16},{1,17},{2,18},{3,19},{4,20},{5,21},{6,22},{7,23},{8,24},{9,... | collective-permute-start | bytes 503816 | tf_op jit(solution)/shard_map/ppermute | solution.py:30
  22.1 3.1 %collective-permute-start.5 = (bf16[80,640]{1,0:T(8,128)(2,1)}, bf16[80,640]{1,0:T(8,128)(2,1)S(1)}, u32[]{:S(2)}, u32[]{:S(2)}) collective-permute-start(bf16[80,640]{1,0:T(8,128)(2,1)} %param.15), channel_id=1, source_target_pairs={{0,8},{1,9},{2,10},{3,11},{4,12},{5,13},{6,14},{7,15},{8,0},{9,1},... | collective-permute-start | bytes 307208 | tf_op jit(solution)/shard_map/ppermute | solution.py:30
  25.9 1.3 broadcast_select_fusion
  27.2 4.3 %all-to-all-start = ((bf16[4,2,128,640]{3,2,1,0:T(8,128)(2,1)}), bf16[4,2,128,640]{3,2,1,0:T(8,128)(2,1)S(1)}, u32[]{:S(2)}, u32[]{:S(2)}) async-start(bf16[4,2,128,640]{3,2,1,0:T(8,128)(2,1)} %broadcast_select_fusion), calls=%async_computation | async-start | bytes 2621440 | tf_op jit(solution)/shard_map/all_to_all | solution.py:198
  32.3 4.8 %collective-permute-start.6 = (bf16[80,640]{1,0:T(8,128)(2,1)S(1)}, bf16[80,640]{1,0:T(8,128)(2,1)S(1)}, u32[]{:S(2)}, u32[]{:S(2)}) collective-permute-start(bf16[80,640]{1,0:T(8,128)(2,1)S(1)} %collective-permute-done.5), channel_id=1, source_target_pairs={{0,24},{1,25},{2,26},{3,27},{4,392},{5,393},{6,394},{7,395},{8,16}... | collective-permute-start | bytes 307208 | tf_op jit(solution)/shard_map/ppermute | solution.py:30
  38.6 1.9 %collective-permute-start.1 = (bf16[2,656,128]{2,1,0:T(8,128)(2,1)}, bf16[2,656,128]{2,1,0:T(8,128)(2,1)}, u32[]{:S(2)}, u32[]{:S(2)}) collective-permute-start(bf16[2,656,128]{2,1,0:T(8,128)(2,1)} %pad_maximum_fusion.qa_ref), channel_id=1, source_target_pairs={{0,8},{1,9},{2,10},{3,11},{4,12},{5,13},{6,14},{7,15},{8,0},{9,1},... | collective-permute-start | bytes 1007624 | tf_op jit(solution)/shard_map/ppermute | solution.py:30
  40.5 8.8 %collective-permute-done.6 = bf16[80,640]{1,0:T(8,128)(2,1)S(1)} collective-permute-done((bf16[80,640]{1,0:T(8,128)(2,1)S(1)}, bf16[80,640]{1,0:T(8,128)(2,1)S(1)}, u32[]{:S(2)}, u32[]{:S(2)}) %collective-permute-start.6) | collective-permute-done | bytes 102432 | tf_op jit(solution)/shard_map/ppermute | solution.py:30
  49.4 2.1 %broadcast_in_dim.49 = bf16[16,2,80,640]{3,2,1,0:T(8,128)(2,1)} broadcast(bf16[2,80,640]{2,1,0:T(8,128)(2,1)S(1)} %pad_maximum_fusion.2), dimensions={1,2,3} | broadcast | bytes 3481600 | tf_op jit(solution)/shard_map/broadcast_in_dim | solution.py:236
  51.5 12.7 %all-to-all-start.1 = ((bf16[16,2,80,640]{3,2,1,0:T(8,128)(2,1)}), bf16[16,2,80,640]{3,2,1,0:T(8,128)(2,1)S(1)}, u32[]{:S(2)}, u32[]{:S(2)}) async-start(bf16[16,2,80,640]{3,2,1,0:T(8,128)(2,1)} %broadcast_in_dim.49), calls=%async_computation.1 | async-start | bytes 6553600 | tf_op jit(solution)/shard_map/all_to_all | solution.py:236
  64.2 7.3 %attend.1 = (bf16[4,128,384]{2,1,0:T(8,128)(2,1)}, bf16[4,128,384]{2,1,0:T(8,128)(2,1)}) custom-call(s32[5,5]{1,0:T(8,128)} %pad_add_fusion.code_ref, bf16[2,656,128]{2,1,0:T(8,128)(2,1)} %pad_maximum_fusion.qa_ref, bf16[2,656,128]{2,1,0:T(8,128)(2,1)} %collective-permute-done.1.qb_ref, bf16[2,128,640]{2,1,0:T(8,128)(2,1)} %copy-done.3, ...), custom_call_target="tpu_custom_call" | custom-call | flops 60000002048 | bytes 4000000 | tf_op jit(solution)/shard_map/attend/pallas_call | solution.py:238
  71.4 2.6 %collective-permute-start.3 = (bf16[4,128,384]{2,1,0:T(8,128)(2,1)}, bf16[4,128,384]{2,1,0:T(8,128)(2,1)}, u32[]{:S(2)}, u32[]{:S(2)}) collective-permute-start(bf16[4,128,384]{2,1,0:T(8,128)(2,1)} %get-tuple-element.15), channel_id=1, source_target_pairs={{0,8},{1,9},{2,10},{3,11},{4,12},{5,13},{6,14},{7,15},{8,0},{9,1},... | collective-permute-start | bytes 1179656 | tf_op jit(solution)/shard_map/ppermute | solution.py:30
  75.7 1.0 copy-done.1
  76.7 1.7 %merge_cores.1 = (bf16[2,128,384]{2,1,0:T(8,128)(2,1)S(1)}, bf16[2,128,384]{2,1,0:T(8,128)(2,1)S(1)}) custom-call(bf16[4,128,384]{2,1,0:T(8,128)(2,1)S(1)} %copy-done.1, bf16[4,128,384]{2,1,0:T(8,128)(2,1)} %collective-permute-done.3.got_ref, bf16[2,128,384]{2,1,0:T(8,128)(2,1)S(1)} %dynamic-slice_bitcast_fusion.table_ref), custom_call_target="tpu_custom_call" | custom-call | tf_op jit(solution)/shard_map/merge_cores/pallas_call | solution.py:249
  78.4 7.2 %collective-permute-start.4 = (bf16[2,128,384]{2,1,0:T(8,128)(2,1)S(1)}, bf16[2,128,384]{2,1,0:T(8,128)(2,1)S(1)}, u32[]{:S(2)}, u32[]{:S(2)}) collective-permute-start(bf16[2,128,384]{2,1,0:T(8,128)(2,1)S(1)} %get-tuple-element.17), channel_id=1, source_target_pairs={{0,16},{1,17},{2,18},{3,19},{4,20},{5,21},{6,22},{7,23},{8,24},{9,... | collective-permute-start | bytes 589832 | tf_op jit(solution)/shard_map/ppermute | solution.py:30
  85.6 16.0 %collective-permute-done.4.got_ref = bf16[2,128,384]{2,1,0:T(8,128)(2,1)S(1)} collective-permute-done((bf16[2,128,384]{2,1,0:T(8,128)(2,1)S(1)}, bf16[2,128,384]{2,1,0:T(8,128)(2,1)S(1)}, u32[]{:S(2)}, u32[]{:S(2)}) %collective-permute-start.4) | collective-permute-done | bytes 196640 | tf_op jit(solution)/shard_map/ppermute | solution.py:30
  102.5 22.3 %all-gather = bf16[512,640]{1,0:T(8,128)(2,1)} all-gather(bf16[128,640]{1,0:T(8,128)(2,1)S(1)} %merge_last.1), channel_id=2, replica_groups={{0,1,2,3},{4,5,6,7},{8,9,10,11},{12,13,14,15},{16,17,18,19},{20,21,22,2..., dimensions={0}, use_global_device_ids=true | all-gather | bytes 819200 | tf_op jit(solution)/shard_map/all_gather | solution.py:266
  124.8 1.1 copy-done
  126.8 4.1 %collective-permute-start.8 = (bf16[128,640]{1,0:T(8,128)(2,1)S(1)}, bf16[128,640]{1,0:T(8,128)(2,1)S(1)}, u32[]{:S(2)}, u32[]{:S(2)}) collective-permute-start(bf16[128,640]{1,0:T(8,128)(2,1)S(1)} %get-tuple-element.19), channel_id=1, source_target_pairs={{0,8},{1,9},{2,10},{3,11},{4,12},{5,13},{6,14},{7,15},{8,0},{9,1},... | collective-permute-start | bytes 491528 | tf_op jit(solution)/shard_map/ppermute | solution.py:30
  132.0 6.3 %collective-permute-start.10 = (bf16[128,640]{1,0:T(8,128)(2,1)S(1)}, bf16[128,640]{1,0:T(8,128)(2,1)S(1)}, u32[]{:S(2)}, u32[]{:S(2)}) collective-permute-start(bf16[128,640]{1,0:T(8,128)(2,1)S(1)} %add_convert_fusion.1), channel_id=1, source_target_pairs={{0,4},{1,5},{2,6},{3,7},{4,0},{5,1},{6,2},{7,3},{8,12},{9,13},{10,... | collective-permute-start | bytes 491528 | tf_op jit(solution)/shard_map/ppermute | solution.py:30
  139.2 2.6 %collective-permute-start.9 = (bf16[128,640]{1,0:T(8,128)(2,1)S(1)}, bf16[128,640]{1,0:T(8,128)(2,1)S(1)}, u32[]{:S(2)}, u32[]{:S(2)}) collective-permute-start(bf16[128,640]{1,0:T(8,128)(2,1)S(1)} %get-tuple-element.22), channel_id=1, source_target_pairs={{0,8},{1,9},{2,10},{3,11},{4,12},{5,13},{6,14},{7,15},{8,0},{9,1},... | collective-permute-start | bytes 491528 | tf_op jit(solution)/shard_map/ppermute | solution.py:30
  142.8 11.6 %collective-permute-done.10 = bf16[128,640]{1,0:T(8,128)(2,1)S(1)} collective-permute-done((bf16[128,640]{1,0:T(8,128)(2,1)S(1)}, bf16[128,640]{1,0:T(8,128)(2,1)S(1)}, u32[]{:S(2)}, u32[]{:S(2)}) %collective-permute-start.10) | collective-permute-done | bytes 163872 | tf_op jit(solution)/shard_map/ppermute | solution.py:30
  (44 shorter events, 8.8 us)
Async XLA Ops:
  1.0 26.2 %copy-start.3 = (bf16[2,128,640]{2,1,0:T(8,128)(2,1)}, bf16[2,128,640]{2,1,0:T(8,128)(2,1)S(1)}, u32[]{:S(2)}) copy-start(bf16[2,128,640]{2,1,0:T(8,128)(2,1)S(1)} %pad_maximum_fusion.1.own_ref) | copy-start | bytes 983044
  1.0 24.8 %collective-permute-start.2 = (bf16[2,128,640]{2,1,0:T(8,128)(2,1)S(1)}, bf16[2,128,640]{2,1,0:T(8,128)(2,1)S(1)}, u32[]{:S(2)}, u32[]{:S(2)}) collective-permute-start(bf16[2,128,640]{2,1,0:T(8,128)(2,1)S(1)} %pad_maximum_fusion.1.own_ref), channel_id=1, source_target_pairs={{0,128},{1,129},{2,130},{3,131},{4,132},{5,133},{6,134},{7,135},{8... | collective-permute-start | bytes 983048 | tf_op jit(solution)/shard_map/ppermute | solution.py:30
  6.6 31.2 %collective-permute-start = (bf16[656,128]{1,0:T(8,128)(2,1)}, bf16[656,128]{1,0:T(8,128)(2,1)S(1)}, u32[]{:S(2)}, u32[]{:S(2)}) collective-permute-start(bf16[656,128]{1,0:T(8,128)(2,1)} %pack.1), channel_id=1, source_target_pairs={{0,16},{1,17},{2,18},{3,19},{4,20},{5,21},{6,22},{7,23},{8,24},{9,... | collective-permute-start | bytes 503816 | tf_op jit(solution)/shard_map/ppermute | solution.py:30
  22.1 10.3 %collective-permute-start.5 = (bf16[80,640]{1,0:T(8,128)(2,1)}, bf16[80,640]{1,0:T(8,128)(2,1)S(1)}, u32[]{:S(2)}, u32[]{:S(2)}) collective-permute-start(bf16[80,640]{1,0:T(8,128)(2,1)} %param.15), channel_id=1, source_target_pairs={{0,8},{1,9},{2,10},{3,11},{4,12},{5,13},{6,14},{7,15},{8,0},{9,1},... | collective-permute-start | bytes 307208 | tf_op jit(solution)/shard_map/ppermute | solution.py:30
  25.9 1.3 copy-start.5
  27.2 10.6 %copy-start.4 = (bf16[656,128]{1,0:T(8,128)(2,1)S(1)}, bf16[656,128]{1,0:T(8,128)(2,1)}, u32[]{:S(2)}) copy-start(bf16[656,128]{1,0:T(8,128)(2,1)} %pack.1) | copy-start | bytes 503812
  27.2 22.1 %copy-start.7 = (bf16[80,640]{1,0:T(8,128)(2,1)S(1)}, bf16[80,640]{1,0:T(8,128)(2,1)}, u32[]{:S(2)}) copy-start(bf16[80,640]{1,0:T(8,128)(2,1)} %param.15) | copy-start | bytes 307204
  27.2 22.1 %all-to-all-start = ((bf16[4,2,128,640]{3,2,1,0:T(8,128)(2,1)}), bf16[4,2,128,640]{3,2,1,0:T(8,128)(2,1)S(1)}, u32[]{:S(2)}, u32[]{:S(2)}) async-start(bf16[4,2,128,640]{3,2,1,0:T(8,128)(2,1)} %broadcast_select_fusion), calls=%async_computation | async-start | bytes 2621440 | tf_op jit(solution)/shard_map/all_to_all | solution.py:198
  32.3 16.9 %collective-permute-start.6 = (bf16[80,640]{1,0:T(8,128)(2,1)S(1)}, bf16[80,640]{1,0:T(8,128)(2,1)S(1)}, u32[]{:S(2)}, u32[]{:S(2)}) collective-permute-start(bf16[80,640]{1,0:T(8,128)(2,1)S(1)} %collective-permute-done.5), channel_id=1, source_target_pairs={{0,24},{1,25},{2,26},{3,27},{4,392},{5,393},{6,394},{7,395},{8,16}... | collective-permute-start | bytes 307208 | tf_op jit(solution)/shard_map/ppermute | solution.py:30
  37.1 12.1 %collective-permute-start.7 = (bf16[80,640]{1,0:T(8,128)(2,1)S(1)}, bf16[80,640]{1,0:T(8,128)(2,1)S(1)}, u32[]{:S(2)}, u32[]{:S(2)}) collective-permute-start(bf16[80,640]{1,0:T(8,128)(2,1)S(1)} %collective-permute-done.5), channel_id=1, source_target_pairs={{4,408},{5,409},{6,410},{7,411},{12,400},{13,401},{14,402},{15,403... | collective-permute-start | bytes 307208 | tf_op jit(solution)/shard_map/ppermute | solution.py:30
  38.6 25.6 %collective-permute-start.1 = (bf16[2,656,128]{2,1,0:T(8,128)(2,1)}, bf16[2,656,128]{2,1,0:T(8,128)(2,1)}, u32[]{:S(2)}, u32[]{:S(2)}) collective-permute-start(bf16[2,656,128]{2,1,0:T(8,128)(2,1)} %pad_maximum_fusion.qa_ref), channel_id=1, source_target_pairs={{0,8},{1,9},{2,10},{3,11},{4,12},{5,13},{6,14},{7,15},{8,0},{9,1},... | collective-permute-start | bytes 1007624 | tf_op jit(solution)/shard_map/ppermute | solution.py:30
  49.4 2.1 %copy-start.2 = (bf16[4,2,128,640]{3,2,1,0:T(8,128)(2,1)}, bf16[4,2,128,640]{3,2,1,0:T(8,128)(2,1)S(1)}, u32[]{:S(2)}) copy-start(bf16[4,2,128,640]{3,2,1,0:T(8,128)(2,1)S(1)} %all-to-all-done.row_ref) | copy-start | bytes 3932164
  51.5 73.3 %all-to-all-start.1 = ((bf16[16,2,80,640]{3,2,1,0:T(8,128)(2,1)}), bf16[16,2,80,640]{3,2,1,0:T(8,128)(2,1)S(1)}, u32[]{:S(2)}, u32[]{:S(2)}) async-start(bf16[16,2,80,640]{3,2,1,0:T(8,128)(2,1)} %broadcast_in_dim.49), calls=%async_computation.1 | async-start | bytes 6553600 | tf_op jit(solution)/shard_map/all_to_all | solution.py:236
  71.4 4.3 %collective-permute-start.3 = (bf16[4,128,384]{2,1,0:T(8,128)(2,1)}, bf16[4,128,384]{2,1,0:T(8,128)(2,1)}, u32[]{:S(2)}, u32[]{:S(2)}) collective-permute-start(bf16[4,128,384]{2,1,0:T(8,128)(2,1)} %get-tuple-element.15), channel_id=1, source_target_pairs={{0,8},{1,9},{2,10},{3,11},{4,12},{5,13},{6,14},{7,15},{8,0},{9,1},... | collective-permute-start | bytes 1179656 | tf_op jit(solution)/shard_map/ppermute | solution.py:30
  75.7 1.0 copy-start.1
  78.4 23.2 %collective-permute-start.4 = (bf16[2,128,384]{2,1,0:T(8,128)(2,1)S(1)}, bf16[2,128,384]{2,1,0:T(8,128)(2,1)S(1)}, u32[]{:S(2)}, u32[]{:S(2)}) collective-permute-start(bf16[2,128,384]{2,1,0:T(8,128)(2,1)S(1)} %get-tuple-element.17), channel_id=1, source_target_pairs={{0,16},{1,17},{2,18},{3,19},{4,20},{5,21},{6,22},{7,23},{8,24},{9,... | collective-permute-start | bytes 589832 | tf_op jit(solution)/shard_map/ppermute | solution.py:30
  124.8 1.1 copy-start
  126.8 5.1 %collective-permute-start.8 = (bf16[128,640]{1,0:T(8,128)(2,1)S(1)}, bf16[128,640]{1,0:T(8,128)(2,1)S(1)}, u32[]{:S(2)}, u32[]{:S(2)}) collective-permute-start(bf16[128,640]{1,0:T(8,128)(2,1)S(1)} %get-tuple-element.19), channel_id=1, source_target_pairs={{0,8},{1,9},{2,10},{3,11},{4,12},{5,13},{6,14},{7,15},{8,0},{9,1},... | collective-permute-start | bytes 491528 | tf_op jit(solution)/shard_map/ppermute | solution.py:30
  132.0 9.8 %copy-start.8 = (f32[8,640]{1,0:T(8,128)S(1)}, f32[8,640]{1,0:T(8,128)}, u32[]{:S(2)}) copy-start(f32[8,640]{1,0:T(8,128)} %param.16) | copy-start | bytes 61444
  132.0 22.4 %copy-start.6 = (bf16[128,640]{1,0:T(8,128)(2,1)S(1)}, bf16[128,640]{1,0:T(8,128)(2,1)}, u32[]{:S(2)}) copy-start(bf16[128,640]{1,0:T(8,128)(2,1)} %param.14) | copy-start | bytes 491524
  132.0 22.4 %collective-permute-start.10 = (bf16[128,640]{1,0:T(8,128)(2,1)S(1)}, bf16[128,640]{1,0:T(8,128)(2,1)S(1)}, u32[]{:S(2)}, u32[]{:S(2)}) collective-permute-start(bf16[128,640]{1,0:T(8,128)(2,1)S(1)} %add_convert_fusion.1), channel_id=1, source_target_pairs={{0,4},{1,5},{2,6},{3,7},{4,0},{5,1},{6,2},{7,3},{8,12},{9,13},{10,... | collective-permute-start | bytes 491528 | tf_op jit(solution)/shard_map/ppermute | solution.py:30
  139.2 3.6 %collective-permute-start.9 = (bf16[128,640]{1,0:T(8,128)(2,1)S(1)}, bf16[128,640]{1,0:T(8,128)(2,1)S(1)}, u32[]{:S(2)}, u32[]{:S(2)}) collective-permute-start(bf16[128,640]{1,0:T(8,128)(2,1)S(1)} %get-tuple-element.22), channel_id=1, source_target_pairs={{0,8},{1,9},{2,10},{3,11},{4,12},{5,13},{6,14},{7,15},{8,0},{9,1},... | collective-permute-start | bytes 491528 | tf_op jit(solution)/shard_map/ppermute | solution.py:30
